TPU v7x, 32 devices: a whole 2x2x4 slice. The times are simulated.
32 devices in a mesh: dp: 16 (over z, y, core), tensor: 2 (over x).
Axes of the slice: x: 2, y: 2, z: 4, core: 2. Of those that a mesh axis runs over, the one named last changes fastest.
Arguments:
- tokens: bfloat16 [16384, 1536], P(('dp', 'tensor')), may hold values from -6 to 6
- cotangent: bfloat16 [16384, 1536], P(('dp', 'tensor')), may hold values from -6 to 6
- lengths: int32 [64], replicated, may hold values from 1 to 1021, as said below
- sequence_adapter: int32 [64], replicated, may hold values from 0 to 7
- perm: int32 [16384], P(('dp', 'tensor')), may hold values from 0 to 16383, as said below
- dealt_position: int32 [16384], P(('dp', 'tensor')), may hold values from 0 to 16383, as said below
- block_norm_gain: float32 [1536], replicated, may hold values from 0.5 to 1.5
- gate_input_weight: bfloat16 [1536, 2, 3072], P('dp', None, 'tensor'), may hold values from -0.15625 to 0.15625
- rest_weight: bfloat16 [1536, 304], P('dp'), may hold values from -0.15625 to 0.15625
- filter_taps_input: float32 [5, 3072], P(None, 'tensor'), may hold values from -0.5 to 0.5
- filter_taps_bc: float32 [5, 256], replicated, may hold values from -0.5 to 0.5
- step_bias: float32 [48], P('tensor'), may hold values from -6.9 to -2.3
- head_decay_rate: float32 [48], P('tensor'), may hold values from 1 to 16
- skip_weight: float32 [48], P('tensor'), may hold values from 0.5 to 2
- gated_norm_gain: float32 [3072], P('tensor'), may hold values from 0.5 to 1.5
- output_weight: bfloat16 [3072, 1536], P('tensor', 'dp'), may hold values from -0.109375 to 0.109375
- adapter_down_in: bfloat16 [1536, 128], replicated, may hold values from -0.15625 to 0.15625
- adapter_up_gate_input: bfloat16 [128, 2, 3072], P(None, None, 'tensor'), may hold values from -1.5 to 1.5
- adapter_up_rest: bfloat16 [128, 304], replicated, may hold values from -1.5 to 1.5
- adapter_down_out: bfloat16 [3072, 128], P('tensor'), may hold values from -0.109375 to 0.109375
- adapter_up_out: bfloat16 [128, 1536], replicated, may hold values from -1.5 to 1.5
Outputs:
- output: bfloat16 [16384, 1536], P(('dp', 'tensor'))
- input_grad: bfloat16 [16384, 1536], P(('dp', 'tensor'))
- gradient_down_in: float32 [1536, 128], replicated
- gradient_up_gate_input: float32 [128, 2, 3072], P(None, None, 'tensor')
- gradient_up_rest: float32 [128, 304], replicated
- gradient_down_out: float32 [3072, 128], P('tensor')
- gradient_up_out: float32 [128, 1536], replicated
Inputs may be any that keep to these rules, and one draw needn't show every extreme that they name: `lengths`: each run of 4 entries (the sequences of one dp index, end to end in the dealt order) sums to 1024; in each run one sequence is longer than 512 and the others together are shorter than 512. `perm`: A permutation; every device of the given order sends exactly 32 of its rows to each dp index, all to devices of its own tensor index. `dealt_position`: the inverse of perm.
All inputs are finite; a program needn't handle non-finite values.
Results may differ from a plain program's by a relative error of at most 0.012.
Values may be sent and summed in bfloat16 or wider, within the bound.
No kernel may reach another device: no remote copies, remote signals or barrier semaphores. Data moves between devices by JAX's collectives and lax.ppermute only.
A program may use at most 256 MiB of HBM per device.

v0:
```python
from functools import partial

import jax
import jax.numpy as jnp
from jax import lax
from jax.sharding import PartitionSpec as P

MODEL_WIDTH = 1536
HEADDIM = 64
STATE = 128
SPAN = 256
ADAPTER_RANK = 16
SEQ_GROUP = 4


epsilon = 1e-05


def rounded(values):
    return lax.optimization_barrier(values.astype(jnp.bfloat16)).astype(jnp.float32)


def matrix_product(left, right):
    return jnp.dot(left, right, preferred_element_type=jnp.float32)


def shift_down(values, offset):
    padding = jnp.zeros((offset,) + values.shape[1:], values.dtype)
    return jnp.concatenate([padding, values[:-offset]], axis=0)


def conv_valid(segment):
    same_seq = []
    for offset in (1, 2, 3):
        before = jnp.concatenate([jnp.full((offset,), -1, jnp.int32), segment[:-offset]])
        same_seq.append((before == segment).astype(jnp.float32)[:, None])
    return same_seq


def causal_conv(values, kernel, same_seq):
    summed = kernel[3] * values + kernel[4]
    for offset in (1, 2, 3):
        summed = summed + kernel[3 - offset] * shift_down(values, offset) * same_seq[offset - 1]
    return jax.nn.silu(summed)


def ssd_block(carried_in, pieces, head_decay_rate, skip_weight):
    carry_state, seg_prev = carried_in
    inputs, b_block, c_block, step_sizes, segment = pieces
    highest_precision = lax.Precision.HIGHEST
    block_len = segment.shape[0]
    log_decay = -head_decay_rate[None, :] * step_sizes
    cumul = jnp.cumsum(log_decay, axis=0)
    span_total = cumul[-1]
    heads_first = cumul.T
    gaps = heads_first[:, :, None] - heads_first[:, None, :]
    causal = jnp.arange(block_len)[:, None] >= jnp.arange(block_len)[None, :]
    allowed = (causal & (segment[:, None] == segment[None, :])).astype(jnp.float32)
    decays = jnp.exp(jnp.minimum(gaps, 0.0)) * allowed[None, :, :]
    scores = jnp.dot(c_block, b_block.T, precision=highest_precision)
    weights = scores[None, :, :] * decays * step_sizes.T[:, None, :]
    outputs = jnp.einsum("hts,shp->thp", weights, inputs, precision=highest_precision)
    carried = (segment == seg_prev).astype(jnp.float32)
    from_state = jnp.einsum("tn,hpn->thp", c_block, carry_state, precision=highest_precision)
    outputs = outputs + (jnp.exp(cumul) * carried[:, None])[:, :, None] * from_state
    seg_end = segment[-1]
    kept_state = (seg_end == seg_prev).astype(jnp.float32)
    in_last = (segment == seg_end).astype(jnp.float32)
    coefficient = jnp.exp(span_total[None, :] - cumul) * step_sizes * in_last[:, None]
    carry_state = kept_state * jnp.exp(span_total)[:, None, None] * carry_state + jnp.einsum(
        "sh,shp,sn->hpn", coefficient, inputs, b_block, precision=highest_precision
    )
    outputs = outputs + skip_weight[None, :, None] * inputs
    return ((carry_state, seg_end), outputs)


def ssd(inputs, b_matrix, c_matrix, step_sizes, segment, head_decay_rate, skip_weight):
    row_count, head_count, head_width = inputs.shape
    span_count = row_count // SPAN
    pieces = (
        inputs.reshape(span_count, SPAN, head_count, head_width),
        b_matrix.reshape(span_count, SPAN, b_matrix.shape[1]),
        c_matrix.reshape(span_count, SPAN, c_matrix.shape[1]),
        step_sizes.reshape(span_count, SPAN, head_count),
        segment.reshape(span_count, SPAN),
    )
    start_state = jnp.zeros((head_count, head_width, b_matrix.shape[1]), jnp.float32)
    stepper = jax.checkpoint(
        partial(ssd_block, head_decay_rate=head_decay_rate, skip_weight=skip_weight)
    )
    final_carry, outputs = lax.scan(stepper, (start_state, jnp.int32(-1)), pieces)
    return outputs.reshape(row_count, head_count, head_width)


def body(
    tokens,
    cotangent,
    lengths,
    sequence_adapter,
    perm,
    dealt_position,
    block_norm_gain,
    gate_input_weight,
    rest_weight,
    filter_taps_input,
    filter_taps_bc,
    step_bias,
    head_decay_rate,
    skip_weight,
    gated_norm_gain,
    output_weight,
    adapter_down_in,
    adapter_up_gate_input,
    adapter_up_rest,
    adapter_down_out,
    adapter_up_out,
):
    tensor_count = lax.axis_size("tensor")
    tok_dev = tokens.shape[0]
    group_rows = tok_dev * tensor_count
    heads_local = step_bias.shape[0]
    inner_width_local = heads_local * HEADDIM
    inner_all = inner_width_local * tensor_count
    adapter_width = adapter_down_in.shape[1]
    dp_rank = lax.axis_index("dp")
    tensor_rank = lax.axis_index("tensor")
    order_send = jnp.argsort(dealt_position)
    dealt_in = (
        lax.all_to_all(tokens[order_send], "dp", split_axis=0, concat_axis=0, tiled=True),
        lax.all_to_all(cotangent[order_send], "dp", split_axis=0, concat_axis=0, tiled=True),
    )
    order_recv = jnp.argsort(perm // group_rows, stable=True)
    placed = jnp.argsort(order_recv)
    residual_input = dealt_in[0][placed].astype(jnp.float32)
    incoming_gradient_local = dealt_in[1][placed]
    w_zx_full, rest_weight_full, output_weight_local = (
        lax.all_gather(gate_input_weight, "dp", axis=0, tiled=True),
        lax.all_gather(rest_weight, "dp", axis=0, tiled=True),
        lax.all_gather(output_weight, "dp", axis=1, tiled=True),
    )
    w_zx_flat = w_zx_full.reshape(w_zx_full.shape[0], 2 * inner_width_local)
    up_gate_input_flat = adapter_up_gate_input.reshape(adapter_width, 2 * inner_width_local)
    group_lens = lax.dynamic_slice_in_dim(lengths, dp_rank * SEQ_GROUP, SEQ_GROUP)
    starts = jnp.cumsum(group_lens) - group_lens
    position = jnp.arange(group_rows, dtype=jnp.int32)
    segment = jnp.sum((position[:, None] >= starts[None, :]).astype(jnp.int32), axis=1) - 1
    group_ids = lax.dynamic_slice_in_dim(sequence_adapter, dp_rank * SEQ_GROUP, SEQ_GROUP)
    seq_slots = jnp.arange(SEQ_GROUP, dtype=jnp.int32)
    token_adapter = jnp.sum(
        jnp.where(segment[:, None] == seq_slots[None, :], group_ids[None, :], 0), axis=1
    )
    column_adapter_owner = jnp.arange(adapter_width, dtype=jnp.int32) // ADAPTER_RANK
    adapter_select_mask = (column_adapter_owner[None, :] == token_adapter[:, None]).astype(
        jnp.float32
    )
    local_owner_mask = lax.dynamic_slice_in_dim(
        adapter_select_mask, tensor_rank * tok_dev, tok_dev, 0
    )

    def prenorm(values):
        return (
            values
            * lax.rsqrt(jnp.mean(values * values, axis=1, keepdims=True) + epsilon)
            * block_norm_gain
        )

    normed_mine, norm_pull = jax.vjp(prenorm, residual_input)
    collected_rows = lax.all_gather(normed_mine.astype(jnp.bfloat16), "tensor", axis=0, tiled=True)
    middle_input = (matrix_product(collected_rows, adapter_down_in) * adapter_select_mask).astype(
        jnp.bfloat16
    )
    proj_zx = matrix_product(collected_rows, w_zx_flat) + matrix_product(
        middle_input, up_gate_input_flat
    )
    rest_projection = matrix_product(collected_rows, rest_weight_full) + matrix_product(
        middle_input, adapter_up_rest
    )
    gate_pre = proj_zx[:, :inner_width_local]
    dt_start = 2 * STATE + tensor_rank * heads_local
    dt_cols = lax.dynamic_slice_in_dim(rest_projection, dt_start, heads_local, 1)
    same_seq = conv_valid(segment)

    def section_in(conv_in, bc_pre, dt_pre):
        return (
            causal_conv(conv_in, filter_taps_input, same_seq),
            causal_conv(bc_pre, filter_taps_bc, same_seq),
            jax.nn.softplus(dt_pre + step_bias),
        )

    (conv_out, bc_act, step_sizes), section_pull = jax.vjp(
        section_in, proj_zx[:, inner_width_local:], rest_projection[:, : 2 * STATE], dt_cols
    )
    x_act = rounded(conv_out)
    b_matrix = rounded(bc_act[:, :STATE])
    c_matrix = rounded(bc_act[:, STATE:])

    def mixer(inputs, b_part, c_part, sizes):
        scanned = ssd(
            inputs.reshape(group_rows, heads_local, HEADDIM),
            b_part,
            c_part,
            sizes,
            segment,
            head_decay_rate,
            skip_weight,
        )
        return scanned.reshape(group_rows, inner_width_local)

    scan_out, scan_pull = jax.vjp(mixer, x_act, b_matrix, c_matrix, step_sizes)
    silu_gate = jax.nn.silu(gate_pre)
    gated = scan_out * silu_gate
    total_sq = lax.psum(jnp.sum(gated * gated, axis=1), "tensor")
    norm_factor = lax.rsqrt(total_sq / inner_all + epsilon)[:, None]
    normalized_output = (gated * norm_factor * gated_norm_gain).astype(jnp.bfloat16)
    joined_columns = jnp.concatenate([output_weight_local, adapter_down_out], axis=1)
    summed = lax.psum_scatter(
        matrix_product(normalized_output, joined_columns), "tensor", scatter_dimension=0, tiled=True
    )
    output_local = summed[:, :MODEL_WIDTH]
    mid_mine = summed[:, MODEL_WIDTH:]
    middle_output = (mid_mine * local_owner_mask).astype(jnp.bfloat16)
    block_result = residual_input + output_local + matrix_product(middle_output, adapter_up_out)
    gradient_middle_local = (
        matrix_product(incoming_gradient_local, adapter_up_out.T) * local_owner_mask
    ).astype(jnp.bfloat16)
    gradient_up_out = matrix_product(middle_output.T, incoming_gradient_local)
    incoming_gradient_full, gradient_middle_full = (
        lax.all_gather(incoming_gradient_local, "tensor", axis=0, tiled=True),
        lax.all_gather(gradient_middle_local, "tensor", axis=0, tiled=True),
    )
    gradient_normalized_output = matrix_product(
        incoming_gradient_full, output_weight_local.T
    ) + matrix_product(gradient_middle_full, adapter_down_out.T)
    gradient_down_out = matrix_product(normalized_output.T, gradient_middle_full)
    weighted = gradient_normalized_output * gated_norm_gain
    cross_sum = lax.psum(jnp.sum(weighted * gated, axis=1), "tensor")
    grad_gated = weighted * norm_factor - gated * norm_factor**3 * (cross_sum / inner_all)[:, None]
    grad_scan = rounded(grad_gated * silu_gate)
    sigma = jax.nn.sigmoid(gate_pre)
    grad_gate = grad_gated * scan_out * sigma * (1.0 + gate_pre * (1.0 - sigma))
    grad_x_act, grad_b, grad_c, grad_steps = scan_pull(grad_scan)
    grad_conv_in, grad_bc, grad_dt = section_pull(
        (grad_x_act, jnp.concatenate([grad_b, grad_c], axis=1), grad_steps)
    )
    gradient_gate_input = jnp.concatenate([grad_gate, grad_conv_in], axis=1).astype(jnp.bfloat16)
    rest_width = rest_projection.shape[1]
    grad_rest_wide = jnp.concatenate(
        [grad_bc, jnp.zeros((group_rows, rest_width - 2 * STATE), jnp.float32)], axis=1
    )
    gradient_rest_columns = lax.dynamic_update_slice(grad_rest_wide, grad_dt, (0, dt_start)).astype(
        jnp.bfloat16
    )
    gradient_middle_input = (
        (
            matrix_product(gradient_gate_input, up_gate_input_flat.T)
            + matrix_product(gradient_rest_columns, adapter_up_rest.T)
        )
        * adapter_select_mask
    ).astype(jnp.bfloat16)
    gradient_down_in = matrix_product(collected_rows.T, gradient_middle_input)
    gradient_up_gate_input = matrix_product(middle_input.T, gradient_gate_input).reshape(
        adapter_width, 2, inner_width_local
    )
    gradient_up_rest = matrix_product(middle_input.T, gradient_rest_columns)
    grad_normed = lax.psum_scatter(
        matrix_product(gradient_gate_input, w_zx_flat.T)
        + matrix_product(gradient_rest_columns, rest_weight_full.T)
        + matrix_product(gradient_middle_input, adapter_down_in.T),
        "tensor",
        scatter_dimension=0,
        tiled=True,
    )
    (grad_resid,) = norm_pull(grad_normed)
    grad_tokens = (incoming_gradient_local.astype(jnp.float32) + grad_resid).astype(jnp.bfloat16)
    out_tokens = block_result.astype(jnp.bfloat16)
    order_back = jnp.argsort(perm)
    returned = (
        lax.all_to_all(out_tokens[order_back], "dp", split_axis=0, concat_axis=0, tiled=True),
        lax.all_to_all(grad_tokens[order_back], "dp", split_axis=0, concat_axis=0, tiled=True),
    )
    placed_back = jnp.argsort(jnp.argsort(dealt_position // group_rows, stable=True))
    output = returned[0][placed_back]
    input_grad = returned[1][placed_back]
    shared_values = lax.psum(
        (gradient_down_in, gradient_up_rest, gradient_up_out), ("dp", "tensor")
    )
    local_heads = lax.psum((gradient_up_gate_input, gradient_down_out), "dp")
    return (
        output,
        input_grad,
        shared_values[0],
        local_heads[0],
        shared_values[1],
        local_heads[1],
        shared_values[2],
    )


def solution(mesh):
    placed = (
        P(("dp", "tensor"), None),
        P(("dp", "tensor"), None),
        P(),
        P(),
        P(("dp", "tensor")),
        P(("dp", "tensor")),
        P(),
        P("dp", None, "tensor"),
        P("dp", None),
        P(None, "tensor"),
        P(),
        P("tensor"),
        P("tensor"),
        P("tensor"),
        P("tensor"),
        P("tensor", "dp"),
        P(),
        P(None, None, "tensor"),
        P(),
        P("tensor", None),
        P(),
    )
    return jax.shard_map(
        body,
        mesh=mesh,
        in_specs=placed,
        out_specs=(
            P(("dp", "tensor"), None),
            P(("dp", "tensor"), None),
            P(),
            P(None, None, "tensor"),
            P(),
            P("tensor", None),
            P(),
        ),
        check_vma=False,
    )
```

profile of v0, /device:TPU:1, one launch (start us, length us, event | category | flops | bytes accessed | tf_op | source)
XLA Modules:
  0.0 1399.3 jit_solution(16369346926156466345)
XLA Ops:
  29.7 24.7 %all-to-all-done = bf16[16,32,1536]{2,1,0:T(8,128)(2,1)S(1)} async-done(((bf16[16,32,1536]{2,1,0:T(8,128)(2,1)}), bf16[16,32,1536]{2,1,0:T(8,128)(2,1)S(1)}, u32[]{:S(2)}, u32[]{:S(2)}) %all-to-all-start) | async-done | bytes 1572896 | tf_op jit(solution)/shard_map/all_to_all | solution.py:129
  62.7 45.2 %all_to_all.48 = bf16[16,32,1536]{2,1,0:T(8,128)(2,1)S(1)} all-to-all(bf16[16,32,1536]{2,1,0:T(8,128)(2,1)} %bitcast.414), channel_id=1, replica_groups=mesh['dp'=16,'tensor'=2] {'dp'}, dimensions={0} | all-to-all | bytes 3145728 | tf_op jit(solution)/shard_map/all_to_all | solution.py:130
  116.5 24.0 %all_gather.19 = bf16[1536,304]{1,0:T(8,128)(2,1)S(1)} all-gather(bf16[96,304]{1,0:T(8,128)(2,1)S(1)} %copy-done.49), channel_id=1, replica_groups=mesh['dp'=16,'tensor'=2] {'dp'}, dimensions={0}, use_global_device_ids=true | all-gather | bytes 992256 | tf_op jit(solution)/shard_map/all_gather | solution.py:138
  142.9 8.9 all_gather.23
  163.0 51.4 %all-gather.10.cloned.1.call-done = bf16[1536,1536]{0,1:T(8,128)(2,1)} async-done(((bf16[1536,96]{0,1:T(8,128)(2,1)}), bf16[1536,1536]{0,1:T(8,128)(2,1)}) %all-gather.10.cloned.1.call-update) | async-done | bytes 4718608 | tf_op jit(solution)/shard_map/all_gather | solution.py:139
  214.4 9.9 fusion.175
  224.3 72.3 %all-gather.8.cloned.1.call-done = bf16[1536,2,1536]{2,1,0:T(2,128)(2,1)} async-done(((bf16[96,2,1536]{2,1,0:T(2,128)(2,1)}), bf16[1536,2,1536]{2,1,0:T(2,128)(2,1)}) %all-gather.8.cloned.1.call-update) | async-done | bytes 9437200 | tf_op jit(solution)/shard_map/all_gather | solution.py:137
  296.6 9.7 copy.265
  306.3 13.5 fusion.174
  328.2 10.7 multiply_convert_fusion.3
  338.9 19.3 %reshape.580 = f32[4,256,24,64]{3,2,1,0:T(8,128)} reshape(bf16[1024,1536]{1,0:T(8,128)(2,1)} %get-tuple-element.814) | data formatting | bytes 9437184 | tf_op jit(solution)/shard_map/jvp()/reshape;jvp()/reshape | solution.py:81
  358.3 9.8 copy.221
  371.4 88.6 %while.42 = (s32[]{:T(128)}, f32[24,64,128]{2,1,0:T(8,128)S(1)}, s32[]{:T(128)}, f32[4,256,24,64]{1,3,2,0:T(8,128)}, f32[4,24,64,128]{3,2,1,0:T(8,128)}, /*index...) while((s32[]{:T(128)}, f32[24,64,128]{2,1,0:T(8,128)S(1)}, ...), condition=%wide.region_10.11_spmd.clone, body=%wide.region_7.10_spmd.clone.sunk | while | flops 2528482304 | bytes 15449087 | solution.py:91
  460.1 9.8 copy.255
  469.9 11.2 reshape.581
  481.0 11.4 multiply_reduce_fusion.3
  496.3 13.1 multiply_convert_fusion.1
  509.4 9.1 reshape.579
  518.5 9.8 copy.233
  534.2 333.9 %while.43 = (s32[]{:T(128)}, f32[24,64,128]{2,1,0:T(8,128)}, f32[4,256,24,64]{1,3,2,0:T(8,128)}, f32[4,256,128]{2,1,0:T(8,128)}, f32[4,256,128]{2,1,0:T(8,128)},...) while((s32[]{:T(128)}, f32[24,64,128]{2,1,0:T(8,128)}, ...), condition=%wide.region_31.32_spmd.clone, body=%wide.region_19.31_spmd.clone.sunk | while | flops 5782836224 | bytes 42664912 | solution.py:91
  554.1 12.6 fusion.296
  637.7 12.6 fusion.296
  721.4 12.6 fusion.296
  805.0 12.6 fusion.296
  868.1 9.8 copy.257
  877.9 11.2 reshape.582
  926.4 12.2 fusion.126
  949.5 11.4 fusion.113
  965.3 59.1 %reduce-scatter.5.cloned.1.call-done = f32[512,1536]{1,0:T(8,128)} async-done(((f32[1024,1536]{1,0:T(8,128)}), f32[512,1536]{1,0:T(8,128)}) %reduce-scatter.5.cloned.1.call-update) | async-done | bytes 3145744 | tf_op jit(solution)/shard_map/reduce_scatter | solution.py:265
  1039.1 70.3 %reduce-scatter.3.cloned.1.call-done = f32[512,1664]{1,0:T(8,128)} async-done(((f32[1024,1664]{1,0:T(8,128)}), f32[512,1664]{1,0:T(8,128)}) %reduce-scatter.3.cloned.1.call-update) | async-done | bytes 3407888 | tf_op jit(solution)/shard_map/reduce_scatter | solution.py:216
  1161.2 81.2 %all-reduce.24.cloned.1.call-done = (f32[128,2,1536]{2,1,0:T(2,128)}, f32[1536,128]{1,0:T(8,128)}) async-done(((f32[128,2,1536]{2,1,0:T(2,128)}, f32[1536,128]{1,0:T(8,128)}), (f32[128,2,1536]{2,1,0:T(2,128)}, f32[1536,128]{1,0:T(8,128)})) %all-reduce.24.cloned.1.call-update) | async-done | bytes 2359312 | tf_op jit(solution)/shard_map/psum | solution.py:287
  1242.4 140.3 %all-reduce.22.cloned.1.call-done = (f32[1536,128]{1,0:T(8,128)}, f32[128,304]{0,1:T(8,128)}, f32[128,1536]{1,0:T(8,128)}) async-done(((f32[1536,128]{1,0:T(8,128)}, f32[128,304]{0,1:T(8,128)}, f32[128,1536]{1,0:T(8,128)}), (f32[1536,128]{1,0:T(8,128)}, f32[128,304]{0,1:T(8,128)}, f32[128,1536]{1,0:T(8,128)})) %all-reduce.22.cloned.1.call-update) | async-done | bytes 1728528 | tf_op jit(solution)/shard_map/psum | solution.py:284
  (690 shorter events, 562.5 us)
Async XLA Ops:
  14.7 39.7 %all-to-all-start = ((bf16[16,32,1536]{2,1,0:T(8,128)(2,1)}), bf16[16,32,1536]{2,1,0:T(8,128)(2,1)S(1)}, u32[]{:S(2)}, u32[]{:S(2)}) async-start(bf16[16,32,1536]{2,1,0:T(8,128)(2,1)} %bitcast), calls=%async_computation | async-start | bytes 3145728 | tf_op jit(solution)/shard_map/all_to_all | solution.py:129
  22.1 129.7 %all-gather.6.cloned.1.call-start = ((), (), s32[]{:S(2)}) async-start(), calls=%async_computation.6 | async-start | bytes 4718592 | tf_op jit(solution)/shard_map/all_gather | solution.py:168
  59.7 103.2 %all-gather.12.cloned.1.call-start = ((), (), s32[]{:S(2)}) async-start(), calls=%async_computation.11 | async-start | bytes 4718592 | tf_op jit(solution)/shard_map/all_gather | solution.py:228
  110.9 40.9 %copy-start.39 = (bf16[1536,128]{1,0:T(8,128)(2,1)S(1)}, bf16[1536,128]{1,0:T(8,128)(2,1)}, u32[]{:S(2)}) copy-start(bf16[1536,128]{1,0:T(8,128)(2,1)} %param.41) | copy-start | bytes 1179652
  111.0 103.4 %all-gather.10.cloned.1.call-start = ((), (), s32[]{:S(2)}) async-start(), calls=%async_computation.8 | async-start | bytes 5013504 | tf_op jit(solution)/shard_map/all_gather | solution.py:139
  111.7 184.9 %all-gather.8.cloned.1.call-start = ((), (), s32[]{:S(2)}) async-start(), calls=%async_computation.7 | async-start | bytes 10027008 | tf_op jit(solution)/shard_map/all_gather | solution.py:137
  112.3 912.2 %reduce-scatter.5.cloned.1.call-start = ((), (), s32[]{:S(2)}) async-start(), calls=%async_computation.10 | async-start | bytes 9437184 | tf_op jit(solution)/shard_map/reduce_scatter | solution.py:265
  116.0 41.9 %copy-start.85 = (s32[128]{0:T(128)}, s32[128]{0:T(128)S(1)}, u32[]{:S(2)}) copy-start(s32[128]{0:T(128)S(1)} %and_select_fusion) | copy-start | bytes 1540
  116.1 41.8 %copy-start.62 = (s32[1024]{0:T(1024)}, s32[1024]{0:T(1024)S(1)}, u32[]{:S(2)}) copy-start(s32[1024]{0:T(1024)S(1)} %select_reduce_fusion) | copy-start | bytes 12292
  116.2 210.5 %copy-start.43 = (f32[1536]{0:T(1024)}, f32[1536]{0:T(1024)S(1)}, u32[]{:S(2)}) copy-start(f32[1536]{0:T(1024)S(1)} %get-tuple-element.742) | copy-start | bytes 18436
  116.2 210.5 %copy-start.45 = (f32[1536]{0:T(1024)}, f32[1536]{0:T(1024)S(1)}, u32[]{:S(2)}) copy-start(f32[1536]{0:T(1024)S(1)} %get-tuple-element.744) | copy-start | bytes 18436
  116.2 210.5 %copy-start.47 = (f32[1536]{0:T(1024)}, f32[1536]{0:T(1024)S(1)}, u32[]{:S(2)}) copy-start(f32[1536]{0:T(1024)S(1)} %get-tuple-element.745) | copy-start | bytes 18436
  116.2 210.5 %copy-start.52 = (f32[1536]{0:T(1024)}, f32[1536]{0:T(1024)S(1)}, u32[]{:S(2)}) copy-start(f32[1536]{0:T(1024)S(1)} %get-tuple-element.741) | copy-start | bytes 18436
  116.2 42.4 %copy-start.69 = (f32[1,256]{1,0:T(1,128)}, f32[1,256]{1,0:T(1,128)S(1)}, u32[]{:S(2)}) copy-start(f32[1,256]{1,0:T(1,128)S(1)} %get-tuple-element.837) | copy-start | bytes 3076
  116.3 42.4 %copy-start.71 = (f32[1,256]{1,0:T(1,128)}, f32[1,256]{1,0:T(1,128)S(1)}, u32[]{:S(2)}) copy-start(f32[1,256]{1,0:T(1,128)S(1)} %get-tuple-element.838) | copy-start | bytes 3076
  116.3 42.4 %copy-start.73 = (f32[1,256]{1,0:T(1,128)}, f32[1,256]{1,0:T(1,128)S(1)}, u32[]{:S(2)}) copy-start(f32[1,256]{1,0:T(1,128)S(1)} %get-tuple-element.840) | copy-start | bytes 3076
  116.3 42.4 %copy-start.75 = (f32[1,256]{1,0:T(1,128)}, f32[1,256]{1,0:T(1,128)S(1)}, u32[]{:S(2)}) copy-start(f32[1,256]{1,0:T(1,128)S(1)} %get-tuple-element.841) | copy-start | bytes 3076
  154.7 165.1 %copy-start.18 = (bf16[1024,128]{1,0:T(8,128)(2,1)}, bf16[1024,128]{1,0:T(8,128)(2,1)S(1)}, u32[]{:S(2)}) copy-start(bf16[1024,128]{1,0:T(8,128)(2,1)S(1)} %fusion.129) | copy-start | bytes 786436
  621.5 35.6 %copy-start.8 = (f32[256,128]{1,0:T(8,128)}, f32[256,128]{1,0:T(8,128)S(1)}, u32[]{:S(2)}) copy-start(f32[256,128]{1,0:T(8,128)S(1)} %get-tuple-element.1072) | copy-start | bytes 393220 | tf_op jit(solution)/shard_map/transpose(jvp())/while
  705.1 35.6 %copy-start.8 = (f32[256,128]{1,0:T(8,128)}, f32[256,128]{1,0:T(8,128)S(1)}, u32[]{:S(2)}) copy-start(f32[256,128]{1,0:T(8,128)S(1)} %get-tuple-element.1072) | copy-start | bytes 393220 | tf_op jit(solution)/shard_map/transpose(jvp())/while
  788.7 35.6 %copy-start.8 = (f32[256,128]{1,0:T(8,128)}, f32[256,128]{1,0:T(8,128)S(1)}, u32[]{:S(2)}) copy-start(f32[256,128]{1,0:T(8,128)S(1)} %get-tuple-element.1072) | copy-start | bytes 393220 | tf_op jit(solution)/shard_map/transpose(jvp())/while
  948.4 161.1 %reduce-scatter.3.cloned.1.call-start = ((), (), s32[]{:S(2)}) async-start(), calls=%async_computation.9 | async-start | bytes 10223616 | tf_op jit(solution)/shard_map/reduce_scatter | solution.py:216
  960.9 63.6 %copy-start.7 = (bf16[512,1536]{1,0:T(8,128)(2,1)S(1)}, bf16[512,1536]{1,0:T(8,128)(2,1)}, u32[]{:S(2)}) copy-start(bf16[512,1536]{1,0:T(8,128)(2,1)} %copy-done.6) | copy-start | bytes 4718596
  960.9 63.6 %copy-start.51 = (f32[1536]{0:T(1024)S(1)}, f32[1536]{0:T(1024)}, u32[]{:S(2)}) copy-start(f32[1536]{0:T(1024)} %param.31) | copy-start | bytes 18436
  960.9 66.1 %copy-start.66 = (f32[512]{0:T(512)S(1)}, f32[512]{0:T(512)}, u32[]{:S(2)}) copy-start(f32[512]{0:T(512)} %copy-done.65) | copy-start | bytes 6148
  960.9 66.1 %copy-start.68 = (f32[512]{0:T(512)S(1)}, f32[512]{0:T(512)}, u32[]{:S(2)}) copy-start(f32[512]{0:T(512)} %copy-done.67) | copy-start | bytes 6148
  1029.6 79.8 %copy-start.28 = (bf16[128,1536]{1,0:T(8,128)(2,1)S(1)}, bf16[128,1536]{1,0:T(8,128)(2,1)}, u32[]{:S(2)}) copy-start(bf16[128,1536]{1,0:T(8,128)(2,1)} %param.45) | copy-start | bytes 1179652
  1032.6 82.9 %all-to-all-start.3 = ((bf16[16,32,1536]{2,1,0:T(8,128)(2,1)}), bf16[16,32,1536]{2,1,0:T(8,128)(2,1)S(1)}, u32[]{:S(2)}, u32[]{:S(2)}) async-start(bf16[16,32,1536]{2,1,0:T(8,128)(2,1)} %bitcast.18), calls=%async_computation.5 | async-start | bytes 3145728 | tf_op jit(solution)/shard_map/all_to_all | solution.py:279
  1115.5 42.8 %all-to-all-start.1 = ((bf16[16,32,1536]{2,1,0:T(8,128)(2,1)}), bf16[16,32,1536]{2,1,0:T(8,128)(2,1)S(1)}, u32[]{:S(2)}, u32[]{:S(2)}) async-start(bf16[16,32,1536]{2,1,0:T(8,128)(2,1)} %bitcast.413), calls=%async_computation.2 | async-start | bytes 3145728 | tf_op jit(solution)/shard_map/all_to_all | solution.py:278
  1121.7 120.7 %all-reduce.24.cloned.1.call-start = ((), (), s32[]{:S(2)}) async-start(), calls=%async_computation.13 | async-start | bytes 4718592 | tf_op jit(solution)/shard_map/psum | solution.py:287
  1135.1 247.6 %all-reduce.22.cloned.1.call-start = ((), (), s32[]{:S(2)}) async-start(), calls=%async_computation.12 | async-start | bytes 3457024 | tf_op jit(solution)/shard_map/psum | solution.py:284
  1158.3 233.8 %copy-start.1 = (bf16[512,1536]{1,0:T(8,128)(2,1)S(1)}, bf16[512,1536]{1,0:T(8,128)(2,1)}, u32[]{:S(2)}) copy-start(bf16[512,1536]{1,0:T(8,128)(2,1)} %param.25) | copy-start | bytes 4718596
  (110 other events, 821.9 us)
Sparse Core Ops, SparseCore 0:
  59.9 48.4 all-gather.5
  111.1 47.2 all-gather.11
  160.6 53.7 all-gather.9
  216.5 79.9 all-gather.7
  948.5 75.9 reduce-scatter.4
  1026.7 82.7 reduce-scatter.2
  1135.2 107.1 all-reduce.23
  1248.8 133.9 all-reduce.21
where the time goes:
time: 1410 us; the launch traced here: 1400 us
  waiting for transfers between devices  505 us (36%)
  matrix products  340 us (24%)
  local copies, waits for them, and re-layouts  261 us (19%)
  other arithmetic  164 us (12%)
  blocking collectives  81.9 us (6%)
  starting transfers between devices  20.4 us (1%)
  between operations  15.7 us (1%)
    psum x1, waiting for transfers between devices, body(): lax.psum((gradient_down_in, gradient_up_rest, gradient_up_out), ('dp', 't...  140 us
    dot_general x12, matrix products, ssd_block(): jnp.einsum('hts,shp->thp', weights, inputs, precision=highest_precision)  118 us
    dot_general x20, matrix products, matrix_product(): return jnp.dot(left, right, preferred_element_type=jnp.float32)  102 us
    psum x1, waiting for transfers between devices, body(): local_heads = lax.psum((gradient_up_gate_input, gradient_down_out), 'dp')  81.2 us
    all_gather x1, waiting for transfers between devices, body(): lax.all_gather(gate_input_weight, 'dp', axis=0, tiled=True)  72.3 us
    reduce_scatter x1, waiting for transfers between devices, body(): lax.psum_scatter(matrix_product(normalized_output, joined_columns), 'tens...  70.3 us
    reduce_scatter x1, waiting for transfers between devices, body(): lax.psum_scatter(matrix_product(gradient_gate_input, w_zx_flat.T) + matri...  59.1 us
    all_gather x1, waiting for transfers between devices, body(): lax.all_gather(output_weight, 'dp', axis=1, tiled=True)  51.4 us
  transfers between devices with their start and end apart: 11, of which 8 were waited for; matrix products, arithmetic and copies ran while one was open for 7% of the time, Pallas kernels for 0%

commit v1 on v0

v1 whole, which is shorter than its diff:
```python
from functools import partial

import jax
import jax.numpy as jnp
from jax import lax
from jax.experimental import pallas as pl
from jax.experimental.pallas import tpu as pltpu
from jax.sharding import PartitionSpec as P

MODEL_WIDTH = 1536
HEADDIM = 64
STATE = 128
LANES = 128
CHUNK = 128
BLOCK = 256
ADAPTER_RANK = 16
SEQ_GROUP = 4
REST_LOCAL = 2 * STATE + LANES

epsilon = 1e-05
LOG2E = 1.4426950408889634
VMEM_BYTES = 56 * 1024 * 1024
f32 = jnp.float32
bf16 = jnp.bfloat16

NN = (((1,), (0,)), ((), ()))
NT = (((1,), (1,)), ((), ()))
TN = (((0,), (0,)), ((), ()))


def mm(left, right, dims=NN):
    return lax.dot_general(left, right, dims, preferred_element_type=f32)


def params(count=1):
    return pltpu.CompilerParams(
        dimension_semantics=("arbitrary",) * count, vmem_limit_bytes=VMEM_BYTES
    )


def whole(shape):
    return pl.BlockSpec(shape, lambda *_: (0,) * len(shape))


def iota(shape, axis):
    return lax.broadcasted_iota(jnp.int32, shape, axis)


def pack_matrix(key_col, key_row):
    count = key_row.shape[1]
    rank = jnp.sum((key_col < key_row).astype(f32), axis=0, keepdims=True).astype(jnp.int32)
    return (iota((count, count), 0) == rank).astype(f32).astype(bf16)


def unpack_matrix(key_col, key_row):
    count = key_row.shape[1]
    rank = jnp.sum((key_row < key_col).astype(f32), axis=1, keepdims=True).astype(jnp.int32)
    return (iota((count, count), 1) == rank).astype(f32).astype(bf16)


def pack_kernel(key_col, key_row, first, second, first_out, second_out):
    select = pack_matrix(key_col[...], key_row[...])
    first_out[...] = mm(select, first[...]).astype(bf16)
    second_out[...] = mm(select, second[...]).astype(bf16)


def unpack_kernel(key_col, key_row, rows, rows_out):
    select = unpack_matrix(key_col[...], key_row[...])
    rows_out[...] = mm(select, rows[...]).astype(bf16)


def place_norm_kernel(key_col, key_row, rows, gain, rows_out, normed_out):
    select = unpack_matrix(key_col[...], key_row[...])
    resid = mm(select, rows[...])
    rows_out[...] = resid.astype(bf16)
    scale = lax.rsqrt(jnp.mean(resid * resid, axis=1, keepdims=True) + epsilon)
    normed_out[...] = (resid * scale * gain[...]).astype(bf16)


def simple_call(kernel, outs, flops, *args, scalars=0):
    vector = pl.BlockSpec(memory_space=pltpu.VMEM)
    scalar = pl.BlockSpec(memory_space=pltpu.SMEM)
    return pl.pallas_call(
        kernel,
        out_shape=outs,
        in_specs=[scalar] * scalars + [vector] * (len(args) - scalars),
        out_specs=jax.tree.map(lambda _: vector, outs),
        compiler_params=pltpu.CompilerParams(vmem_limit_bytes=VMEM_BYTES),
        cost_estimate=pl.CostEstimate(flops=flops, bytes_accessed=6_000_000, transcendentals=0),
    )(*args)


def segment_start(meta, position):
    begin = jnp.zeros_like(position)
    for k in range(1, SEQ_GROUP):
        begin = jnp.where(position >= meta[k], meta[k], begin)
    return begin


def adapter_mask(meta, first, rows):
    position = first + iota((rows, LANES), 0)
    owner = jnp.full((rows, LANES), meta[SEQ_GROUP], jnp.int32)
    for k in range(1, SEQ_GROUP):
        owner = jnp.where(position >= meta[k], meta[SEQ_GROUP + k], owner)
    return (iota((rows, LANES), 1) // ADAPTER_RANK == owner).astype(f32)


def cumulate(values):
    total = values
    step = 1
    while step < values.shape[0]:
        pad = jnp.zeros((step, values.shape[1]), f32)
        total = total + jnp.concatenate([pad, total[:-step]], axis=0)
        step *= 2
    return total


def cumulate_back(values):
    total = values
    step = 1
    while step < values.shape[0]:
        pad = jnp.zeros((step, values.shape[1]), f32)
        total = total + jnp.concatenate([total[step:], pad], axis=0)
        step *= 2
    return total


def sigmoid(values):
    return 1.0 / (1.0 + jnp.exp(-values))


def column(values, h):
    return jnp.broadcast_to(values[:, h : h + 1], (values.shape[0], LANES))


def decay_tables(dt, decay_rate):
    cumul = cumulate(dt * (-LOG2E * decay_rate))
    source = cumul - jnp.log(jnp.maximum(dt, 1e-37)) * LOG2E
    return cumul, source


def forward_kernel(
    meta,
    normed, w_x, w_rest, down_in, up_x, up_rest, taps, taps_bc, step_bias, decay_rate, skip,
    x_out, dx_out, y_out, state_out, bc_out, dbc_out, dt_out, sig_out, mid_out,
    conv_in, rest, state, from_state, scaled,
    *, heads, block,
):
    i = pl.program_id(0)
    inner = heads * HEADDIM
    per_block = block // CHUNK
    first = i * CHUNK

    @pl.when(i == 0)
    def _():
        conv_in[block : block + 8, :] = jnp.zeros((8, inner), f32)
        rest[block : block + 8, :] = jnp.zeros((8, REST_LOCAL), f32)
        state[...] = jnp.zeros_like(state)

    @pl.when(i % per_block == 0)
    def _():
        conv_in[0:8, :] = conv_in[block : block + 8, :]
        rest[0:8, :] = rest[block : block + 8, :]
        rows = normed[...]
        mid = (mm(rows, down_in[...]) * adapter_mask(meta, first, block)).astype(bf16)
        mid_out[...] = mid
        conv_in[8 : block + 8, :] = mm(rows, w_x[...]) + mm(mid, up_x[...])
        rest[8 : block + 8, :] = mm(rows, w_rest[...]) + mm(mid, up_rest[...])

    offset = pl.multiple_of((i % per_block) * CHUNK, CHUNK)
    window = pl.ds(offset, CHUNK + 8)
    position = first + iota((CHUNK, LANES), 0)
    begin = segment_start(meta, position)
    depth = position - begin
    same = [(depth >= k).astype(f32) for k in (1, 2, 3)]

    def conv(ext, tap):
        summed = tap[3:4] * ext[8:] + tap[4:5]
        for k in (1, 2, 3):
            summed = summed + tap[3 - k : 4 - k] * (ext[8 - k : 8 - k + CHUNK] * same[k - 1])
        sig = sigmoid(summed)
        act = summed * sig
        return act, sig + act * (1.0 - sig)

    b_act, b_slope = conv(rest[window, 0:STATE], taps_bc[:, 0:STATE])
    c_act, c_slope = conv(rest[window, STATE : 2 * STATE], taps_bc[:, STATE : 2 * STATE])
    b_mat = b_act.astype(bf16)
    c_mat = c_act.astype(bf16)
    bc_out[:, 0:STATE] = b_mat
    bc_out[:, STATE : 2 * STATE] = c_mat
    dbc_out[:, 0:STATE] = b_slope
    dbc_out[:, STATE : 2 * STATE] = c_slope
    step_pre = rest[window, 2 * STATE : REST_LOCAL][8:] + step_bias[...]
    dt = jnp.maximum(step_pre, 0.0) + jnp.log(1.0 + jnp.exp(-jnp.abs(step_pre)))
    small = jnp.exp(step_pre)
    dt = jnp.where(step_pre < -8.0, small * (1.0 - 0.5 * small), dt)
    dt_out[...] = dt
    sig_out[...] = sigmoid(step_pre)
    cumul, source = decay_tables(dt, decay_rate[...])
    source_rows = source.T
    total = cumul[CHUNK - 1 : CHUNK, :]
    s_pos = first + iota((CHUNK, CHUNK), 1)
    allowed = jnp.where((s_pos <= position) & (s_pos >= begin), 0.0, -1e30)
    scores = mm(c_mat, b_mat, NT)
    begin_last = segment_start(meta, first + CHUNK - 1)
    kept = jnp.where(begin_last < first, 1.0, 0.0)
    in_last = (position >= begin_last).astype(f32)
    carried = (begin < first).astype(f32)
    state_low = state[...].astype(bf16)
    state_out[...] = state_low
    from_state[...] = mm(c_mat, state_low)
    left = iota((CHUNK, LANES), 1) < HEADDIM
    left_row = left[0:1]
    for pair in range(heads // 2):
        h0, h1 = 2 * pair, 2 * pair + 1
        cols = slice(pair * LANES, (pair + 1) * LANES)
        act, slope = conv(conv_in[window, cols], taps[:, cols])
        x_low = act.astype(bf16)
        x_out[:, cols] = x_low
        dx_out[:, cols] = slope.astype(bf16)
        x = x_low.astype(f32)
        cum0, cum1 = column(cumul, h0), column(cumul, h1)
        m0 = jnp.exp2(cum0 - source_rows[h0 : h0 + 1] + allowed) * scores
        m1 = jnp.exp2(cum1 - source_rows[h1 : h1 + 1] + allowed) * scores
        weights = jnp.concatenate([m0.astype(bf16), m1.astype(bf16)], axis=1)
        x_split = jnp.concatenate(
            [jnp.where(left, x, 0.0).astype(bf16), jnp.where(left, 0.0, x).astype(bf16)], axis=0
        )
        inside = mm(weights, x_split)
        reach = jnp.exp2(jnp.where(left, cum0, cum1)) * carried
        y_out[:, cols] = inside + reach * from_state[:, cols] + skip[:, cols] * x
        total_pair = jnp.where(left_row, column(total, h0), column(total, h1))
        source_pair = jnp.where(left, column(source, h0), column(source, h1))
        coefficient = jnp.exp2(total_pair - source_pair) * in_last
        scaled[:, cols] = (x * coefficient).astype(bf16)
        state[:, cols] = state[:, cols] * (jnp.exp2(total_pair) * kept)
    state[...] += mm(b_mat, scaled[...], TN)


def forward_scan(meta, normed, w_x, w_rest, down_in, up_x, up_rest, taps, taps_bc, bias, decay, skip, heads):
    rows = normed.shape[0]
    inner = heads * HEADDIM
    block = min(BLOCK, rows)
    per_block = block // CHUNK
    chunk_rows = lambda width: pl.BlockSpec((CHUNK, width), lambda i, *_: (i, 0))
    block_rows = lambda width: pl.BlockSpec((block, width), lambda i, *_: (i // per_block, 0))
    outs = (
        jax.ShapeDtypeStruct((rows, inner), bf16),
        jax.ShapeDtypeStruct((rows, inner), bf16),
        jax.ShapeDtypeStruct((rows, inner), f32),
        jax.ShapeDtypeStruct((rows // CHUNK * STATE, inner), bf16),
        jax.ShapeDtypeStruct((rows, 2 * STATE), bf16),
        jax.ShapeDtypeStruct((rows, 2 * STATE), f32),
        jax.ShapeDtypeStruct((rows, LANES), f32),
        jax.ShapeDtypeStruct((rows, LANES), f32),
        jax.ShapeDtypeStruct((rows, LANES), bf16),
    )
    operands = (w_x, w_rest, down_in, up_x, up_rest, taps, taps_bc, bias, decay, skip)
    grid = pltpu.PrefetchScalarGridSpec(
        num_scalar_prefetch=1,
        grid=(rows // CHUNK,),
        in_specs=[block_rows(MODEL_WIDTH)] + [whole(a.shape) for a in operands],
        out_specs=[
            chunk_rows(inner), chunk_rows(inner), chunk_rows(inner), chunk_rows(inner),
            chunk_rows(2 * STATE), chunk_rows(2 * STATE), chunk_rows(LANES), chunk_rows(LANES),
            block_rows(LANES),
        ],
        scratch_shapes=[
            pltpu.VMEM((block + 8, inner), f32),
            pltpu.VMEM((block + 8, REST_LOCAL), f32),
            pltpu.VMEM((STATE, inner), f32),
            pltpu.VMEM((CHUNK, inner), f32),
            pltpu.VMEM((CHUNK, inner), bf16),
        ],
    )
    return pl.pallas_call(
        partial(forward_kernel, heads=heads, block=block),
        out_shape=outs,
        grid_spec=grid,
        compiler_params=params(),
        cost_estimate=pl.CostEstimate(
            flops=3 * rows * MODEL_WIDTH * inner, bytes_accessed=40_000_000, transcendentals=0
        ),
    )(meta, normed, *operands)


def gate_kernel(
    meta,
    normed, mid, scan_out, cotangent, w_gate, up_gate, w_out, down_out, up_out, gain,
    gate_out, weighted_out, gained_out, part_out, mid_part_out, gmid_out, stats_out,
    *, inner,
):
    block = normed.shape[0]
    first = pl.program_id(0) * block
    gate = mm(normed[...], w_gate[...]) + mm(mid[...], up_gate[...])
    gate_out[...] = gate
    gated = scan_out[...] * (gate * sigmoid(gate))
    square = jnp.sum(gated * gated, axis=1, keepdims=True)
    gained = (gated * gain[...]).astype(bf16)
    gained_out[...] = gained
    part_out[...] = mm(gained, w_out[...], NT).astype(bf16)
    mid_part_out[...] = mm(gained, down_out[...])
    gd = cotangent[...]
    gmid = (mm(gd, up_out[...], NT) * adapter_mask(meta, first, block)).astype(bf16)
    gmid_out[...] = gmid
    weighted = (mm(gd, w_out[...]) + mm(gmid, down_out[...], NT)) * gain[...]
    weighted_out[...] = weighted
    cross = jnp.sum(weighted * gated, axis=1, keepdims=True)
    lane = iota((block, LANES), 1)
    stats = jnp.where(lane == 0, square, jnp.where(lane == 1, cross, 0.0))
    stats_out[...] = stats.T[0:8, :]


def gate_stage(meta, normed, mid, scan_out, cotangent, w_gate, up_gate, w_out, down_out, up_out, gain):
    rows, inner = scan_out.shape
    block = min(BLOCK, rows)
    block_rows = lambda width: pl.BlockSpec((block, width), lambda i, *_: (i, 0))
    operands = (w_gate, up_gate, w_out, down_out, up_out, gain)
    outs = (
        jax.ShapeDtypeStruct((rows, inner), f32),
        jax.ShapeDtypeStruct((rows, inner), f32),
        jax.ShapeDtypeStruct((rows, inner), bf16),
        jax.ShapeDtypeStruct((rows, MODEL_WIDTH), bf16),
        jax.ShapeDtypeStruct((rows, LANES), f32),
        jax.ShapeDtypeStruct((rows, LANES), bf16),
        jax.ShapeDtypeStruct((8, rows), f32),
    )
    grid = pltpu.PrefetchScalarGridSpec(
        num_scalar_prefetch=1,
        grid=(rows // block,),
        in_specs=[block_rows(MODEL_WIDTH), block_rows(LANES), block_rows(inner), block_rows(MODEL_WIDTH)]
        + [whole(a.shape) for a in operands],
        out_specs=[
            block_rows(inner), block_rows(inner), block_rows(inner), block_rows(MODEL_WIDTH),
            block_rows(LANES), block_rows(LANES),
            pl.BlockSpec((8, block), lambda i, *_: (0, i)),
        ],
    )
    return pl.pallas_call(
        partial(gate_kernel, inner=inner),
        out_shape=outs,
        grid_spec=grid,
        compiler_params=params(),
        cost_estimate=pl.CostEstimate(
            flops=6 * rows * MODEL_WIDTH * inner, bytes_accessed=50_000_000, transcendentals=0
        ),
    )(meta, normed, mid, scan_out, cotangent, *operands)


def split_sum(values, indicator):
    high = values.astype(bf16)
    low = (values - high.astype(f32)).astype(bf16)
    return mm(high, indicator) + mm(low, indicator)


def backward_kernel(
    meta,
    scan_out, gate_pre, weighted, x_in, slope_in, bc_in, dbc_in, dt_in, sig_in, state_in, stats,
    gained, gmid, taps, taps_bc, decay_rate, skip, indicator,
    gz_out, grest_out, gdown_out,
    dstate, g_next, gbc_next, from_dstate, scaled, reached, product, source_product, row_product,
    *, heads, inner_all,
):
    i = pl.program_id(0)
    inner = heads * HEADDIM
    first = (pl.num_programs(0) - 1 - i) * CHUNK

    @pl.when(i == 0)
    def _():
        dstate[...] = jnp.zeros_like(dstate)
        g_next[...] = jnp.zeros_like(g_next)
        gbc_next[...] = jnp.zeros_like(gbc_next)
        gdown_out[...] = jnp.zeros_like(gdown_out)
        row_product[...] = jnp.zeros_like(row_product)

    s_pos = first + iota((CHUNK, LANES), 0)
    begin = segment_start(meta, s_pos)
    long_pos = first + iota((CHUNK + 8, LANES), 0)
    long_depth = long_pos - segment_start(meta, long_pos)
    same = [(long_depth >= k).astype(f32) for k in (1, 2, 3)]
    t_pos = first + iota((CHUNK, CHUNK), 1)
    t_begin = segment_start(meta, t_pos)
    allowed = jnp.where((s_pos <= t_pos) & (s_pos >= t_begin), 0.0, -1e30)
    begin_last = segment_start(meta, first + CHUNK - 1)
    kept = jnp.where(begin_last < first, 1.0, 0.0)
    in_last = (s_pos >= begin_last).astype(f32)
    carried = (begin < first).astype(f32)

    factor = lax.rsqrt(stats[0:1, :] * (1.0 / inner_all) + epsilon)
    pull = factor * factor * factor * stats[1:2, :] * (1.0 / inner_all)
    row_id = iota((LANES, CHUNK), 0)
    both = jnp.where(row_id == 0, factor, jnp.where(row_id == 1, pull, 0.0)).T
    factor_col, pull_col = column(both, 0), column(both, 1)

    gmid_scaled = (gmid[...].astype(f32) * factor_col).astype(bf16)
    gdown_out[...] += mm(gmid_scaled, gained[...], TN)

    dt = dt_in[...]
    sig = sig_in[...]
    cumul, source = decay_tables(dt, decay_rate[...])
    cumul_rows = cumul.T
    total = cumul[CHUNK - 1 : CHUNK, :]
    b_mat = bc_in[:, 0:STATE]
    c_mat = bc_in[:, STATE : 2 * STATE]
    scores = mm(b_mat, c_mat, NT)
    dstate_low = dstate[...].astype(bf16)
    from_dstate[...] = mm(b_mat, dstate_low)
    left = iota((CHUNK, LANES), 1) < HEADDIM
    left_row = left[0:1]
    gscores = jnp.zeros((CHUNK, CHUNK), f32)

    def conv_back(grad, later, tap):
        ext = jnp.concatenate([grad, later], axis=0)
        out = tap[3:4] * grad
        for k in (1, 2, 3):
            out = out + tap[3 - k : 4 - k] * (ext * same[k - 1])[k : k + CHUNK]
        return out

    for pair in range(heads // 2):
        h0, h1 = 2 * pair, 2 * pair + 1
        cols = slice(pair * LANES, (pair + 1) * LANES)
        gate = gate_pre[:, cols]
        y = scan_out[:, cols]
        gate_sig = sigmoid(gate)
        silu = gate * gate_sig
        ggated = weighted[:, cols] * factor_col - y * silu * pull_col
        gy_low = (ggated * silu).astype(bf16)
        gz_out[:, cols] = (ggated * y * (gate_sig + silu * (1.0 - gate_sig))).astype(bf16)
        gy = gy_low.astype(f32)
        gy_split = jnp.concatenate(
            [jnp.where(left, gy, 0.0).astype(bf16), jnp.where(left, 0.0, gy).astype(bf16)], axis=0
        )
        x_low = x_in[:, cols]
        x = x_low.astype(f32)
        dots = mm(x_low, gy_split, NT)
        src0, src1 = column(source, h0), column(source, h1)
        e0 = jnp.exp2(cumul_rows[h0 : h0 + 1] - src0 + allowed)
        e1 = jnp.exp2(cumul_rows[h1 : h1 + 1] - src1 + allowed)
        gscores = gscores + dots[:, 0:CHUNK] * e0 + dots[:, CHUNK:] * e1
        weights = jnp.concatenate([(e0 * scores).astype(bf16), (e1 * scores).astype(bf16)], axis=1)
        inside = mm(weights, gy_split)
        total_pair = jnp.where(left_row, column(total, h0), column(total, h1))
        coefficient = jnp.exp2(total_pair - jnp.where(left, src0, src1)) * in_last
        reach = jnp.exp2(jnp.where(left, column(cumul, h0), column(cumul, h1))) * carried
        outside = coefficient * from_dstate[:, cols]
        gx_scan = inside + outside
        skip_row = skip[:, cols]
        gx = gx_scan + skip_row * gy
        x_side = x * gx_scan
        source_product[:, cols] = x_side
        product[:, cols] = gy * (y - skip_row * x) - x_side
        scaled[:, cols] = (x * coefficient).astype(bf16)
        reached[:, cols] = (gy * reach).astype(bf16)
        keep_row = jnp.exp2(total_pair) * kept
        dstate_cols = dstate[:, cols]
        row_product[0:1, cols] = jnp.sum(x * outside, axis=0, keepdims=True) + keep_row * jnp.sum(
            dstate_cols * state_in[:, cols].astype(f32), axis=0, keepdims=True
        )
        dstate[:, cols] = dstate_cols * keep_row
        gconv = gx * slope_in[:, cols].astype(f32)
        gz_out[:, inner + pair * LANES : inner + (pair + 1) * LANES] = conv_back(
            gconv, g_next[:, cols], taps[:, cols]
        ).astype(bf16)
        g_next[:, cols] = gconv[0:8]

    gscores_low = gscores.astype(bf16)
    grad_b = mm(gscores_low, c_mat) + mm(scaled[...], dstate_low, NT)
    grad_c = mm(gscores_low, b_mat, TN) + mm(reached[...], state_in[...], NT)
    for part, grad in ((0, grad_b), (1, grad_c)):
        cols = slice(part * STATE, (part + 1) * STATE)
        gconv = grad * dbc_in[:, cols]
        grest_out[:, cols] = conv_back(gconv, gbc_next[:, cols], taps_bc[:, cols]).astype(bf16)
        gbc_next[:, cols] = gconv[0:8]
    dstate[...] += mm(c_mat, reached[...], TN)

    grad_cumul = split_sum(product[...], indicator[...])
    direct = split_sum(source_product[...], indicator[...])
    grad_total = split_sum(row_product[...], indicator[...])[0:1]
    grad_log = cumulate_back(grad_cumul) + grad_total
    ratio = jnp.where(dt > 1e-30, sig / jnp.maximum(dt, 1e-30), 1.0)
    grad_pre = direct * ratio - decay_rate[...] * grad_log * sig
    used = iota((CHUNK, LANES), 1) < heads
    grest_out[:, 2 * STATE : REST_LOCAL] = jnp.where(used, grad_pre, 0.0).astype(bf16)


def backward_scan(meta, scan_out, gate_pre, weighted, x_act, slope, bc, dbc, dt, sig, states, stats, gained, gmid, taps, taps_bc, decay, skip, indicator, heads, inner_all):
    rows, inner = scan_out.shape
    count = rows // CHUNK
    chunk_rows = lambda width: pl.BlockSpec((CHUNK, width), lambda i, *_: (count - 1 - i, 0))
    operands = (taps, taps_bc, decay, skip, indicator)
    streams = (scan_out, gate_pre, weighted, x_act, slope, bc, dbc, dt, sig, states)
    outs = (
        jax.ShapeDtypeStruct((rows, 2 * inner), bf16),
        jax.ShapeDtypeStruct((rows, REST_LOCAL), bf16),
        jax.ShapeDtypeStruct((LANES, inner), f32),
    )
    grid = pltpu.PrefetchScalarGridSpec(
        num_scalar_prefetch=1,
        grid=(count,),
        in_specs=[chunk_rows(a.shape[1]) for a in streams]
        + [pl.BlockSpec((8, CHUNK), lambda i, *_: (0, count - 1 - i))]
        + [chunk_rows(inner), chunk_rows(LANES)]
        + [whole(a.shape) for a in operands],
        out_specs=[chunk_rows(2 * inner), chunk_rows(REST_LOCAL), whole((LANES, inner))],
        scratch_shapes=[
            pltpu.VMEM((STATE, inner), f32),
            pltpu.VMEM((8, inner), f32),
            pltpu.VMEM((8, 2 * STATE), f32),
            pltpu.VMEM((CHUNK, inner), f32),
            pltpu.VMEM((CHUNK, inner), bf16),
            pltpu.VMEM((CHUNK, inner), bf16),
            pltpu.VMEM((CHUNK, inner), f32),
            pltpu.VMEM((CHUNK, inner), f32),
            pltpu.VMEM((8, inner), f32),
        ],
    )
    return pl.pallas_call(
        partial(backward_kernel, heads=heads, inner_all=inner_all),
        out_shape=outs,
        grid_spec=grid,
        compiler_params=params(),
        cost_estimate=pl.CostEstimate(
            flops=6 * rows * MODEL_WIDTH * inner, bytes_accessed=50_000_000, transcendentals=0
        ),
    )(meta, *streams, stats, gained, gmid, *operands)


def project_back_kernel(
    meta,
    gz, grest, normed, mid, w_gate, w_x, w_rest, down_in, up_gate, up_x, up_rest,
    grad_out, gdown_out, gup_out, gup_rest_out,
    *, inner,
):
    block = gz.shape[0]
    first = pl.program_id(0) * block

    @pl.when(pl.program_id(0) == 0)
    def _():
        gdown_out[...] = jnp.zeros_like(gdown_out)
        gup_out[...] = jnp.zeros_like(gup_out)
        gup_rest_out[...] = jnp.zeros_like(gup_rest_out)

    ggate = gz[:, 0:inner]
    gconv = gz[:, inner : 2 * inner]
    grest_rows = grest[...]
    gmid = mm(ggate, up_gate[...], NT) + mm(gconv, up_x[...], NT) + mm(grest_rows, up_rest[...], NT)
    gmid = (gmid * adapter_mask(meta, first, block)).astype(bf16)
    grad = mm(ggate, w_gate[...], NT) + mm(gconv, w_x[...], NT)
    grad = grad + mm(grest_rows, w_rest[...], NT) + mm(gmid, down_in[...], NT)
    grad_out[...] = grad.astype(bf16)
    mid_rows = mid[...]
    gdown_out[...] += mm(gmid, normed[...], TN)
    gup_out[...] += mm(mid_rows, gz[...], TN)
    gup_rest_out[...] += mm(mid_rows, grest_rows, TN)


def project_back(meta, gz, grest, normed, mid, w_gate, w_x, w_rest, down_in, up_gate, up_x, up_rest):
    rows = gz.shape[0]
    inner = gz.shape[1] // 2
    block = min(BLOCK, rows)
    block_rows = lambda width: pl.BlockSpec((block, width), lambda i, *_: (i, 0))
    operands = (w_gate, w_x, w_rest, down_in, up_gate, up_x, up_rest)
    outs = (
        jax.ShapeDtypeStruct((rows, MODEL_WIDTH), bf16),
        jax.ShapeDtypeStruct((LANES, MODEL_WIDTH), f32),
        jax.ShapeDtypeStruct((LANES, 2 * inner), f32),
        jax.ShapeDtypeStruct((LANES, REST_LOCAL), f32),
    )
    grid = pltpu.PrefetchScalarGridSpec(
        num_scalar_prefetch=1,
        grid=(rows // block,),
        in_specs=[block_rows(2 * inner), block_rows(REST_LOCAL), block_rows(MODEL_WIDTH), block_rows(LANES)]
        + [whole(a.shape) for a in operands],
        out_specs=[block_rows(MODEL_WIDTH)] + [whole(o.shape) for o in outs[1:]],
    )
    return pl.pallas_call(
        partial(project_back_kernel, inner=inner),
        out_shape=outs,
        grid_spec=grid,
        compiler_params=params(),
        cost_estimate=pl.CostEstimate(
            flops=5 * rows * MODEL_WIDTH * inner, bytes_accessed=40_000_000, transcendentals=0
        ),
    )(meta, gz, grest, normed, mid, *operands)


def output_kernel(
    meta, key_col, key_row, resid, own, other, mid_own, mid_other, stats, cotangent, up_out,
    sent_out, gup_out, *, inner_all,
):
    rows = resid.shape[0]
    row_id = iota((LANES, rows), 0)
    factor = lax.rsqrt(stats[0:1, :] * (1.0 / inner_all) + epsilon)
    factor_col = jnp.where(row_id == 0, factor, 0.0).T[:, 0:1]
    first = meta[2 * SEQ_GROUP]
    mid = (mid_own[...] + mid_other[...].astype(f32)) * factor_col
    mid = (mid * adapter_mask(meta, first, rows)).astype(bf16)
    summed = (own[...].astype(f32) + other[...].astype(f32)) * factor_col
    result = resid[...].astype(f32) + summed + mm(mid, up_out[...])
    select = pack_matrix(key_col[...], key_row[...])
    sent_out[...] = mm(select, result.astype(bf16)).astype(bf16)
    gup_out[...] = mm(mid, cotangent[...], TN)


def input_grad_kernel(key_col, key_row, resid, own, other, cotangent, gain, sent_out):
    values = resid[...].astype(f32)
    scale = lax.rsqrt(jnp.mean(values * values, axis=1, keepdims=True) + epsilon)
    weighted = (own[...].astype(f32) + other[...].astype(f32)) * gain[...]
    inner = jnp.mean(weighted * values, axis=1, keepdims=True)
    grad = scale * (weighted - values * (scale * scale * inner))
    result = cotangent[...].astype(f32) + grad
    select = pack_matrix(key_col[...], key_row[...])
    sent_out[...] = mm(select, result.astype(bf16)).astype(bf16)


def body(
    tokens,
    cotangent,
    lengths,
    sequence_adapter,
    perm,
    dealt_position,
    block_norm_gain,
    gate_input_weight,
    rest_weight,
    filter_taps_input,
    filter_taps_bc,
    step_bias,
    head_decay_rate,
    skip_weight,
    gated_norm_gain,
    output_weight,
    adapter_down_in,
    adapter_up_gate_input,
    adapter_up_rest,
    adapter_down_out,
    adapter_up_out,
):
    tensor_count = lax.axis_size("tensor")
    tok_dev = tokens.shape[0]
    group_rows = tok_dev * tensor_count
    heads = step_bias.shape[0]
    inner = heads * HEADDIM
    inner_all = inner * tensor_count
    dp_rank = lax.axis_index("dp")
    tensor_rank = lax.axis_index("tensor")
    swap = [(0, 1), (1, 0)]

    def deal(rows):
        return lax.all_to_all(rows, "dp", split_axis=0, concat_axis=0, tiled=True)

    def gather_rows(mine):
        if tensor_count != 2:
            return lax.all_gather(mine, "tensor", axis=0, tiled=True)
        other = lax.ppermute(mine, "tensor", swap)
        first = tensor_rank == 0
        return jnp.concatenate([jnp.where(first, mine, other), jnp.where(first, other, mine)])

    def own_rows(full, axis=0):
        return lax.dynamic_slice_in_dim(full, tensor_rank * tok_dev, tok_dev, axis)

    def reduce_rows(full):
        if tensor_count != 2:
            summed = lax.psum_scatter(full.astype(f32), "tensor", scatter_dimension=0, tiled=True)
            return summed, jnp.zeros_like(summed)
        theirs = lax.dynamic_slice_in_dim(full, (1 - tensor_rank) * tok_dev, tok_dev, 0)
        return own_rows(full), lax.ppermute(theirs.astype(bf16), "tensor", swap)

    group_lens = lax.dynamic_slice_in_dim(lengths, dp_rank * SEQ_GROUP, SEQ_GROUP)
    starts = jnp.cumsum(group_lens) - group_lens
    group_ids = lax.dynamic_slice_in_dim(sequence_adapter, dp_rank * SEQ_GROUP, SEQ_GROUP)
    meta = jnp.concatenate([starts, group_ids, (tensor_rank * tok_dev)[None]]).astype(jnp.int32)
    slot = jnp.arange(tok_dev, dtype=jnp.int32)
    given_key = (perm // group_rows) * tok_dev + slot
    dealt_key = (dealt_position // group_rows) * tok_dev + slot

    def keys(values):
        return values[:, None], values[None, :]

    token_rows = jax.ShapeDtypeStruct((tok_dev, MODEL_WIDTH), bf16)
    move_flops = 2 * tok_dev * tok_dev * MODEL_WIDTH
    gain_row = block_norm_gain[None, :]

    w_x = lax.all_gather(gate_input_weight[:, 1, :], "dp", axis=0, tiled=True)
    w_gate = lax.all_gather(gate_input_weight[:, 0, :], "dp", axis=0, tiled=True)
    w_out = lax.all_gather(output_weight.T, "dp", axis=0, tiled=True)
    rest_full = lax.all_gather(rest_weight, "dp", axis=0, tiled=True)
    dt_start = 2 * STATE + tensor_rank * heads

    def local_rest(matrix):
        steps = lax.dynamic_slice_in_dim(matrix, dt_start, heads, 1)
        return jnp.concatenate(
            [matrix[:, : 2 * STATE], jnp.pad(steps, ((0, 0), (0, LANES - heads)))], axis=1
        )

    w_rest = local_rest(rest_full)
    up_rest = local_rest(adapter_up_rest)
    up_gate = adapter_up_gate_input[:, 0, :]
    up_x = adapter_up_gate_input[:, 1, :]
    taps = jnp.pad(filter_taps_input, ((0, 3), (0, 0)))
    taps_bc = jnp.pad(filter_taps_bc, ((0, 3), (0, 0)))
    head_row = lambda values: jnp.pad(values, (0, LANES - heads))[None, :]
    bias_row, decay_row = head_row(step_bias), head_row(head_decay_rate)
    skip_row = jnp.repeat(skip_weight, HEADDIM)[None, :]
    indicator = (
        jnp.arange(inner)[:, None] // HEADDIM == jnp.arange(LANES)[None, :]
    ).astype(bf16)

    sent_tokens, sent_cotangent = simple_call(
        pack_kernel, (token_rows, token_rows), 2 * move_flops, *keys(dealt_position), tokens, cotangent
    )
    resid, normed_mine = simple_call(
        place_norm_kernel, (token_rows, token_rows), move_flops,
        *keys(given_key), deal(sent_tokens), gain_row,
    )
    normed = gather_rows(normed_mine)
    grad_mine = simple_call(
        unpack_kernel, token_rows, move_flops, *keys(given_key), deal(sent_cotangent)
    )
    grad_full = gather_rows(grad_mine)

    x_act, slope, scan_out, states, bc, dbc, dt, sig, mid_in = forward_scan(
        meta, normed, w_x, w_rest, adapter_down_in, up_x, up_rest, taps, taps_bc,
        bias_row, decay_row, skip_row, heads,
    )
    gate_pre, weighted, gained, part, mid_part, gmid, stats = gate_stage(
        meta, normed, mid_in, scan_out, grad_full, w_gate, up_gate, w_out, adapter_down_out,
        adapter_up_out, gated_norm_gain[None, :],
    )
    if tensor_count == 2:
        stats = stats + lax.ppermute(stats, "tensor", swap)
    else:
        stats = lax.psum(stats, "tensor")
    part_own, part_other = reduce_rows(part)
    mid_own, mid_other = reduce_rows(mid_part)
    sent_output, gup_out = simple_call(
        partial(output_kernel, inner_all=inner_all),
        (token_rows, jax.ShapeDtypeStruct((LANES, MODEL_WIDTH), f32)), 2 * move_flops,
        meta, *keys(perm), resid, part_own, part_other, mid_own, mid_other,
        own_rows(stats, 1), grad_mine, adapter_up_out, scalars=1,
    )
    output = simple_call(
        unpack_kernel, token_rows, move_flops, *keys(dealt_key), deal(sent_output)
    )

    gz, grest, gdown_out = backward_scan(
        meta, scan_out, gate_pre, weighted, x_act, slope, bc, dbc, dt, sig, states, stats,
        gained, gmid, taps, taps_bc, decay_row, skip_row, indicator, heads, inner_all,
    )
    grad_part, gdown_in, gup_zx, gup_rest = project_back(
        meta, gz, grest, normed, mid_in, w_gate, w_x, w_rest, adapter_down_in, up_gate, up_x, up_rest
    )
    grad_own, grad_other = reduce_rows(grad_part)
    sent_grad = simple_call(
        input_grad_kernel, token_rows, move_flops,
        *keys(perm), resid, grad_own, grad_other, grad_mine, gain_row,
    )
    input_grad = simple_call(
        unpack_kernel, token_rows, move_flops, *keys(dealt_key), deal(sent_grad)
    )

    rest_width = adapter_up_rest.shape[1]
    wide = jnp.concatenate(
        [gup_rest[:, : 2 * STATE], jnp.zeros((LANES, rest_width - 2 * STATE), f32)], axis=1
    )
    gup_rest = lax.dynamic_update_slice(
        wide, gup_rest[:, 2 * STATE : 2 * STATE + heads], (0, dt_start)
    )
    gdown_in, gup_rest, gup_out = lax.psum((gdown_in, gup_rest, gup_out), ("dp", "tensor"))
    gup_zx, gdown_out = lax.psum((gup_zx, gdown_out), "dp")
    return (
        output,
        input_grad,
        gdown_in.T,
        gup_zx.reshape(LANES, 2, inner),
        gup_rest,
        gdown_out.T,
        gup_out,
    )


def solution(mesh):
    placed = (
        P(("dp", "tensor"), None),
        P(("dp", "tensor"), None),
        P(),
        P(),
        P(("dp", "tensor")),
        P(("dp", "tensor")),
        P(),
        P("dp", None, "tensor"),
        P("dp", None),
        P(None, "tensor"),
        P(),
        P("tensor"),
        P("tensor"),
        P("tensor"),
        P("tensor"),
        P("tensor", "dp"),
        P(),
        P(None, None, "tensor"),
        P(),
        P("tensor", None),
        P(),
    )
    return jax.shard_map(
        body,
        mesh=mesh,
        in_specs=placed,
        out_specs=(
            P(("dp", "tensor"), None),
            P(("dp", "tensor"), None),
            P(),
            P(None, None, "tensor"),
            P(),
            P("tensor", None),
            P(),
        ),
        check_vma=False,
    )
```

time: 1410 us -> 726 us (0.51)
  matrix products: 340 us -> 0 us
  local copies, waits for them, and re-layouts: 261 us -> 44.5 us
  Pallas kernels: 0 us -> 162 us
  other arithmetic: 164 us -> 12.2 us
  waiting for transfers between devices: 505 us -> 385 us
  starting transfers between devices: 20.4 us -> 48.3 us
  blocking collectives: 81.9 us -> 57.9 us
    dot_general x76 -> x0, matrix products: 340 us -> none  [the longest x12 118 us: ssd_block(): jnp.einsum('hts,shp->thp', weights, inputs, precision=highest_precision)]
    pallas_call x0 -> x11, Pallas kernels: none -> 162 us  [the longest x1 38.6 us: gate_stage(): pl.pallas_call(partial(gate_kernel, inner=inner), out_shape=outs, grid_sp...]
    reduce_scatter x2 -> x0, waiting for transfers between devices: 129 us -> none  [the longest x1 70.3 us: body(): lax.psum_scatter(matrix_product(normalized_output, joined_columns), 'tens...]
    all_gather x4 -> x3, waiting for transfers between devices: 124 us -> 0.04 us  [the longest x1 0.02 us: body(): lax.all_gather(gate_input_weight[:, 0, :], 'dp', axis=0, tiled=True)]
    ppermute x0 -> x6, waiting for transfers between devices: none -> 84.1 us  [the longest x2 48 us: gather_rows(): other = lax.ppermute(mine, 'tensor', swap)]
    reshape x11 -> x1, local copies, waits for them, and re-layouts: 74.5 us -> 3.42 us  [body(): gup_zx.reshape(LANES, 2, inner)]
    another operation x45 -> x1, other arithmetic: 54.5 us -> 0.18 us
    all_to_all x1 -> x0, blocking collectives: 45.2 us -> none  [body(): lax.all_to_all(cotangent[order_send], 'dp', split_axis=0, concat_axis=0,...]
  transfers between devices with their start and end apart: 11 -> 15, of which waited for: 8 -> 7; matrix products, arithmetic and copies ran while one was open for 7% -> 6% of each run, Pallas kernels for 0% -> 16%
where the time goes in v1:
time: 726 us; the launch traced here: 725 us
  waiting for transfers between devices  385 us (53%)
  Pallas kernels  162 us (22%)
  blocking collectives  57.9 us (8%)
  starting transfers between devices  48.3 us (7%)
  local copies, waits for them, and re-layouts  44.5 us (6%)
  between operations  14.1 us (2%)
  other arithmetic  12.2 us (2%)
    psum x1, waiting for transfers between devices, body(): lax.psum((gdown_in, gup_rest, gup_out), ('dp', 'tensor'))  138 us
    psum x1, waiting for transfers between devices, body(): gup_zx, gdown_out = lax.psum((gup_zx, gdown_out), 'dp')  112 us
    all_gather x1, blocking collectives, body(): rest_full = lax.all_gather(rest_weight, 'dp', axis=0, tiled=True)  57.9 us
    all_to_all x4, waiting for transfers between devices, deal(): return lax.all_to_all(rows, 'dp', split_axis=0, concat_axis=0, tiled=True)  50.3 us
    ppermute x2, waiting for transfers between devices, gather_rows(): other = lax.ppermute(mine, 'tensor', swap)  48 us
    all_to_all x4, starting transfers between devices, deal(): return lax.all_to_all(rows, 'dp', split_axis=0, concat_axis=0, tiled=True)  43.6 us
    pallas_call x1, Pallas kernels, gate_stage(): pl.pallas_call(partial(gate_kernel, inner=inner), out_shape=outs, grid_sp...  38.6 us
    ppermute x3, waiting for transfers between devices, reduce_rows(): return (own_rows(full), lax.ppermute(theirs.astype(bf16), 'tensor', swap))  36 us
  transfers between devices with their start and end apart: 15, of which 7 were waited for; matrix products, arithmetic and copies ran while one was open for 6% of the time, Pallas kernels for 16%

profile of v1, /device:TPU:1, one launch (start us, length us, event | category | flops | bytes accessed | tf_op | source)
XLA Modules:
  0.0 724.6 jit_solution(10564869056277246905)
XLA Ops:
  7.2 2.3 fusion.17
  12.0 5.2 shard_map.252
  17.2 7.3 %all-to-all-start = ((bf16[16,32,1536]{2,1,0:T(8,128)(2,1)}), bf16[16,32,1536]{2,1,0:T(8,128)(2,1)S(1)}, u32[]{:S(2)}, u32[]{:S(2)}) async-start(bf16[16,32,1536]{2,1,0:T(8,128)(2,1)} %bitcast.42), calls=%async_computation | async-start | bytes 3145728 | tf_op jit(solution)/shard_map/all_to_all | solution.py:650
  25.3 50.3 %all-to-all-done = bf16[16,32,1536]{2,1,0:T(8,128)(2,1)S(1)} async-done(((bf16[16,32,1536]{2,1,0:T(8,128)(2,1)}), bf16[16,32,1536]{2,1,0:T(8,128)(2,1)S(1)}, u32[]{:S(2)}, u32[]{:S(2)}) %all-to-all-start) | async-done | bytes 1572896 | tf_op jit(solution)/shard_map/all_to_all | solution.py:650
  76.7 15.1 %all-to-all-start.1 = ((bf16[16,32,1536]{2,1,0:T(8,128)(2,1)}), bf16[16,32,1536]{2,1,0:T(8,128)(2,1)S(1)}, u32[]{:S(2)}, u32[]{:S(2)}) async-start(bf16[16,32,1536]{2,1,0:T(8,128)(2,1)} %bitcast.17), calls=%async_computation.1 | async-start | bytes 3145728 | tf_op jit(solution)/shard_map/all_to_all | solution.py:650
  95.3 57.9 %all_gather.13 = bf16[1536,304]{1,0:T(8,128)(2,1)S(1)} all-gather(bf16[96,304]{1,0:T(8,128)(2,1)S(1)} %copy-done.18), channel_id=1, replica_groups=mesh['dp'=16,'tensor'=2] {'dp'}, dimensions={0}, use_global_device_ids=true | all-gather | bytes 992256 | tf_op jit(solution)/shard_map/all_gather | solution.py:687
  153.5 4.6 shard_map.253
  161.2 2.0 fusion.16
  164.4 4.1 shard_map.255.cotangent
  176.3 17.9 %collective-permute-done = bf16[512,1536]{1,0:T(8,128)(2,1)} collective-permute-done((bf16[512,1536]{1,0:T(8,128)(2,1)}, bf16[512,1536]{1,0:T(8,128)(2,1)}, u32[]{:S(2)}, u32[]{:S(2)}) %collective-permute-start) | collective-permute-done | bytes 1572896 | tf_op jit(solution)/shard_map/ppermute | solution.py:655
  195.9 2.0 pad_maximum_fusion.normed
  197.8 30.1 %collective-permute-done.1 = bf16[512,1536]{1,0:T(8,128)(2,1)} collective-permute-done((bf16[512,1536]{1,0:T(8,128)(2,1)}, bf16[512,1536]{1,0:T(8,128)(2,1)}, u32[]{:S(2)}, u32[]{:S(2)}) %collective-permute-start.1) | collective-permute-done | bytes 1572896 | tf_op jit(solution)/shard_map/ppermute | solution.py:655
  227.9 1.8 broadcast_select_fusion.1
  229.8 1.9 pad_maximum_fusion.1.cotangent
  231.7 31.3 %shard_map.254 = (bf16[1024,1536]{1,0:T(8,128)(2,1)}, bf16[1024,1536]{1,0:T(8,128)(2,1)}, f32[1024,1536]{1,0:T(8,128)}, bf16[1024,1536]{1,0:T(8,128)(2,1)}, bf16...) custom-call(s32[9]{0:T(128)} %pad_add_fusion.meta, ...), custom_call_target="tpu_custom_call" | custom-call | flops 7247757312 | bytes 40000000 | tf_op jit(solution)/shard_map/pallas_call | solution.py:276
  263.0 38.6 %shard_map.256 = (f32[1024,1536]{1,0:T(8,128)}, f32[1024,1536]{1,0:T(8,128)}, bf16[1024,1536]{1,0:T(8,128)(2,1)}, bf16[1024,1536]{1,0:T(8,128)(2,1)}, f32[1024,1...) custom-call(s32[9]{0:T(128)} %pad_add_fusion.meta, bf16[1024,1536]{1,0:T(8,128)(2,1)} %pad_maximum_fusion.normed, ...), custom_call_target="tpu_custom_call" | custom-call | flops 14495514624 | bytes 50000000 | tf_op jit(solution)/shard_map/pallas_call | solution.py:339
  302.9 3.3 constant_dynamic-slice_fusion.4
  309.1 33.6 %shard_map.259 = (bf16[1024,3072]{1,0:T(8,128)(2,1)}, bf16[1024,384]{1,0:T(8,128)(2,1)}, f32[128,1536]{1,0:T(8,128)}) custom-call(s32[9]{0:T(128)} %pad_add_fusion.meta, f32[1024,1536]{1,0:T(8,128)} %get-tuple-element.40.scan_out, f32[1024,1536]{1,0:T(8,128)} %get-tuple-element.46.gate_pre, f32[1024,1536]{1,0:T(8,128)} %get-tuple-element.47.weighted, ...), custom_call_target="tpu_custom_call" | custom-call | flops 14495514624 | bytes 50000000 | tf_op jit(solution)/shard_map/pallas_call | solution.py:517
  344.9 6.5 shard_map.257
  351.3 14.6 %all-to-all-start.2 = ((bf16[16,32,1536]{2,1,0:T(8,128)(2,1)}), bf16[16,32,1536]{2,1,0:T(8,128)(2,1)S(1)}, u32[]{:S(2)}, u32[]{:S(2)}) async-start(bf16[16,32,1536]{2,1,0:T(8,128)(2,1)} %bitcast.41), calls=%async_computation.2 | async-start | bytes 3145728 | tf_op jit(solution)/shard_map/all_to_all | solution.py:650
  365.9 24.0 %shard_map.260 = (bf16[1024,1536]{1,0:T(8,128)(2,1)}, f32[128,1536]{1,0:T(8,128)}, f32[128,3072]{1,0:T(8,128)}, f32[128,384]{1,0:T(8,128)}) custom-call(s32[9]{0:T(128)} %pad_add_fusion.meta, bf16[1024,3072]{1,0:T(8,128)(2,1)} %get-tuple-element.57.gz, bf16[1024,384]{1,0:T(8,128)(2,1)} %get-tuple-element.58.grest, ...), custom_call_target="tpu_custom_call" | custom-call | flops 12079595520 | bytes 40000000 | tf_op jit(solution)/shard_map/pallas_call | solution.py:576
  389.9 3.2 constant_dynamic-slice_fusion
  393.4 35.7 %collective-permute-done.5.other = bf16[512,1536]{1,0:T(8,128)(2,1)S(1)} collective-permute-done((bf16[512,1536]{1,0:T(8,128)(2,1)S(1)}, bf16[512,1536]{1,0:T(8,128)(2,1)S(1)}, u32[]{:S(2)}, u32[]{:S(2)}) %collective-permute-start.5) | collective-permute-done | bytes 1572896 | tf_op jit(solution)/shard_map/ppermute | solution.py:667
  430.2 6.4 shard_map.261
  437.8 6.5 all-to-all-start.3
  444.3 3.4 reshape.90
  450.7 112.3 %all-reduce.13.cloned.1.call-done = (f32[128,2,1536]{2,1,0:T(2,128)}, f32[1536,128]{0,1:T(8,128)}) async-done(((f32[128,2,1536]{2,1,0:T(2,128)}, f32[1536,128]{0,1:T(8,128)}), (f32[128,2,1536]{2,1,0:T(2,128)}, f32[1536,128]{0,1:T(8,128)})) %all-reduce.13.cloned.1.call-update) | async-done | bytes 2359312 | tf_op jit(solution)/shard_map/psum | solution.py:770
  563.0 2.3 copy.52
  565.3 137.9 %all-reduce.11.cloned.1.call-done = (f32[1536,128]{0,1:T(8,128)}, f32[128,304]{1,0:T(8,128)}, f32[128,1536]{1,0:T(8,128)}) async-done(((f32[1536,128]{0,1:T(8,128)}, f32[128,304]{1,0:T(8,128)}, f32[128,1536]{1,0:T(8,128)}), (f32[1536,128]{0,1:T(8,128)}, f32[128,304]{1,0:T(8,128)}, f32[128,1536]{1,0:T(8,128)})) %all-reduce.11.cloned.1.call-update) | async-done | bytes 1728528 | tf_op jit(solution)/shard_map/psum | solution.py:769
  703.2 2.3 copy.50
  706.3 4.0 shard_map.258
  711.4 4.1 shard_map.262
  (146 shorter events, 38.1 us)
Async XLA Ops:
  7.2 224.5 %all-gather.8.cloned.1.call-start = ((), (), s32[]{:S(2)}) async-start(), calls=%async_computation.5 | async-start | bytes 5013504 | tf_op jit(solution)/shard_map/all_gather | solution.py:684
  10.3 252.7 %all-gather.10.cloned.1.call-start = ((), (), s32[]{:S(2)}) async-start(), calls=%async_computation.6 | async-start | bytes 5013504 | tf_op jit(solution)/shard_map/all_gather | solution.py:685
  17.2 58.4 %all-to-all-start = ((bf16[16,32,1536]{2,1,0:T(8,128)(2,1)}), bf16[16,32,1536]{2,1,0:T(8,128)(2,1)S(1)}, u32[]{:S(2)}, u32[]{:S(2)}) async-start(bf16[16,32,1536]{2,1,0:T(8,128)(2,1)} %bitcast.42), calls=%async_computation | async-start | bytes 3145728 | tf_op jit(solution)/shard_map/all_to_all | solution.py:650
  24.6 238.4 %all-gather.6.cloned.1.call-start = ((), (), s32[]{:S(2)}) async-start(), calls=%async_computation.4 | async-start | bytes 5013504 | tf_op jit(solution)/shard_map/all_gather | solution.py:686
  75.6 16.3 %copy-start.21 = (s32[512]{0:T(512)S(1)}, s32[512]{0:T(512)}, u32[]{:S(2)}) copy-start(s32[512]{0:T(512)} %param.25) | copy-start | bytes 6148
  75.6 17.2 %copy-start.28 = (f32[1536]{0:T(1024)S(1)}, f32[1536]{0:T(1024)}, u32[]{:S(2)}) copy-start(f32[1536]{0:T(1024)} %param.27) | copy-start | bytes 18436
  75.6 17.8 %copy-start.34 = (s32[64]{0:T(128)S(1)}, s32[64]{0:T(128)}, u32[]{:S(2)}) copy-start(s32[64]{0:T(128)} %param.23) | copy-start | bytes 772
  75.6 18.0 %copy-start.35 = (f32[24]{0:T(128)S(1)}, f32[24]{0:T(128)}, u32[]{:S(2)}) copy-start(f32[24]{0:T(128)} %param.33) | copy-start | bytes 292
  75.6 18.5 %copy-start.15 = (bf16[128,304]{0,1:T(8,128)(2,1)S(1)}, bf16[128,304]{0,1:T(8,128)(2,1)}, u32[]{:S(2)}) copy-start(bf16[128,304]{0,1:T(8,128)(2,1)} %param.39) | copy-start | bytes 233476
  75.6 19.7 %copy-start.18 = (bf16[96,304]{1,0:T(8,128)(2,1)S(1)}, bf16[96,304]{1,0:T(8,128)(2,1)}, u32[]{:S(2)}) copy-start(bf16[96,304]{1,0:T(8,128)(2,1)} %param.29) | copy-start | bytes 175108
  76.7 86.5 %all-to-all-start.1 = ((bf16[16,32,1536]{2,1,0:T(8,128)(2,1)}), bf16[16,32,1536]{2,1,0:T(8,128)(2,1)S(1)}, u32[]{:S(2)}, u32[]{:S(2)}) async-start(bf16[16,32,1536]{2,1,0:T(8,128)(2,1)} %bitcast.17), calls=%async_computation.1 | async-start | bytes 3145728 | tf_op jit(solution)/shard_map/all_to_all | solution.py:650
  91.9 61.6 %copy-start.25 = (s32[512]{0:T(512)}, s32[512]{0:T(512)S(1)}, u32[]{:S(2)}) copy-start(s32[512]{0:T(512)S(1)} %fusion.13) | copy-start | bytes 6148
  153.5 5.9 copy-start.36
  153.5 6.4 copy-start.37
  158.1 36.1 %collective-permute-start = (bf16[512,1536]{1,0:T(8,128)(2,1)}, bf16[512,1536]{1,0:T(8,128)(2,1)}, u32[]{:S(2)}, u32[]{:S(2)}) collective-permute-start(bf16[512,1536]{1,0:T(8,128)(2,1)} %get-tuple-element.38), channel_id=1, source_target_pairs={{0,1},{1,0},{2,3},{3,2},{4,5},{5,4},{6,7},{7,6},{8,9},{9,8},{10,11... | collective-permute-start | bytes 4718600 | tf_op jit(solution)/shard_map/ppermute | solution.py:655
  164.4 5.2 copy-start.5
  164.4 6.0 copy-start.33
  164.4 6.7 copy-start.20
  168.5 59.5 %collective-permute-start.1 = (bf16[512,1536]{1,0:T(8,128)(2,1)}, bf16[512,1536]{1,0:T(8,128)(2,1)}, u32[]{:S(2)}, u32[]{:S(2)}) collective-permute-start(bf16[512,1536]{1,0:T(8,128)(2,1)} %shard_map.255.cotangent), channel_id=1, source_target_pairs={{0,1},{1,0},{2,3},{3,2},{4,5},{5,4},{6,7},{7,6},{8,9},{9,8},{10,11... | collective-permute-start | bytes 4718600 | tf_op jit(solution)/shard_map/ppermute | solution.py:655
  169.6 24.7 %copy-start.9 = (bf16[512,1536]{1,0:T(8,128)(2,1)S(1)}, bf16[512,1536]{1,0:T(8,128)(2,1)}, u32[]{:S(2)}) copy-start(bf16[512,1536]{1,0:T(8,128)(2,1)} %get-tuple-element.38) | copy-start | bytes 4718596
  195.9 32.1 %copy-start = (bf16[512,1536]{1,0:T(8,128)(2,1)S(1)}, bf16[512,1536]{1,0:T(8,128)(2,1)}, u32[]{:S(2)}) copy-start(bf16[512,1536]{1,0:T(8,128)(2,1)} %shard_map.255.cotangent) | copy-start | bytes 4718596
  301.6 6.9 collective-permute-start.4
  302.9 5.6 copy-start.23
  306.2 37.4 %collective-permute-start.2 = (bf16[512,1536]{1,0:T(8,128)(2,1)S(1)}, bf16[512,1536]{1,0:T(8,128)(2,1)S(1)}, u32[]{:S(2)}, u32[]{:S(2)}) collective-permute-start(bf16[512,1536]{1,0:T(8,128)(2,1)S(1)} %get-tuple-element.86), channel_id=1, source_target_pairs={{0,1},{1,0},{2,3},{3,2},{4,5},{5,4},{6,7},{7,6},{8,9},{9,8},{10,11... | collective-permute-start | bytes 4718600 | tf_op jit(solution)/shard_map/ppermute | solution.py:667
  307.1 36.4 %collective-permute-start.3 = (bf16[512,128]{1,0:T(8,128)(2,1)S(1)}, bf16[512,128]{1,0:T(8,128)(2,1)S(1)}, u32[]{:S(2)}, u32[]{:S(2)}) collective-permute-start(bf16[512,128]{1,0:T(8,128)(2,1)S(1)} %dynamic-slice_convert_fusion), channel_id=1, source_target_pairs={{0,1},{1,0},{2,3},{3,2},{4,5},{5,4},{6,7},{7,6},{8,9},{9,8},{10,11... | collective-permute-start | bytes 393224 | tf_op jit(solution)/shard_map/ppermute | solution.py:667
  309.1 33.6 %copy-start.19 = (f32[8,1024]{1,0:T(8,128)S(1)}, f32[8,1024]{1,0:T(8,128)}, u32[]{:S(2)}) copy-start(f32[8,1024]{1,0:T(8,128)} %add.67.stats) | copy-start | bytes 98308
  351.3 85.3 %all-to-all-start.2 = ((bf16[16,32,1536]{2,1,0:T(8,128)(2,1)}), bf16[16,32,1536]{2,1,0:T(8,128)(2,1)S(1)}, u32[]{:S(2)}, u32[]{:S(2)}) async-start(bf16[16,32,1536]{2,1,0:T(8,128)(2,1)} %bitcast.41), calls=%async_computation.2 | async-start | bytes 3145728 | tf_op jit(solution)/shard_map/all_to_all | solution.py:650
  393.1 36.0 %collective-permute-start.5 = (bf16[512,1536]{1,0:T(8,128)(2,1)S(1)}, bf16[512,1536]{1,0:T(8,128)(2,1)S(1)}, u32[]{:S(2)}, u32[]{:S(2)}) collective-permute-start(bf16[512,1536]{1,0:T(8,128)(2,1)S(1)} %get-tuple-element.84), channel_id=1, source_target_pairs={{0,1},{1,0},{2,3},{3,2},{4,5},{5,4},{6,7},{7,6},{8,9},{9,8},{10,11... | collective-permute-start | bytes 4718600 | tf_op jit(solution)/shard_map/ppermute | solution.py:667
  437.8 272.5 %all-to-all-start.3 = ((bf16[16,32,1536]{2,1,0:T(8,128)(2,1)}), bf16[16,32,1536]{2,1,0:T(8,128)(2,1)S(1)}, u32[]{:S(2)}, u32[]{:S(2)}) async-start(bf16[16,32,1536]{2,1,0:T(8,128)(2,1)} %bitcast.37), calls=%async_computation.3 | async-start | bytes 3145728 | tf_op jit(solution)/shard_map/all_to_all | solution.py:650
  444.3 118.8 %all-reduce.13.cloned.1.call-start = ((), (), s32[]{:S(2)}) async-start(), calls=%async_computation.8 | async-start | bytes 4718592 | tf_op jit(solution)/shard_map/psum | solution.py:770
  447.8 255.4 %all-reduce.11.cloned.1.call-start = ((), (), s32[]{:S(2)}) async-start(), calls=%async_computation.7 | async-start | bytes 3538944 | tf_op jit(solution)/shard_map/psum | solution.py:769
  449.8 255.7 %copy-start.22 = (s32[512]{0:T(512)}, s32[512]{0:T(512)S(1)}, u32[]{:S(2)}) copy-start(s32[512]{0:T(512)S(1)} %fusion.10) | copy-start | bytes 6148
  (22 other events, 49.1 us)
Sparse Core Ops, SparseCore 0:
  10.9 76.1 all-gather.7
  89.9 79.4 all-gather.9
  171.7 51.5 all-gather.5
  449.0 113.9 all-reduce.12
  569.2 133.9 all-reduce.10

commit v2 on v1

--- a/solution.py
+++ b/solution.py
@@ -16,6 +16,11 @@
 ADAPTER_RANK = 16
 SEQ_GROUP = 4
 REST_LOCAL = 2 * STATE + LANES
+META_HALF = 2 * SEQ_GROUP
+META_RANK = META_HALF + 1
+META_FIRST = META_HALF + 2
+META_THEIRS = META_HALF + 3
+COLUMNS = 512
 
 epsilon = 1e-05
 LOG2E = 1.4426950408889634
@@ -86,7 +91,7 @@
         in_specs=[scalar] * scalars + [vector] * (len(args) - scalars),
         out_specs=jax.tree.map(lambda _: vector, outs),
         compiler_params=pltpu.CompilerParams(vmem_limit_bytes=VMEM_BYTES),
-        cost_estimate=pl.CostEstimate(flops=flops, bytes_accessed=6_000_000, transcendentals=0),
+        cost_estimate=pl.CostEstimate(flops=flops, bytes_accessed=1_000_000, transcendentals=0),
     )(*args)
 
 
@@ -95,6 +100,22 @@
     for k in range(1, SEQ_GROUP):
         begin = jnp.where(position >= meta[k], meta[k], begin)
     return begin
+
+
+def row_specs(block, width, place):
+    def spec(side):
+        def index(i, meta):
+            half = meta[META_HALF]
+            return (jnp.clip(place(i, meta) - meta[side] * half, 0, half - 1), 0)
+
+        return pl.BlockSpec((block, width), index)
+
+    return [spec(META_RANK), spec(META_THEIRS)]
+
+
+def pick_rows(meta, place, mine, other):
+    own = place // meta[META_HALF] == meta[META_RANK]
+    return jnp.where(own, mine[...], other[...])
 
 
 def adapter_mask(meta, first, rows):
@@ -126,7 +147,7 @@
 
 
 def sigmoid(values):
-    return 1.0 / (1.0 + jnp.exp(-values))
+    return 0.5 * jnp.tanh(0.5 * values) + 0.5
 
 
 def column(values, h):
@@ -141,9 +162,10 @@
 
 def forward_kernel(
     meta,
-    normed, w_x, w_rest, down_in, up_x, up_rest, taps, taps_bc, step_bias, decay_rate, skip,
-    x_out, dx_out, y_out, state_out, bc_out, dbc_out, dt_out, sig_out, mid_out,
-    conv_in, rest, state, from_state, scaled,
+    mine, other, w_in, down_in, up_x, up_rest, up_gate, taps, taps_bc, step_bias, decay_rate, skip, gain,
+    x_out, dx_out, y_out, gate_out, gained_out, state_out, bc_out, dbc_out, dt_out, sig_out, mid_out,
+    square_out,
+    conv_in, rest, gate_pre, state, from_state, scaled,
     *, heads, block,
 ):
     i = pl.program_id(0)
@@ -161,11 +183,12 @@
     def _():
         conv_in[0:8, :] = conv_in[block : block + 8, :]
         rest[0:8, :] = rest[block : block + 8, :]
-        rows = normed[...]
+        rows = pick_rows(meta, i // per_block, mine, other)
         mid = (mm(rows, down_in[...]) * adapter_mask(meta, first, block)).astype(bf16)
         mid_out[...] = mid
-        conv_in[8 : block + 8, :] = mm(rows, w_x[...]) + mm(mid, up_x[...])
-        rest[8 : block + 8, :] = mm(rows, w_rest[...]) + mm(mid, up_rest[...])
+        conv_in[8 : block + 8, :] = mm(rows, w_in[:, 0:inner]) + mm(mid, up_x[...])
+        gate_pre[...] = mm(rows, w_in[:, inner : 2 * inner]) + mm(mid, up_gate[...])
+        rest[8 : block + 8, :] = mm(rows, w_in[:, 2 * inner :]) + mm(mid, up_rest[...])
 
     offset = pl.multiple_of((i % per_block) * CHUNK, CHUNK)
     window = pl.ds(offset, CHUNK + 8)
@@ -211,6 +234,7 @@
     from_state[...] = mm(c_mat, state_low)
     left = iota((CHUNK, LANES), 1) < HEADDIM
     left_row = left[0:1]
+    square = jnp.zeros((CHUNK, LANES), f32)
     for pair in range(heads // 2):
         h0, h1 = 2 * pair, 2 * pair + 1
         cols = slice(pair * LANES, (pair + 1) * LANES)
@@ -228,19 +252,24 @@
         )
         inside = mm(weights, x_split)
         reach = jnp.exp2(jnp.where(left, cum0, cum1)) * carried
-        y_out[:, cols] = inside + reach * from_state[:, cols] + skip[:, cols] * x
+        y = inside + reach * from_state[:, cols] + skip[:, cols] * x
+        y_out[:, cols] = y
+        gate = gate_pre[pl.ds(offset, CHUNK), cols]
+        gate_out[:, cols] = gate
+        gated = y * (gate * sigmoid(gate))
+        square = square + gated * gated
+        gained_out[:, cols] = (gated * gain[:, cols]).astype(bf16)
         total_pair = jnp.where(left_row, column(total, h0), column(total, h1))
         source_pair = jnp.where(left, column(source, h0), column(source, h1))
         coefficient = jnp.exp2(total_pair - source_pair) * in_last
         scaled[:, cols] = (x * coefficient).astype(bf16)
         state[:, cols] = state[:, cols] * (jnp.exp2(total_pair) * kept)
     state[...] += mm(b_mat, scaled[...], TN)
-
-
-def forward_scan(meta, normed, w_x, w_rest, down_in, up_x, up_rest, taps, taps_bc, bias, decay, skip, heads):
-    rows = normed.shape[0]
+    square_out[...] = jnp.sum(square.T, axis=0, keepdims=True)
+
+
+def forward_scan(meta, normed, w_in, down_in, up_x, up_rest, up_gate, taps, taps_bc, bias, decay, skip, gain, heads, rows, block):
     inner = heads * HEADDIM
-    block = min(BLOCK, rows)
     per_block = block // CHUNK
     chunk_rows = lambda width: pl.BlockSpec((CHUNK, width), lambda i, *_: (i, 0))
     block_rows = lambda width: pl.BlockSpec((block, width), lambda i, *_: (i // per_block, 0))
@@ -248,26 +277,32 @@
         jax.ShapeDtypeStruct((rows, inner), bf16),
         jax.ShapeDtypeStruct((rows, inner), bf16),
         jax.ShapeDtypeStruct((rows, inner), f32),
+        jax.ShapeDtypeStruct((rows, inner), f32),
+        jax.ShapeDtypeStruct((rows, inner), bf16),
         jax.ShapeDtypeStruct((rows // CHUNK * STATE, inner), bf16),
         jax.ShapeDtypeStruct((rows, 2 * STATE), bf16),
         jax.ShapeDtypeStruct((rows, 2 * STATE), f32),
         jax.ShapeDtypeStruct((rows, LANES), f32),
         jax.ShapeDtypeStruct((rows, LANES), f32),
         jax.ShapeDtypeStruct((rows, LANES), bf16),
-    )
-    operands = (w_x, w_rest, down_in, up_x, up_rest, taps, taps_bc, bias, decay, skip)
+        jax.ShapeDtypeStruct((1, rows), f32),
+    )
+    operands = (w_in, down_in, up_x, up_rest, up_gate, taps, taps_bc, bias, decay, skip, gain)
     grid = pltpu.PrefetchScalarGridSpec(
         num_scalar_prefetch=1,
         grid=(rows // CHUNK,),
-        in_specs=[block_rows(MODEL_WIDTH)] + [whole(a.shape) for a in operands],
+        in_specs=row_specs(block, MODEL_WIDTH, lambda i, meta: i // per_block)
+        + [whole(a.shape) for a in operands],
         out_specs=[
             chunk_rows(inner), chunk_rows(inner), chunk_rows(inner), chunk_rows(inner),
+            chunk_rows(inner), chunk_rows(inner),
             chunk_rows(2 * STATE), chunk_rows(2 * STATE), chunk_rows(LANES), chunk_rows(LANES),
-            block_rows(LANES),
+            block_rows(LANES), pl.BlockSpec((1, CHUNK), lambda i, *_: (0, i)),
         ],
         scratch_shapes=[
             pltpu.VMEM((block + 8, inner), f32),
             pltpu.VMEM((block + 8, REST_LOCAL), f32),
+            pltpu.VMEM((block, inner), f32),
             pltpu.VMEM((STATE, inner), f32),
             pltpu.VMEM((CHUNK, inner), f32),
             pltpu.VMEM((CHUNK, inner), bf16),
@@ -279,72 +314,119 @@
         grid_spec=grid,
         compiler_params=params(),
         cost_estimate=pl.CostEstimate(
-            flops=3 * rows * MODEL_WIDTH * inner, bytes_accessed=40_000_000, transcendentals=0
+            flops=5 * rows * MODEL_WIDTH * inner, bytes_accessed=50_000_000, transcendentals=0
         ),
-    )(meta, normed, *operands)
-
-
-def gate_kernel(
+    )(meta, *normed, *operands)
+
+
+def out_grad_kernel(
     meta,
-    normed, mid, scan_out, cotangent, w_gate, up_gate, w_out, down_out, up_out, gain,
-    gate_out, weighted_out, gained_out, part_out, mid_part_out, gmid_out, stats_out,
-    *, inner,
+    gd_mine, gd_other, gained, square, w_out, down_out, up_out, gain,
+    weighted_out, gmid_out, stats_out,
+    gd, cross,
+    *, pairwise,
 ):
-    block = normed.shape[0]
-    first = pl.program_id(0) * block
-    gate = mm(normed[...], w_gate[...]) + mm(mid[...], up_gate[...])
-    gate_out[...] = gate
-    gated = scan_out[...] * (gate * sigmoid(gate))
-    square = jnp.sum(gated * gated, axis=1, keepdims=True)
-    gained = (gated * gain[...]).astype(bf16)
-    gained_out[...] = gained
-    part_out[...] = mm(gained, w_out[...], NT).astype(bf16)
-    mid_part_out[...] = mm(gained, down_out[...])
-    gd = cotangent[...]
-    gmid = (mm(gd, up_out[...], NT) * adapter_mask(meta, first, block)).astype(bf16)
-    gmid_out[...] = gmid
-    weighted = (mm(gd, w_out[...]) + mm(gmid, down_out[...], NT)) * gain[...]
-    weighted_out[...] = weighted
-    cross = jnp.sum(weighted * gated, axis=1, keepdims=True)
-    lane = iota((block, LANES), 1)
-    stats = jnp.where(lane == 0, square, jnp.where(lane == 1, cross, 0.0))
-    stats_out[...] = stats.T[0:8, :]
-
-
-def gate_stage(meta, normed, mid, scan_out, cotangent, w_gate, up_gate, w_out, down_out, up_out, gain):
-    rows, inner = scan_out.shape
-    block = min(BLOCK, rows)
-    block_rows = lambda width: pl.BlockSpec((block, width), lambda i, *_: (i, 0))
-    operands = (w_gate, up_gate, w_out, down_out, up_out, gain)
+    step = pl.program_id(0)
+    rows = gd.shape[0]
+
+    @pl.when(step == 0)
+    def _():
+        if pairwise:
+            tokens = gd_mine.shape[0]
+            gd[pl.ds(pl.multiple_of(meta[META_FIRST], LANES), tokens), :] = gd_mine[...]
+            gd[pl.ds(pl.multiple_of(rows - tokens - meta[META_FIRST], LANES), tokens), :] = gd_other[...]
+        else:
+            gd[...] = gd_mine[...]
+        gmid = mm(gd[...], up_out[...], NT) * adapter_mask(meta, 0, rows)
+        gmid_out[...] = gmid.astype(bf16)
+        cross[...] = jnp.zeros_like(cross)
+
+    grad = mm(gd[...], w_out[...]) + mm(gmid_out[...], down_out[...], NT)
+    weighted_out[...] = grad * gain[...]
+    product = grad * gained[...].astype(f32)
+    total = cross[...]
+    for tile in range(product.shape[1] // LANES):
+        total = total + product[:, tile * LANES : (tile + 1) * LANES]
+    cross[...] = total
+
+    @pl.when(step == pl.num_programs(0) - 1)
+    def _():
+        row = jnp.sum(cross[...].T, axis=0, keepdims=True)
+        stats_out[...] = jnp.where(iota((8, rows), 0) == 0, square[...], row)
+
+
+def out_grad(meta, cotangent, gained, square, w_out, down_out, up_out, gain, pairwise):
+    rows, inner = gained.shape
+    width = 4 * LANES if inner % (4 * LANES) == 0 else LANES
+    columns = lambda height: pl.BlockSpec((height, width), lambda i, *_: (0, i))
     outs = (
         jax.ShapeDtypeStruct((rows, inner), f32),
-        jax.ShapeDtypeStruct((rows, inner), f32),
-        jax.ShapeDtypeStruct((rows, inner), bf16),
-        jax.ShapeDtypeStruct((rows, MODEL_WIDTH), bf16),
-        jax.ShapeDtypeStruct((rows, LANES), f32),
         jax.ShapeDtypeStruct((rows, LANES), bf16),
         jax.ShapeDtypeStruct((8, rows), f32),
     )
     grid = pltpu.PrefetchScalarGridSpec(
         num_scalar_prefetch=1,
-        grid=(rows // block,),
-        in_specs=[block_rows(MODEL_WIDTH), block_rows(LANES), block_rows(inner), block_rows(MODEL_WIDTH)]
-        + [whole(a.shape) for a in operands],
-        out_specs=[
-            block_rows(inner), block_rows(inner), block_rows(inner), block_rows(MODEL_WIDTH),
-            block_rows(LANES), block_rows(LANES),
-            pl.BlockSpec((8, block), lambda i, *_: (0, i)),
+        grid=(inner // width,),
+        in_specs=[
+            whole(cotangent[0].shape), whole(cotangent[1].shape), columns(rows), whole(square.shape),
+            columns(MODEL_WIDTH), pl.BlockSpec((width, LANES), lambda i, *_: (i, 0)),
+            whole(up_out.shape), columns(1),
         ],
+        out_specs=[columns(rows), whole(outs[1].shape), whole(outs[2].shape)],
+        scratch_shapes=[pltpu.VMEM((rows, MODEL_WIDTH), bf16), pltpu.VMEM((rows, LANES), f32)],
     )
     return pl.pallas_call(
-        partial(gate_kernel, inner=inner),
+        partial(out_grad_kernel, pairwise=pairwise),
         out_shape=outs,
         grid_spec=grid,
         compiler_params=params(),
         cost_estimate=pl.CostEstimate(
-            flops=6 * rows * MODEL_WIDTH * inner, bytes_accessed=50_000_000, transcendentals=0
+            flops=2 * rows * MODEL_WIDTH * inner, bytes_accessed=20_000_000, transcendentals=0
         ),
-    )(meta, normed, mid, scan_out, cotangent, *operands)
+    )(meta, *cotangent, gained, square, w_out, down_out, up_out, gain)
+
+
+def halves(meta_rows, width):
+    theirs = pl.BlockSpec((meta_rows, width), lambda i, meta: (meta[META_THEIRS], 0))
+    own = pl.BlockSpec((meta_rows, width), lambda i, meta: (meta[META_RANK], 0))
+    return theirs, own
+
+
+def out_project_kernel(meta, theirs, own, w_out, down_out, sent_out, kept_out):
+    step = pl.program_id(0)
+    width = w_out.shape[0]
+    columns = pl.ds(pl.multiple_of(step * width, LANES), width)
+    sent_out[:, columns] = mm(theirs[...], w_out[...], NT).astype(bf16)
+    kept_out[:, columns] = mm(own[...], w_out[...], NT).astype(bf16)
+
+    @pl.when(step == 0)
+    def _():
+        sent_out[:, MODEL_WIDTH:] = mm(theirs[...], down_out[...]).astype(bf16)
+        kept_out[:, MODEL_WIDTH:] = mm(own[...], down_out[...]).astype(bf16)
+
+
+def out_project(meta, gained, w_out, down_out, half_rows):
+    inner = gained.shape[1]
+    out = jax.ShapeDtypeStruct((half_rows, MODEL_WIDTH + LANES), bf16)
+    grid = pltpu.PrefetchScalarGridSpec(
+        num_scalar_prefetch=1,
+        grid=(MODEL_WIDTH // COLUMNS,),
+        in_specs=[
+            *halves(half_rows, inner),
+            pl.BlockSpec((COLUMNS, inner), lambda i, *_: (i, 0)),
+            whole(down_out.shape),
+        ],
+        out_specs=[whole(out.shape)] * 2,
+    )
+    return pl.pallas_call(
+        out_project_kernel,
+        out_shape=(out, out),
+        grid_spec=grid,
+        compiler_params=params(),
+        cost_estimate=pl.CostEstimate(
+            flops=4 * half_rows * MODEL_WIDTH * inner, bytes_accessed=15_000_000, transcendentals=0
+        ),
+    )(meta, gained, gained, w_out, down_out)
 
 
 def split_sum(values, indicator):
@@ -356,9 +438,9 @@
 def backward_kernel(
     meta,
     scan_out, gate_pre, weighted, x_in, slope_in, bc_in, dbc_in, dt_in, sig_in, state_in, stats,
-    gained, gmid, taps, taps_bc, decay_rate, skip, indicator,
-    gz_out, grest_out, gdown_out,
-    dstate, g_next, gbc_next, from_dstate, scaled, reached, product, source_product, row_product,
+    taps, taps_bc, decay_rate, skip, indicator,
+    gz_out, grest_out,
+    dstate, g_next, gbc_next, from_dstate, scaled, reached, product, source_product,
     *, heads, inner_all,
 ):
     i = pl.program_id(0)
@@ -370,8 +452,7 @@
         dstate[...] = jnp.zeros_like(dstate)
         g_next[...] = jnp.zeros_like(g_next)
         gbc_next[...] = jnp.zeros_like(gbc_next)
-        gdown_out[...] = jnp.zeros_like(gdown_out)
-        row_product[...] = jnp.zeros_like(row_product)
+        product[CHUNK:, :] = jnp.zeros((8, inner), f32)
 
     s_pos = first + iota((CHUNK, LANES), 0)
     begin = segment_start(meta, s_pos)
@@ -391,9 +472,6 @@
     row_id = iota((LANES, CHUNK), 0)
     both = jnp.where(row_id == 0, factor, jnp.where(row_id == 1, pull, 0.0)).T
     factor_col, pull_col = column(both, 0), column(both, 1)
-
-    gmid_scaled = (gmid[...].astype(f32) * factor_col).astype(bf16)
-    gdown_out[...] += mm(gmid_scaled, gained[...], TN)
 
     dt = dt_in[...]
     sig = sig_in[...]
@@ -447,13 +525,13 @@
         skip_row = skip[:, cols]
         gx = gx_scan + skip_row * gy
         x_side = x * gx_scan
-        source_product[:, cols] = x_side
-        product[:, cols] = gy * (y - skip_row * x) - x_side
+        source_product[:, cols] = x_side.astype(bf16)
+        product[0:CHUNK, cols] = gy * (y - skip_row * x) - x_side
         scaled[:, cols] = (x * coefficient).astype(bf16)
         reached[:, cols] = (gy * reach).astype(bf16)
         keep_row = jnp.exp2(total_pair) * kept
         dstate_cols = dstate[:, cols]
-        row_product[0:1, cols] = jnp.sum(x * outside, axis=0, keepdims=True) + keep_row * jnp.sum(
+        product[CHUNK : CHUNK + 1, cols] = jnp.sum(x * outside, axis=0, keepdims=True) + keep_row * jnp.sum(
             dstate_cols * state_in[:, cols].astype(f32), axis=0, keepdims=True
         )
         dstate[:, cols] = dstate_cols * keep_row
@@ -473,17 +551,16 @@
         gbc_next[:, cols] = gconv[0:8]
     dstate[...] += mm(c_mat, reached[...], TN)
 
-    grad_cumul = split_sum(product[...], indicator[...])
-    direct = split_sum(source_product[...], indicator[...])
-    grad_total = split_sum(row_product[...], indicator[...])[0:1]
-    grad_log = cumulate_back(grad_cumul) + grad_total
+    sums = split_sum(product[...], indicator[...])
+    direct = mm(source_product[...], indicator[...])
+    grad_log = cumulate_back(sums[0:CHUNK]) + sums[CHUNK : CHUNK + 1]
     ratio = jnp.where(dt > 1e-30, sig / jnp.maximum(dt, 1e-30), 1.0)
     grad_pre = direct * ratio - decay_rate[...] * grad_log * sig
     used = iota((CHUNK, LANES), 1) < heads
     grest_out[:, 2 * STATE : REST_LOCAL] = jnp.where(used, grad_pre, 0.0).astype(bf16)
 
 
-def backward_scan(meta, scan_out, gate_pre, weighted, x_act, slope, bc, dbc, dt, sig, states, stats, gained, gmid, taps, taps_bc, decay, skip, indicator, heads, inner_all):
+def backward_scan(meta, scan_out, gate_pre, weighted, x_act, slope, bc, dbc, dt, sig, states, stats, taps, taps_bc, decay, skip, indicator, heads, inner_all):
     rows, inner = scan_out.shape
     count = rows // CHUNK
     chunk_rows = lambda width: pl.BlockSpec((CHUNK, width), lambda i, *_: (count - 1 - i, 0))
@@ -492,16 +569,14 @@
     outs = (
         jax.ShapeDtypeStruct((rows, 2 * inner), bf16),
         jax.ShapeDtypeStruct((rows, REST_LOCAL), bf16),
-        jax.ShapeDtypeStruct((LANES, inner), f32),
     )
     grid = pltpu.PrefetchScalarGridSpec(
         num_scalar_prefetch=1,
         grid=(count,),
         in_specs=[chunk_rows(a.shape[1]) for a in streams]
         + [pl.BlockSpec((8, CHUNK), lambda i, *_: (0, count - 1 - i))]
-        + [chunk_rows(inner), chunk_rows(LANES)]
         + [whole(a.shape) for a in operands],
-        out_specs=[chunk_rows(2 * inner), chunk_rows(REST_LOCAL), whole((LANES, inner))],
+        out_specs=[chunk_rows(2 * inner), chunk_rows(REST_LOCAL)],
         scratch_shapes=[
             pltpu.VMEM((STATE, inner), f32),
             pltpu.VMEM((8, inner), f32),
@@ -509,9 +584,8 @@
             pltpu.VMEM((CHUNK, inner), f32),
             pltpu.VMEM((CHUNK, inner), bf16),
             pltpu.VMEM((CHUNK, inner), bf16),
-            pltpu.VMEM((CHUNK, inner), f32),
-            pltpu.VMEM((CHUNK, inner), f32),
-            pltpu.VMEM((8, inner), f32),
+            pltpu.VMEM((CHUNK + 8, inner), f32),
+            pltpu.VMEM((CHUNK, inner), bf16),
         ],
     )
     return pl.pallas_call(
@@ -522,81 +596,129 @@
         cost_estimate=pl.CostEstimate(
             flops=6 * rows * MODEL_WIDTH * inner, bytes_accessed=50_000_000, transcendentals=0
         ),
-    )(meta, *streams, stats, gained, gmid, *operands)
-
-
-def project_back_kernel(
+    )(meta, *streams, stats, *operands)
+
+
+def turn_tiles(out, first, values):
+    for tile in range(values.shape[1] // LANES):
+        out[:, first + tile * LANES : first + (tile + 1) * LANES] = values[
+            :, tile * LANES : (tile + 1) * LANES
+        ].T
+
+
+def adapter_back_kernel(
     meta,
-    gz, grest, normed, mid, w_gate, w_x, w_rest, down_in, up_gate, up_x, up_rest,
-    grad_out, gdown_out, gup_out, gup_rest_out,
-    *, inner,
+    gz, grest, normed_mine, normed_other, mid, gained, gmid_out_rows, stats, gup_out, up_gate, up_x, up_rest,
+    gmid_out, grads, down_in, down_out,
+    *, inner, inner_all,
 ):
     block = gz.shape[0]
-    first = pl.program_id(0) * block
-
-    @pl.when(pl.program_id(0) == 0)
+    place = pl.program_id(0)
+    rest_at = 2 * MODEL_WIDTH
+    zx_at = rest_at + REST_LOCAL
+    out_at = zx_at + 2 * inner
+
+    @pl.when(place == 0)
     def _():
-        gdown_out[...] = jnp.zeros_like(gdown_out)
-        gup_out[...] = jnp.zeros_like(gup_out)
-        gup_rest_out[...] = jnp.zeros_like(gup_rest_out)
-
-    ggate = gz[:, 0:inner]
-    gconv = gz[:, inner : 2 * inner]
+        grads[...] = jnp.zeros_like(grads)
+        grads[:, MODEL_WIDTH:rest_at] = gup_out[...]
+        down_in[...] = jnp.zeros_like(down_in)
+        down_out[...] = jnp.zeros_like(down_out)
+
     grest_rows = grest[...]
-    gmid = mm(ggate, up_gate[...], NT) + mm(gconv, up_x[...], NT) + mm(grest_rows, up_rest[...], NT)
-    gmid = (gmid * adapter_mask(meta, first, block)).astype(bf16)
-    grad = mm(ggate, w_gate[...], NT) + mm(gconv, w_x[...], NT)
-    grad = grad + mm(grest_rows, w_rest[...], NT) + mm(gmid, down_in[...], NT)
-    grad_out[...] = grad.astype(bf16)
+    gmid = mm(gz[:, 0:inner], up_gate[...], NT) + mm(gz[:, inner : 2 * inner], up_x[...], NT)
+    gmid = gmid + mm(grest_rows, up_rest[...], NT)
+    gmid = (gmid * adapter_mask(meta, place * block, block)).astype(bf16)
+    gmid_out[...] = gmid
     mid_rows = mid[...]
-    gdown_out[...] += mm(gmid, normed[...], TN)
-    gup_out[...] += mm(mid_rows, gz[...], TN)
-    gup_rest_out[...] += mm(mid_rows, grest_rows, TN)
-
-
-def project_back(meta, gz, grest, normed, mid, w_gate, w_x, w_rest, down_in, up_gate, up_x, up_rest):
+    down_in[...] += mm(gmid, pick_rows(meta, place, normed_mine, normed_other), TN)
+    grads[:, zx_at:out_at] += mm(mid_rows, gz[...], TN)
+    grads[:, rest_at:zx_at] += mm(mid_rows, grest_rows, TN)
+    factor = lax.rsqrt(stats[0:1, :] * (1.0 / inner_all) + epsilon)
+    factor_col = jnp.broadcast_to(factor, (LANES, block)).T
+    scaled = (gmid_out_rows[...].astype(f32) * factor_col).astype(bf16)
+    down_out[...] += mm(scaled, gained[...], TN)
+
+    @pl.when(place == pl.num_programs(0) - 1)
+    def _():
+        turn_tiles(grads, 0, down_in[...])
+        turn_tiles(grads, out_at, down_out[...])
+
+
+def adapter_back(meta, gz, grest, normed, mid, gained, gmid, stats, gup_out, up_gate, up_x, up_rest, block, inner_all):
     rows = gz.shape[0]
     inner = gz.shape[1] // 2
-    block = min(BLOCK, rows)
     block_rows = lambda width: pl.BlockSpec((block, width), lambda i, *_: (i, 0))
-    operands = (w_gate, w_x, w_rest, down_in, up_gate, up_x, up_rest)
-    outs = (
-        jax.ShapeDtypeStruct((rows, MODEL_WIDTH), bf16),
-        jax.ShapeDtypeStruct((LANES, MODEL_WIDTH), f32),
-        jax.ShapeDtypeStruct((LANES, 2 * inner), f32),
-        jax.ShapeDtypeStruct((LANES, REST_LOCAL), f32),
-    )
+    operands = (gup_out, up_gate, up_x, up_rest)
+    columns = 2 * MODEL_WIDTH + REST_LOCAL + 3 * inner
     grid = pltpu.PrefetchScalarGridSpec(
         num_scalar_prefetch=1,
         grid=(rows // block,),
-        in_specs=[block_rows(2 * inner), block_rows(REST_LOCAL), block_rows(MODEL_WIDTH), block_rows(LANES)]
+        in_specs=[block_rows(2 * inner), block_rows(REST_LOCAL)]
+        + row_specs(block, MODEL_WIDTH, lambda i, meta: i)
+        + [block_rows(LANES), block_rows(inner), block_rows(LANES)]
+        + [pl.BlockSpec((8, block), lambda i, *_: (0, i))]
         + [whole(a.shape) for a in operands],
-        out_specs=[block_rows(MODEL_WIDTH)] + [whole(o.shape) for o in outs[1:]],
+        out_specs=[block_rows(LANES), whole((LANES, columns))],
+        scratch_shapes=[pltpu.VMEM((LANES, MODEL_WIDTH), f32), pltpu.VMEM((LANES, inner), f32)],
     )
     return pl.pallas_call(
-        partial(project_back_kernel, inner=inner),
-        out_shape=outs,
+        partial(adapter_back_kernel, inner=inner, inner_all=inner_all),
+        out_shape=(
+            jax.ShapeDtypeStruct((rows, LANES), bf16),
+            jax.ShapeDtypeStruct((LANES, columns), f32),
+        ),
         grid_spec=grid,
         compiler_params=params(),
         cost_estimate=pl.CostEstimate(
-            flops=5 * rows * MODEL_WIDTH * inner, bytes_accessed=40_000_000, transcendentals=0
+            flops=2 * rows * LANES * (5 * inner + MODEL_WIDTH), bytes_accessed=20_000_000, transcendentals=0
         ),
-    )(meta, gz, grest, normed, mid, *operands)
+    )(meta, gz, grest, *normed, mid, gained, gmid, stats, *operands)
+
+
+def project_back_kernel(meta, gz, grest, gmid, w_in, down_in, grad_out, *, inner):
+    grad = mm(gz[:, 0:inner], w_in[:, inner : 2 * inner], NT)
+    grad = grad + mm(gz[:, inner : 2 * inner], w_in[:, 0:inner], NT)
+    grad = grad + mm(grest[...], w_in[:, 2 * inner :], NT) + mm(gmid[...], down_in[...], NT)
+    grad_out[...] = grad.astype(bf16)
+
+
+def project_back(meta, gz, grest, gmid, w_in, down_in, half_rows, side):
+    inner = gz.shape[1] // 2
+    rows_of = lambda width: halves(half_rows, width)[side]
+    grid = pltpu.PrefetchScalarGridSpec(
+        num_scalar_prefetch=1,
+        grid=(MODEL_WIDTH // COLUMNS,),
+        in_specs=[
+            rows_of(2 * inner), rows_of(REST_LOCAL), rows_of(LANES),
+            pl.BlockSpec((COLUMNS, w_in.shape[1]), lambda i, *_: (i, 0)),
+            pl.BlockSpec((COLUMNS, LANES), lambda i, *_: (i, 0)),
+        ],
+        out_specs=pl.BlockSpec((half_rows, COLUMNS), lambda i, *_: (0, i)),
+    )
+    return pl.pallas_call(
+        partial(project_back_kernel, inner=inner),
+        out_shape=jax.ShapeDtypeStruct((half_rows, MODEL_WIDTH), bf16),
+        grid_spec=grid,
+        compiler_params=params(),
+        cost_estimate=pl.CostEstimate(
+            flops=4 * half_rows * MODEL_WIDTH * inner, bytes_accessed=15_000_000, transcendentals=0
+        ),
+    )(meta, gz, grest, gmid, w_in, down_in)
 
 
 def output_kernel(
-    meta, key_col, key_row, resid, own, other, mid_own, mid_other, stats, cotangent, up_out,
+    meta, key_col, key_row, resid, own, other, stats, cotangent, up_out,
     sent_out, gup_out, *, inner_all,
 ):
     rows = resid.shape[0]
     row_id = iota((LANES, rows), 0)
     factor = lax.rsqrt(stats[0:1, :] * (1.0 / inner_all) + epsilon)
     factor_col = jnp.where(row_id == 0, factor, 0.0).T[:, 0:1]
-    first = meta[2 * SEQ_GROUP]
-    mid = (mid_own[...] + mid_other[...].astype(f32)) * factor_col
-    mid = (mid * adapter_mask(meta, first, rows)).astype(bf16)
+    first = meta[META_FIRST]
     summed = (own[...].astype(f32) + other[...].astype(f32)) * factor_col
-    result = resid[...].astype(f32) + summed + mm(mid, up_out[...])
+    mid = (summed[:, MODEL_WIDTH:] * adapter_mask(meta, first, rows)).astype(bf16)
+    result = resid[...].astype(f32) + summed[:, 0:MODEL_WIDTH] + mm(mid, up_out[...])
     select = pack_matrix(key_col[...], key_row[...])
     sent_out[...] = mm(select, result.astype(bf16)).astype(bf16)
     gup_out[...] = mm(mid, cotangent[...], TN)
@@ -611,6 +733,25 @@
     result = cotangent[...].astype(f32) + grad
     select = pack_matrix(key_col[...], key_row[...])
     sent_out[...] = mm(select, result.astype(bf16)).astype(bf16)
+
+
+def finish_kernel(
+    key_col, key_row, rows, total, rows_out, gdown_in, gup, gup_rest, gdown_out, gup_out
+):
+    select = unpack_matrix(key_col[...], key_row[...])
+    rows_out[...] = mm(select, rows[...]).astype(bf16)
+    inner = gup.shape[2]
+    rest_at = 2 * MODEL_WIDTH
+    zx_at = rest_at + REST_LOCAL
+    out_at = zx_at + 2 * inner
+    for first, out in ((0, gdown_in), (out_at, gdown_out)):
+        for tile in range(out.shape[0] // LANES):
+            span = slice(tile * LANES, (tile + 1) * LANES)
+            out[span, :] = total[:, first + tile * LANES : first + (tile + 1) * LANES].astype(f32)
+    gup_out[...] = total[:, MODEL_WIDTH:rest_at].astype(f32)
+    gup_rest[...] = total[:, rest_at:zx_at].astype(f32)[:, 0 : gup_rest.shape[1]]
+    gup[:, 0, :] = total[:, zx_at : zx_at + inner].astype(f32)
+    gup[:, 1, :] = total[:, zx_at + inner : out_at].astype(f32)
 
 
 def body(
@@ -644,32 +785,69 @@
     inner_all = inner * tensor_count
     dp_rank = lax.axis_index("dp")
     tensor_rank = lax.axis_index("tensor")
+    dp_count = lax.axis_size("dp")
     swap = [(0, 1), (1, 0)]
 
     def deal(rows):
         return lax.all_to_all(rows, "dp", split_axis=0, concat_axis=0, tiled=True)
 
+    pairwise = tensor_count == 2
+    block = min(BLOCK, group_rows)
+    block_count = group_rows // block
+    half_count = block_count // 2 if pairwise else block_count
+
     def gather_rows(mine):
-        if tensor_count != 2:
-            return lax.all_gather(mine, "tensor", axis=0, tiled=True)
-        other = lax.ppermute(mine, "tensor", swap)
-        first = tensor_rank == 0
-        return jnp.concatenate([jnp.where(first, mine, other), jnp.where(first, other, mine)])
+        if pairwise:
+            return mine, lax.ppermute(mine, "tensor", swap)
+        full = lax.all_gather(mine, "tensor", axis=0, tiled=True)
+        return full, full
 
     def own_rows(full, axis=0):
         return lax.dynamic_slice_in_dim(full, tensor_rank * tok_dev, tok_dev, axis)
 
-    def reduce_rows(full):
-        if tensor_count != 2:
-            summed = lax.psum_scatter(full.astype(f32), "tensor", scatter_dimension=0, tiled=True)
-            return summed, jnp.zeros_like(summed)
-        theirs = lax.dynamic_slice_in_dim(full, (1 - tensor_rank) * tok_dev, tok_dev, 0)
-        return own_rows(full), lax.ppermute(theirs.astype(bf16), "tensor", swap)
+    def sum_tensor(values):
+        if pairwise:
+            return values + lax.ppermute(values, "tensor", swap)
+        return lax.psum(values, "tensor")
+
+    def scatter_rows(full):
+        summed = lax.psum_scatter(full.astype(f32), "tensor", scatter_dimension=0, tiled=True)
+        return summed, jnp.zeros_like(summed)
+
+    bits = [1 << k for k in range(dp_count.bit_length() - 1)]
+
+    def exchange(values, bit):
+        pairs = [(k, k ^ bit) for k in range(dp_count)]
+        return lax.ppermute(values.astype(bf16), "dp", pairs)
+
+    def sum_dp(values, after):
+        height = values.shape[0] // dp_count
+        for bit, other_work in zip(bits, [None, *after] + [None] * len(bits)):
+            if other_work is not None:
+                values, _ = lax.optimization_barrier((values, other_work))
+            pairs = values.reshape(values.shape[0] // (2 * height), 2, height, values.shape[1])
+            mine = (dp_rank // bit) % 2
+            pick = lambda side: lax.dynamic_index_in_dim(pairs, side, 1, keepdims=False).reshape(
+                values.shape[0] // 2, values.shape[1]
+            )
+            values = pick(mine) + exchange(pick(1 - mine), bit).astype(f32)
+        return values
+
+    def spread_dp(share):
+        return lax.all_gather(share.astype(bf16), "dp", axis=0, tiled=True)
 
     group_lens = lax.dynamic_slice_in_dim(lengths, dp_rank * SEQ_GROUP, SEQ_GROUP)
     starts = jnp.cumsum(group_lens) - group_lens
     group_ids = lax.dynamic_slice_in_dim(sequence_adapter, dp_rank * SEQ_GROUP, SEQ_GROUP)
-    meta = jnp.concatenate([starts, group_ids, (tensor_rank * tok_dev)[None]]).astype(jnp.int32)
+    placing = jnp.stack(
+        [
+            jnp.int32(half_count),
+            tensor_rank if pairwise else jnp.int32(0),
+            tensor_rank * tok_dev,
+            1 - tensor_rank if pairwise else jnp.int32(0),
+        ]
+    )
+    meta = jnp.concatenate([starts, group_ids, placing]).astype(jnp.int32)
     slot = jnp.arange(tok_dev, dtype=jnp.int32)
     given_key = (perm // group_rows) * tok_dev + slot
     dealt_key = (dealt_position // group_rows) * tok_dev + slot
@@ -681,10 +859,6 @@
     move_flops = 2 * tok_dev * tok_dev * MODEL_WIDTH
     gain_row = block_norm_gain[None, :]
 
-    w_x = lax.all_gather(gate_input_weight[:, 1, :], "dp", axis=0, tiled=True)
-    w_gate = lax.all_gather(gate_input_weight[:, 0, :], "dp", axis=0, tiled=True)
-    w_out = lax.all_gather(output_weight.T, "dp", axis=0, tiled=True)
-    rest_full = lax.all_gather(rest_weight, "dp", axis=0, tiled=True)
     dt_start = 2 * STATE + tensor_rank * heads
 
     def local_rest(matrix):
@@ -693,7 +867,13 @@
             [matrix[:, : 2 * STATE], jnp.pad(steps, ((0, 0), (0, LANES - heads)))], axis=1
         )
 
-    w_rest = local_rest(rest_full)
+    def gather_weight(*shards):
+        return lax.all_gather(jnp.concatenate(shards, axis=1), "dp", axis=0, tiled=True)
+
+    w_in = gather_weight(
+        gate_input_weight[:, 1, :], gate_input_weight[:, 0, :], local_rest(rest_weight)
+    )
+    w_out = gather_weight(output_weight.T)
     up_rest = local_rest(adapter_up_rest)
     up_gate = adapter_up_gate_input[:, 0, :]
     up_x = adapter_up_gate_input[:, 1, :]
@@ -719,64 +899,81 @@
     )
     grad_full = gather_rows(grad_mine)
 
-    x_act, slope, scan_out, states, bc, dbc, dt, sig, mid_in = forward_scan(
-        meta, normed, w_x, w_rest, adapter_down_in, up_x, up_rest, taps, taps_bc,
-        bias_row, decay_row, skip_row, heads,
-    )
-    gate_pre, weighted, gained, part, mid_part, gmid, stats = gate_stage(
-        meta, normed, mid_in, scan_out, grad_full, w_gate, up_gate, w_out, adapter_down_out,
-        adapter_up_out, gated_norm_gain[None, :],
-    )
-    if tensor_count == 2:
-        stats = stats + lax.ppermute(stats, "tensor", swap)
+    gated_gain = gated_norm_gain[None, :]
+    x_act, slope, scan_out, gate_pre, gained, states, bc, dbc, dt, sig, mid_in, square = forward_scan(
+        meta, normed, w_in, adapter_down_in, up_x, up_rest, up_gate, taps, taps_bc,
+        bias_row, decay_row, skip_row, gated_gain, heads, group_rows, block,
+    )
+    weighted, gmid, stats = out_grad(
+        meta, grad_full, gained, square, w_out, adapter_down_out, adapter_up_out, gated_gain, pairwise
+    )
+    half_rows = tok_dev if pairwise else group_rows
+    gained, _ = lax.optimization_barrier((gained, stats))
+    part_sent, part_own = out_project(meta, gained, w_out, adapter_down_out, half_rows)
+    stats = sum_tensor(stats)
+    if pairwise:
+        part_sent, stats = lax.optimization_barrier((part_sent, stats))
+        part_other = lax.ppermute(part_sent, "tensor", swap)
     else:
-        stats = lax.psum(stats, "tensor")
-    part_own, part_other = reduce_rows(part)
-    mid_own, mid_other = reduce_rows(mid_part)
+        part_own, part_other = scatter_rows(part_sent)
+
+    gz, grest = backward_scan(
+        meta, scan_out, gate_pre, weighted, x_act, slope, bc, dbc, dt, sig, states, stats,
+        taps, taps_bc, decay_row, skip_row, indicator, heads, inner_all,
+    )
+    part_other, _ = lax.optimization_barrier((part_other, gz))
     sent_output, gup_out = simple_call(
         partial(output_kernel, inner_all=inner_all),
         (token_rows, jax.ShapeDtypeStruct((LANES, MODEL_WIDTH), f32)), 2 * move_flops,
-        meta, *keys(perm), resid, part_own, part_other, mid_own, mid_other,
+        meta, *keys(perm), resid, part_own, part_other,
         own_rows(stats, 1), grad_mine, adapter_up_out, scalars=1,
     )
-    output = simple_call(
-        unpack_kernel, token_rows, move_flops, *keys(dealt_key), deal(sent_output)
-    )
-
-    gz, grest, gdown_out = backward_scan(
-        meta, scan_out, gate_pre, weighted, x_act, slope, bc, dbc, dt, sig, states, stats,
-        gained, gmid, taps, taps_bc, decay_row, skip_row, indicator, heads, inner_all,
-    )
-    grad_part, gdown_in, gup_zx, gup_rest = project_back(
-        meta, gz, grest, normed, mid_in, w_gate, w_x, w_rest, adapter_down_in, up_gate, up_x, up_rest
-    )
-    grad_own, grad_other = reduce_rows(grad_part)
+    dealt_output = deal(sent_output)
+    gmid_in, gradients = adapter_back(
+        meta, gz, grest, normed, mid_in, gained, gmid, stats, gup_out, up_gate, up_x, up_rest,
+        block, inner_all,
+    )
+    gz, _ = lax.optimization_barrier((gz, gradients))
+    back = partial(project_back, meta, gz, grest, gmid_in, w_in, adapter_down_in, half_rows)
+    if pairwise:
+        sent_back = back(0)
+        grad_other = lax.ppermute(sent_back, "tensor", swap)
+        gz, _, dealt_output = lax.optimization_barrier((gz, sent_back, dealt_output))
+        grad_own = project_back(meta, gz, grest, gmid_in, w_in, adapter_down_in, half_rows, 1)
+    else:
+        grad_own, grad_other = scatter_rows(back(0))
+    output = simple_call(unpack_kernel, token_rows, move_flops, *keys(dealt_key), dealt_output)
+    grad_other, output = lax.optimization_barrier((grad_other, output))
     sent_grad = simple_call(
         input_grad_kernel, token_rows, move_flops,
         *keys(perm), resid, grad_own, grad_other, grad_mine, gain_row,
     )
-    input_grad = simple_call(
-        unpack_kernel, token_rows, move_flops, *keys(dealt_key), deal(sent_grad)
-    )
-
-    rest_width = adapter_up_rest.shape[1]
-    wide = jnp.concatenate(
-        [gup_rest[:, : 2 * STATE], jnp.zeros((LANES, rest_width - 2 * STATE), f32)], axis=1
-    )
-    gup_rest = lax.dynamic_update_slice(
-        wide, gup_rest[:, 2 * STATE : 2 * STATE + heads], (0, dt_start)
-    )
-    gdown_in, gup_rest, gup_out = lax.psum((gdown_in, gup_rest, gup_out), ("dp", "tensor"))
-    gup_zx, gdown_out = lax.psum((gup_zx, gdown_out), "dp")
-    return (
-        output,
-        input_grad,
-        gdown_in.T,
-        gup_zx.reshape(LANES, 2, inner),
-        gup_rest,
-        gdown_out.T,
-        gup_out,
-    )
+
+    rest_at = 2 * MODEL_WIDTH
+    zx_at = rest_at + REST_LOCAL
+    out_at = zx_at + 2 * inner
+    total = sum_dp(gradients, (sent_back, grad_own, grad_other) if pairwise else ())
+    steps = total[:, rest_at + 2 * STATE : rest_at + 2 * STATE + heads]
+    wide = jnp.zeros((total.shape[0], LANES), f32)
+    wide = lax.dynamic_update_slice(wide, steps, (0, tensor_rank * heads))
+    shared = jnp.concatenate([total[:, : rest_at + 2 * STATE], wide], axis=1)
+    share = jnp.concatenate([sum_tensor(shared), total[:, zx_at:]], axis=1)
+    share, sent_grad = lax.optimization_barrier((share, sent_grad))
+    total = spread_dp(share)
+    dealt_grad = deal(sent_grad)
+    input_grad, gdown_in, gup_zx, gup_rest, gdown_out, gup_out = simple_call(
+        finish_kernel,
+        (
+            token_rows,
+            jax.ShapeDtypeStruct((MODEL_WIDTH, LANES), f32),
+            jax.ShapeDtypeStruct((LANES, 2, inner), f32),
+            jax.ShapeDtypeStruct((LANES, adapter_up_rest.shape[1]), f32),
+            jax.ShapeDtypeStruct((inner, LANES), f32),
+            jax.ShapeDtypeStruct((LANES, MODEL_WIDTH), f32),
+        ),
+        move_flops, *keys(dealt_key), dealt_grad, total,
+    )
+    return output, input_grad, gdown_in, gup_zx, gup_rest, gdown_out, gup_out
 
 
 def solution(mesh):

time: 726 us -> 451 us (0.62)
  waiting for transfers between devices: 385 us -> 97.8 us
  blocking collectives: 57.9 us -> 117 us
  starting transfers between devices: 48.3 us -> 21.8 us
  local copies, waits for them, and re-layouts: 44.5 us -> 21.7 us
  Pallas kernels: 162 us -> 172 us
    psum x2 -> x0, waiting for transfers between devices: 250 us -> none  [the longest x1 138 us: body(): lax.psum((gdown_in, gup_rest, gup_out), ('dp', 'tensor'))]
    all_to_all x0 -> x2, blocking collectives: none -> 117 us  [deal(): return lax.all_to_all(rows, 'dp', split_axis=0, concat_axis=0, tiled=True)]
    all_gather x1 -> x0, blocking collectives: 57.9 us -> none  [body(): rest_full = lax.all_gather(rest_weight, 'dp', axis=0, tiled=True)]
    ppermute x6 -> x10, waiting for transfers between devices: 84.1 us -> 32.9 us  [the longest x4 27.7 us: exchange(): return lax.ppermute(values.astype(bf16), 'dp', pairs)]
    all_to_all x4 -> x2, starting transfers between devices: 43.6 us -> 9.13 us  [deal(): return lax.all_to_all(rows, 'dp', split_axis=0, concat_axis=0, tiled=True)]
    all_gather x3, waiting for transfers between devices: 0.04 us -> 23.8 us  [the longest x2 23.8 us: gather_weight(): lax.all_gather(jnp.concatenate(shards, axis=1), 'dp', axis=0, tiled=True)]
    unnamed x87 -> x49, local copies, waits for them, and re-layouts: 19.9 us -> 4.35 us
    pallas_call x1, Pallas kernels: 31.3 us -> 41.3 us  [forward_scan(): pl.pallas_call(partial(forward_kernel, heads=heads, block=block), out_sha...]
  transfers between devices with their start and end apart: 15 -> 15, of which waited for: 7 -> 7; matrix products, arithmetic and copies ran while one was open for 6% -> 3% of each run, Pallas kernels for 16% -> 29%
where the time goes in v2:
time: 451 us; the launch traced here: 450 us
  Pallas kernels  172 us (38%)
  blocking collectives  117 us (26%)
  waiting for transfers between devices  97.8 us (22%)
  starting transfers between devices  21.8 us (5%)
  local copies, waits for them, and re-layouts  21.7 us (5%)
  between operations  14.1 us (3%)
  other arithmetic  4.96 us (1%)
    all_to_all x2, blocking collectives, deal(): return lax.all_to_all(rows, 'dp', split_axis=0, concat_axis=0, tiled=True)  117 us
    pallas_call x1, Pallas kernels, forward_scan(): pl.pallas_call(partial(forward_kernel, heads=heads, block=block), out_sha...  41.3 us
    all_to_all x2, waiting for transfers between devices, deal(): return lax.all_to_all(rows, 'dp', split_axis=0, concat_axis=0, tiled=True)  40.4 us
    pallas_call x7, Pallas kernels, simple_call(): pl.pallas_call(kernel, out_shape=outs, in_specs=[scalar] * scalars + [vec...  36.7 us
    pallas_call x1, Pallas kernels, backward_scan(): pl.pallas_call(partial(backward_kernel, heads=heads, inner_all=inner_all)...  31.4 us
    ppermute x4, waiting for transfers between devices, exchange(): return lax.ppermute(values.astype(bf16), 'dp', pairs)  27.7 us
    all_gather x2, waiting for transfers between devices, gather_weight(): lax.all_gather(jnp.concatenate(shards, axis=1), 'dp', axis=0, tiled=True)  23.8 us
    pallas_call x2, Pallas kernels, project_back(): pl.pallas_call(partial(project_back_kernel, inner=inner), out_shape=jax.S...  23.4 us
  transfers between devices with their start and end apart: 15, of which 7 were waited for; matrix products, arithmetic and copies ran while one was open for 3% of the time, Pallas kernels for 29%

profile of v2, /device:TPU:1, one launch (start us, length us, event | category | flops | bytes accessed | tf_op | source)
XLA Modules:
  0.0 450.0 jit_solution(5920387121544571326)
XLA Ops:
  8.0 2.3 fusion.22
  13.0 5.2 %shard_map.252 = (bf16[512,1536]{1,0:T(8,128)(2,1)}, bf16[512,1536]{1,0:T(8,128)(2,1)}) custom-call(s32[512,1]{1,0:T(8,128)} %copy.49.key_col, s32[1,512]{1,0:T(1,128)} %bitcast.79, bf16[512,1536]{1,0:T(8,128)(2,1)} %first.1, bf16[512,1536]{1,0:T(8,128)(2,1)} %second.1), custom_call_target="tpu_custom_call" | custom-call | flops 1610612736 | bytes 1000000 | tf_op jit(solution)/shard_map/pallas_call | solution.py:88
  18.2 61.9 %all_to_all.45 = bf16[16,32,1536]{2,1,0:T(8,128)(2,1)} all-to-all(bf16[16,32,1536]{2,1,0:T(8,128)(2,1)} %bitcast.68), channel_id=1, replica_groups=mesh['dp'=16,'tensor'=2] {'dp'}, dimensions={0} | all-to-all | bytes 3145728 | tf_op jit(solution)/shard_map/all_to_all | solution.py:792
  80.1 4.8 %all-to-all-start.1 = ((bf16[16,32,1536]{2,1,0:T(8,128)(2,1)}), bf16[16,32,1536]{2,1,0:T(8,128)(2,1)S(1)}, u32[]{:S(2)}, u32[]{:S(2)}) async-start(bf16[16,32,1536]{2,1,0:T(8,128)(2,1)} %bitcast.17), calls=%async_computation.1 | async-start | bytes 3145728 | tf_op jit(solution)/shard_map/all_to_all | solution.py:792
  86.8 4.7 %shard_map.253 = (bf16[512,1536]{1,0:T(8,128)(2,1)}, bf16[512,1536]{1,0:T(8,128)(2,1)}) custom-call(s32[512,1]{1,0:T(8,128)} %copy.50.key_col, s32[1,512]{1,0:T(1,128)} %bitcast.77, bf16[512,1536]{1,0:T(8,128)(2,1)} %bitcast.67, f32[1,1536]{1,0:T(1,128)} %broadcast_in_dim.54.gain), custom_call_target="tpu_custom_call" | custom-call | flops 805306368 | bytes 1000000 | tf_op jit(solution)/shard_map/pallas_call | solution.py:88
  99.2 2.0 fusion.21
  101.1 40.4 %all-to-all-done.1 = bf16[16,32,1536]{2,1,0:T(8,128)(2,1)S(1)} async-done(((bf16[16,32,1536]{2,1,0:T(8,128)(2,1)}), bf16[16,32,1536]{2,1,0:T(8,128)(2,1)S(1)}, u32[]{:S(2)}, u32[]{:S(2)}) %all-to-all-start.1) | async-done | bytes 1572896 | tf_op jit(solution)/shard_map/all_to_all | solution.py:792
  142.7 4.1 shard_map.255.gd_mine.cotangent
  146.8 1.5 collective-permute-start.1
  149.3 10.5 %all-gather.4.cloned.1.call-done.w_in = bf16[1536,3456]{1,0:T(8,128)(2,1)} async-done(((bf16[96,3456]{1,0:T(8,128)(2,1)}), bf16[1536,3456]{1,0:T(8,128)(2,1)}) %all-gather.4.cloned.1.call-update) | async-done | bytes 10616848 | tf_op jit(solution)/shard_map/all_gather | solution.py:871
  159.8 41.3 %shard_map.254 = (bf16[1024,1536]{1,0:T(8,128)(2,1)}, bf16[1024,1536]{1,0:T(8,128)(2,1)}, f32[1024,1536]{1,0:T(8,128)}, f32[1024,1536]{1,0:T(8,128)}, bf16[1024,...) custom-call(s32[12]{0:T(128)} %concatenate.15.meta, ...), custom_call_target="tpu_custom_call" | custom-call | flops 12079595520 | bytes 50000000 | tf_op jit(solution)/shard_map/pallas_call | solution.py:311
  201.2 13.2 %all-gather.6.cloned.1.call-done.w_out = bf16[1536,1536]{1,0:T(8,128)(2,1)} async-done(((bf16[96,1536]{1,0:T(8,128)(2,1)}), bf16[1536,1536]{1,0:T(8,128)(2,1)}) %all-gather.6.cloned.1.call-update) | async-done | bytes 4718608 | tf_op jit(solution)/shard_map/all_gather | solution.py:871
  214.4 13.4 %shard_map.256 = (f32[1024,1536]{1,0:T(8,128)}, bf16[1024,128]{1,0:T(8,128)(2,1)}, f32[8,1024]{1,0:T(8,128)}) custom-call(s32[12]{0:T(128)} %concatenate.15.meta, bf16[512,1536]{1,0:T(8,128)(2,1)} %shard_map.255.gd_mine.cotangent, bf16[512,1536]{1,0:T(8,128)(2,1)} %copy-done.19, bf16[1024,1536]{1,0:T(8,128)(2,1)} %get-tuple-element.70.gained.theirs.own, ...), custom_call_target="tpu_custom_call" | custom-call | flops 4831838208 | bytes 20000000 | tf_op jit(solution)/shard_map/pallas_call | solution.py:378
  229.1 11.6 %shard_map.257 = (bf16[512,1664]{1,0:T(8,128)(2,1)}, bf16[512,1664]{1,0:T(8,128)(2,1)}) custom-call(s32[12]{0:T(128)} %concatenate.15.meta, bf16[1024,1536]{1,0:T(8,128)(2,1)} %get-tuple-element.70.gained.theirs.own, bf16[1024,1536]{1,0:T(8,128)(2,1)} %get-tuple-element.70.gained.theirs.own, bf16[1536,1536]{1,0:T(8,128)(2,1)} %all-gather.6.cloned.1.call-done.w_out, ...), custom_call_target="tpu_custom_call" | custom-call | flops 4831838208 | bytes 15000000 | tf_op jit(solution)/shard_map/pallas_call | solution.py:421
  242.6 31.4 %shard_map.258 = (bf16[1024,3072]{1,0:T(8,128)(2,1)}, bf16[1024,384]{1,0:T(8,128)(2,1)}) custom-call(s32[12]{0:T(128)} %concatenate.15.meta, f32[1024,1536]{1,0:T(8,128)} %get-tuple-element.56.scan_out, f32[1024,1536]{1,0:T(8,128)} %get-tuple-element.57.gate_pre, f32[1024,1536]{1,0:T(8,128)} %get-tuple-element.61.weighted, ...), custom_call_target="tpu_custom_call" | custom-call | flops 14495514624 | bytes 50000000 | tf_op jit(solution)/shard_map/pallas_call | solution.py:591
  274.0 5.2 %collective-permute-done.3.other = bf16[512,1664]{1,0:T(8,128)(2,1)S(1)} collective-permute-done((bf16[512,1664]{1,0:T(8,128)(2,1)}, bf16[512,1664]{1,0:T(8,128)(2,1)S(1)}, u32[]{:S(2)}, u32[]{:S(2)}) %collective-permute-start.3) | collective-permute-done | bytes 1703968 | tf_op jit(solution)/shard_map/ppermute | solution.py:916
  280.3 6.4 %shard_map.259 = (bf16[512,1536]{1,0:T(8,128)(2,1)}, f32[128,1536]{1,0:T(8,128)}) custom-call(s32[12]{0:T(128)} %concatenate.15.meta, s32[512,1]{1,0:T(8,128)} %copy.58.key_col, s32[1,512]{1,0:T(1,128)} %bitcast.73, bf16[512,1536]{1,0:T(8,128)(2,1)} %get-tuple-element.77.resid, bf16[512,1664]{1,0:T(8,128)(2,1)} %get-tuple-element.78.own, ...), custom_call_target="tpu_custom_call" | custom-call | flops 1610612736 | bytes 1000000 | tf_op jit(solution)/shard_map/pallas_call | solution.py:88
  286.8 14.5 %shard_map.260 = (bf16[1024,128]{1,0:T(8,128)(2,1)}, f32[128,8064]{1,0:T(8,128)}) custom-call(s32[12]{0:T(128)} %concatenate.15.meta, bf16[1024,3072]{1,0:T(8,128)(2,1)} %get-tuple-element.89.gz, bf16[1024,384]{1,0:T(8,128)(2,1)} %get-tuple-element.74.grest, bf16[512,1536]{1,0:T(8,128)(2,1)} %get-tuple-element.55.mine.normed_mine, ...), custom_call_target="tpu_custom_call" | custom-call | flops 2415919104 | bytes 20000000 | tf_op jit(solution)/shard_map/pallas_call | solution.py:665
  301.3 1.7 fusion.1
  304.4 4.3 all-to-all-start.2
  308.8 11.9 %shard_map.261 = bf16[512,1536]{1,0:T(8,128)(2,1)} custom-call(s32[12]{0:T(128)} %concatenate.15.meta, bf16[1024,3072]{1,0:T(8,128)(2,1)} %get-tuple-element.89.gz, bf16[1024,384]{1,0:T(8,128)(2,1)} %get-tuple-element.74.grest, bf16[1024,128]{1,0:T(8,128)(2,1)} %get-tuple-element.84.gmid, bf16[1536,3456]{1,0:T(8,128)(2,1)} %all-gather.4.cloned.1.call-done.w_in, ...), custom_call_target="tpu_custom_call" | custom-call | flops 4831838208 | bytes 15000000 | tf_op jit(solution)/shard_map/pallas_call | solution.py:699
  322.9 19.1 %collective-permute-done.6 = bf16[32,8064]{1,0:T(8,128)(2,1)} collective-permute-done((bf16[32,8064]{1,0:T(8,128)(2,1)S(1)}, bf16[32,8064]{1,0:T(8,128)(2,1)}, u32[]{:S(2)}, u32[]{:S(2)}) %collective-permute-start.6) | collective-permute-done | bytes 516128 | tf_op jit(solution)/shard_map/ppermute | solution.py:821
  343.1 11.5 %shard_map.263.own = bf16[512,1536]{1,0:T(8,128)(2,1)} custom-call(s32[12]{0:T(128)} %concatenate.15.meta, bf16[1024,3072]{1,0:T(8,128)(2,1)} %get-tuple-element.89.gz, bf16[1024,384]{1,0:T(8,128)(2,1)} %get-tuple-element.74.grest, bf16[1024,128]{1,0:T(8,128)(2,1)} %get-tuple-element.84.gmid, bf16[1536,3456]{1,0:T(8,128)(2,1)} %all-gather.4.cloned.1.call-done.w_in, ...), custom_call_target="tpu_custom_call" | custom-call | flops 4831838208 | bytes 15000000 | tf_op jit(solution)/shard_map/pallas_call | solution.py:699
  354.6 2.7 collective-permute-start.7
  358.2 4.0 shard_map.262
  362.2 1.9 collective-permute-done.7
  364.1 1.5 collective-permute-start.8
  365.6 6.7 %collective-permute-done.8 = bf16[8,8064]{1,0:T(8,128)(2,1)S(1)} collective-permute-done((bf16[8,8064]{1,0:T(8,128)(2,1)S(1)}, bf16[8,8064]{1,0:T(8,128)(2,1)S(1)}, u32[]{:S(2)}, u32[]{:S(2)}) %collective-permute-start.8) | collective-permute-done | bytes 129056 | tf_op jit(solution)/shard_map/ppermute | solution.py:821
  373.3 6.3 %shard_map.264 = bf16[512,1536]{1,0:T(8,128)(2,1)} custom-call(s32[512,1]{1,0:T(8,128)} %copy.58.key_col, s32[1,512]{1,0:T(1,128)} %bitcast.74, bf16[512,1536]{1,0:T(8,128)(2,1)} %get-tuple-element.77.resid, bf16[512,1536]{1,0:T(8,128)(2,1)} %shard_map.263.own, bf16[512,1536]{1,0:T(8,128)(2,1)} %collective-permute-done.4.other, ...), custom_call_target="tpu_custom_call" | custom-call | flops 805306368 | bytes 1000000 | tf_op jit(solution)/shard_map/pallas_call | solution.py:88
  380.3 55.5 %all_to_all.46 = bf16[16,32,1536]{2,1,0:T(8,128)(2,1)} all-to-all(bf16[16,32,1536]{2,1,0:T(8,128)(2,1)} %bitcast.59), channel_id=1, replica_groups=mesh['dp'=16,'tensor'=2] {'dp'}, dimensions={0} | all-to-all | bytes 3145728 | tf_op jit(solution)/shard_map/all_to_all | solution.py:792
  435.8 6.0 %shard_map.265 = (bf16[512,1536]{1,0:T(8,128)(2,1)}, f32[1536,128]{1,0:T(8,128)}, f32[128,2,1536]{2,1,0:T(2,128)}, f32[128,304]{1,0:T(8,128)}, f32[1536,128]{1,0:T(8,128)}, /*index=5*/f32[128,1536]{1,0:T(8,128)}) custom-call(s32[512,1]{1,0:T(8,128)} %copy.59.key_col, s32[1,512]{1,0:T(1,128)} %bitcast.72, bf16[512,1536]{1,0:T(8,128)(2,1)} %bitcast.60, ...), custom_call_target="tpu_custom_call" | custom-call | flops 805306368 | bytes 1000000 | tf_op jit(solution)/shard_map/pallas_call | solution.py:88
  441.8 1.7 copy.62
  (117 shorter events, 26.8 us)
Async XLA Ops:
  7.2 152.7 %all-gather.4.cloned.1.call-start = ((), (), s32[]{:S(2)}) async-start(), calls=%async_computation.4 | async-start | bytes 11280384 | tf_op jit(solution)/shard_map/all_gather | solution.py:871
  11.3 203.1 %all-gather.6.cloned.1.call-start = ((), (), s32[]{:S(2)}) async-start(), calls=%async_computation.5 | async-start | bytes 5013504 | tf_op jit(solution)/shard_map/all_gather | solution.py:871
  80.1 5.1 %copy-start.10 = (s32[512]{0:T(512)S(1)}, s32[512]{0:T(512)}, u32[]{:S(2)}) copy-start(s32[512]{0:T(512)} %param.25) | copy-start | bytes 6148
  80.1 6.0 %copy-start.14 = (f32[1536]{0:T(1024)S(1)}, f32[1536]{0:T(1024)}, u32[]{:S(2)}) copy-start(f32[1536]{0:T(1024)} %param.27) | copy-start | bytes 18436
  80.1 61.5 %all-to-all-start.1 = ((bf16[16,32,1536]{2,1,0:T(8,128)(2,1)}), bf16[16,32,1536]{2,1,0:T(8,128)(2,1)S(1)}, u32[]{:S(2)}, u32[]{:S(2)}) async-start(bf16[16,32,1536]{2,1,0:T(8,128)(2,1)} %bitcast.17), calls=%async_computation.1 | async-start | bytes 3145728 | tf_op jit(solution)/shard_map/all_to_all | solution.py:792
  85.2 7.8 %copy-start.5 = (bf16[128,304]{0,1:T(8,128)(2,1)S(1)}, bf16[128,304]{0,1:T(8,128)(2,1)}, u32[]{:S(2)}) copy-start(bf16[128,304]{0,1:T(8,128)(2,1)} %param.39) | copy-start | bytes 233476
  86.7 6.2 %copy-start.20 = (s32[64]{0:T(128)S(1)}, s32[64]{0:T(128)}, u32[]{:S(2)}) copy-start(s32[64]{0:T(128)} %param.24) | copy-start | bytes 772
  86.7 6.4 %slice-start = ((bf16[128,304]{0,1:T(8,128)(2,1)}), bf16[128,256]{0,1:T(8,128)(2,1)S(1)}, s32[]{:S(2)}) async-start(bf16[128,304]{0,1:T(8,128)(2,1)} %param.39), calls=%async_computation.7 | async-start | bytes 131072 | tf_op jit(solution)/shard_map/slice | solution.py:867
  86.7 6.5 %copy-start.17 = (f32[24]{0:T(128)S(1)}, f32[24]{0:T(128)}, u32[]{:S(2)}) copy-start(f32[24]{0:T(128)} %param.34) | copy-start | bytes 292
  86.7 7.3 %copy-start.7 = (f32[5,1536]{1,0:T(8,128)S(1)}, f32[5,1536]{1,0:T(8,128)}, u32[]{:S(2)}) copy-start(f32[5,1536]{1,0:T(8,128)} %param.30) | copy-start | bytes 92164
  86.7 7.9 %copy-start.16 = (f32[5,256]{1,0:T(8,128)S(1)}, f32[5,256]{1,0:T(8,128)}, u32[]{:S(2)}) copy-start(f32[5,256]{1,0:T(8,128)} %param.31) | copy-start | bytes 15364
  86.8 8.5 %copy-start.15 = (f32[1536]{0:T(1024)S(1)}, f32[1536]{0:T(1024)}, u32[]{:S(2)}) copy-start(f32[1536]{0:T(1024)} %param.35) | copy-start | bytes 18436
  86.8 10.6 %copy-start.21 = (f32[24]{0:T(128)S(1)}, f32[24]{0:T(128)}, u32[]{:S(2)}) copy-start(f32[24]{0:T(128)} %param.33) | copy-start | bytes 292
  86.8 11.1 %copy-start.22 = (f32[24]{0:T(128)S(1)}, f32[24]{0:T(128)}, u32[]{:S(2)}) copy-start(f32[24]{0:T(128)} %param.32) | copy-start | bytes 292
  86.8 12.4 %copy-start.1 = (bf16[128,2,1536]{2,1,0:T(2,128)(2,1)S(1)}, bf16[128,2,1536]{2,1,0:T(2,128)(2,1)}, u32[]{:S(2)}) copy-start(bf16[128,2,1536]{2,1,0:T(2,128)(2,1)} %param.38) | copy-start | bytes 2359300
  91.5 57.8 %collective-permute-start = (bf16[512,1536]{1,0:T(8,128)(2,1)}, bf16[512,1536]{1,0:T(8,128)(2,1)}, u32[]{:S(2)}, u32[]{:S(2)}) collective-permute-start(bf16[512,1536]{1,0:T(8,128)(2,1)} %get-tuple-element.55.mine.normed_mine), channel_id=1, source_target_pairs={{0,1},{1,0},{2,3},{3,2},{4,5},{5,4},{6,7},{7,6},{8,9},{9,8},{10,11... | collective-permute-start | bytes 4718600 | tf_op jit(solution)/shard_map/ppermute | solution.py:801
  142.7 5.6 %copy-start.2 = (bf16[128,1,1536]{2,1,0:T(2,128)(2,1)S(1)}, bf16[128,1,1536]{2,1,0:T(2,128)(2,1)}, u32[]{:S(2)}) copy-start(bf16[128,1,1536]{2,1,0:T(2,128)(2,1)} %get-tuple-element.123) | copy-start | bytes 1179652
  146.8 54.4 %collective-permute-start.1 = (bf16[512,1536]{1,0:T(8,128)(2,1)}, bf16[512,1536]{1,0:T(8,128)(2,1)S(1)}, u32[]{:S(2)}, u32[]{:S(2)}) collective-permute-start(bf16[512,1536]{1,0:T(8,128)(2,1)} %shard_map.255.gd_mine.cotangent), channel_id=1, source_target_pairs={{0,1},{1,0},{2,3},{3,2},{4,5},{5,4},{6,7},{7,6},{8,9},{9,8},{10,11... | collective-permute-start | bytes 4718600 | tf_op jit(solution)/shard_map/ppermute | solution.py:801
  201.2 13.2 %copy-start.19 = (bf16[512,1536]{1,0:T(8,128)(2,1)}, bf16[512,1536]{1,0:T(8,128)(2,1)S(1)}, u32[]{:S(2)}) copy-start(bf16[512,1536]{1,0:T(8,128)(2,1)S(1)} %collective-permute-done.1.gd_other) | copy-start | bytes 4718596
  227.8 12.8 %copy-start.9 = (f32[8,1024]{1,0:T(8,128)S(1)}, f32[8,1024]{1,0:T(8,128)}, u32[]{:S(2)}) copy-start(f32[8,1024]{1,0:T(8,128)} %get-tuple-element.69) | copy-start | bytes 98308
  227.8 12.8 %collective-permute-start.2 = (f32[8,1024]{1,0:T(8,128)}, f32[8,1024]{1,0:T(8,128)S(1)}, u32[]{:S(2)}, u32[]{:S(2)}) collective-permute-start(f32[8,1024]{1,0:T(8,128)} %get-tuple-element.69), channel_id=1, source_target_pairs={{0,1},{1,0},{2,3},{3,2},{4,5},{5,4},{6,7},{7,6},{8,9},{9,8},{10,11... | collective-permute-start | bytes 98312 | tf_op jit(solution)/shard_map/ppermute | solution.py:810
  240.7 38.5 %collective-permute-start.3 = (bf16[512,1664]{1,0:T(8,128)(2,1)}, bf16[512,1664]{1,0:T(8,128)(2,1)S(1)}, u32[]{:S(2)}, u32[]{:S(2)}) collective-permute-start(bf16[512,1664]{1,0:T(8,128)(2,1)} %get-tuple-element.79), channel_id=1, source_target_pairs={{0,1},{1,0},{2,3},{3,2},{4,5},{5,4},{6,7},{7,6},{8,9},{9,8},{10,11... | collective-permute-start | bytes 5111816 | tf_op jit(solution)/shard_map/ppermute | solution.py:916
  303.0 17.7 %collective-permute-start.5 = (bf16[64,8064]{1,0:T(8,128)(2,1)S(1)}, bf16[64,8064]{1,0:T(8,128)(2,1)S(1)}, u32[]{:S(2)}, u32[]{:S(2)}) collective-permute-start(bf16[64,8064]{1,0:T(8,128)(2,1)S(1)} %fusion.1), channel_id=1, source_target_pairs={{0,2},{2,0},{4,6},{6,4},{8,10},{10,8},{12,14},{14,12},{16,18},{18,... | collective-permute-start | bytes 3096584 | tf_op jit(solution)/shard_map/ppermute | solution.py:821
  304.4 38.6 %all-to-all-start.2 = ((bf16[16,32,1536]{2,1,0:T(8,128)(2,1)}), bf16[16,32,1536]{2,1,0:T(8,128)(2,1)}, u32[]{:S(2)}, u32[]{:S(2)}) async-start(bf16[16,32,1536]{2,1,0:T(8,128)(2,1)} %bitcast.24), calls=%async_computation.2 | async-start | bytes 3145728 | tf_op jit(solution)/shard_map/all_to_all | solution.py:792
  308.8 127.1 %all-gather.8.cloned.1.call-start = ((), (), s32[]{:S(2)}) async-start(), calls=%async_computation.6 | async-start | bytes 2193408 | tf_op jit(solution)/shard_map/all_gather | solution.py:837
  308.8 11.9 %copy-start.3 = (f32[128,8064]{1,0:T(8,128)S(1)}, f32[128,8064]{1,0:T(8,128)}, u32[]{:S(2)}) copy-start(f32[128,8064]{1,0:T(8,128)} %get-tuple-element.82) | copy-start | bytes 12386308
  321.0 20.9 %collective-permute-start.6 = (bf16[32,8064]{1,0:T(8,128)(2,1)S(1)}, bf16[32,8064]{1,0:T(8,128)(2,1)}, u32[]{:S(2)}, u32[]{:S(2)}) collective-permute-start(bf16[32,8064]{1,0:T(8,128)(2,1)S(1)} %fusion.4), channel_id=1, source_target_pairs={{0,4},{2,6},{4,0},{6,2},{8,12},{10,14},{12,8},{14,10},{16,20},{18,... | collective-permute-start | bytes 1548296 | tf_op jit(solution)/shard_map/ppermute | solution.py:821
  322.4 39.8 %collective-permute-start.4 = (bf16[512,1536]{1,0:T(8,128)(2,1)}, bf16[512,1536]{1,0:T(8,128)(2,1)}, u32[]{:S(2)}, u32[]{:S(2)}) collective-permute-start(bf16[512,1536]{1,0:T(8,128)(2,1)} %shard_map.261), channel_id=1, source_target_pairs={{0,1},{1,0},{2,3},{3,2},{4,5},{5,4},{6,7},{7,6},{8,9},{9,8},{10,11... | collective-permute-start | bytes 4718600 | tf_op jit(solution)/shard_map/ppermute | solution.py:940
  343.1 14.2 %copy-start.13 = (s32[512]{0:T(512)S(1)}, s32[512]{0:T(512)}, u32[]{:S(2)}) copy-start(s32[512]{0:T(512)} %param.26) | copy-start | bytes 6148
  354.6 9.4 %collective-permute-start.7 = (bf16[16,8064]{1,0:T(8,128)(2,1)S(1)}, bf16[16,8064]{1,0:T(8,128)(2,1)S(1)}, u32[]{:S(2)}, u32[]{:S(2)}) collective-permute-start(bf16[16,8064]{1,0:T(8,128)(2,1)S(1)} %fusion.5), channel_id=1, source_target_pairs={{0,8},{2,10},{4,12},{6,14},{8,0},{10,2},{12,4},{14,6},{16,24},{18,... | collective-permute-start | bytes 774152 | tf_op jit(solution)/shard_map/ppermute | solution.py:821
  364.1 8.2 %collective-permute-start.8 = (bf16[8,8064]{1,0:T(8,128)(2,1)S(1)}, bf16[8,8064]{1,0:T(8,128)(2,1)S(1)}, u32[]{:S(2)}, u32[]{:S(2)}) collective-permute-start(bf16[8,8064]{1,0:T(8,128)(2,1)S(1)} %fusion.7), channel_id=1, source_target_pairs={{0,16},{2,18},{4,20},{6,22},{8,24},{10,26},{12,28},{14,30},{16,0},... | collective-permute-start | bytes 387080 | tf_op jit(solution)/shard_map/ppermute | solution.py:821
  372.6 7.0 %collective-permute-start.9 = (f32[8,3456]{1,0:T(8,128)S(1)}, f32[8,3456]{1,0:T(8,128)S(1)}, u32[]{:S(2)}, u32[]{:S(2)}) collective-permute-start(f32[8,3456]{1,0:T(8,128)S(1)} %pad_maximum_fusion.1), channel_id=1, source_target_pairs={{0,1},{1,0},{2,3},{3,2},{4,5},{5,4},{6,7},{7,6},{8,9},{9,8},{10,11... | collective-permute-start | bytes 331784 | tf_op jit(solution)/shard_map/ppermute | solution.py:810
  (8 other events, 15.6 us)
Sparse Core Ops, SparseCore 0:
  11.5 148.3 all-gather.3
  162.1 52.2 all-gather.5
  380.5 52.1 all-gather.7

commit v3 on v2

--- a/solution.py
+++ b/solution.py
@@ -2,6 +2,7 @@
 
 import jax
 import jax.numpy as jnp
+import numpy as np
 from jax import lax
 from jax.experimental import pallas as pl
 from jax.experimental.pallas import tpu as pltpu
@@ -102,10 +103,10 @@
     return begin
 
 
-def row_specs(block, width, place):
+def row_specs(block, width, place, scale=1):
     def spec(side):
         def index(i, meta):
-            half = meta[META_HALF]
+            half = meta[META_HALF] * scale
             return (jnp.clip(place(i, meta) - meta[side] * half, 0, half - 1), 0)
 
         return pl.BlockSpec((block, width), index)
@@ -113,8 +114,8 @@
     return [spec(META_RANK), spec(META_THEIRS)]
 
 
-def pick_rows(meta, place, mine, other):
-    own = place // meta[META_HALF] == meta[META_RANK]
+def pick_rows(meta, place, mine, other, scale=1):
+    own = place // (meta[META_HALF] * scale) == meta[META_RANK]
     return jnp.where(own, mine[...], other[...])
 
 
@@ -435,17 +436,29 @@
     return mm(high, indicator) + mm(low, indicator)
 
 
+def turn_tiles(out, first, values):
+    for tile in range(values.shape[1] // LANES):
+        out[:, first + tile * LANES : first + (tile + 1) * LANES] = values[
+            :, tile * LANES : (tile + 1) * LANES
+        ].T
+
+
 def backward_kernel(
     meta,
     scan_out, gate_pre, weighted, x_in, slope_in, bc_in, dbc_in, dt_in, sig_in, state_in, stats,
-    taps, taps_bc, decay_rate, skip, indicator,
-    gz_out, grest_out,
-    dstate, g_next, gbc_next, from_dstate, scaled, reached, product, source_product,
-    *, heads, inner_all,
+    normed_mine, normed_other, mid_rows, gained, gmid_rows,
+    taps, taps_bc, decay_rate, skip, indicator, up_gate, up_x, up_rest,
+    gz_out, grest_out, gmid_out, grads,
+    down_in, down_out, dstate, g_next, gbc_next, from_dstate, scaled, reached, product, source_product,
+    *, heads, inner_all, scale,
 ):
     i = pl.program_id(0)
     inner = heads * HEADDIM
-    first = (pl.num_programs(0) - 1 - i) * CHUNK
+    place = pl.num_programs(0) - 1 - i
+    first = place * CHUNK
+    rest_at = 2 * MODEL_WIDTH
+    zx_at = rest_at + REST_LOCAL
+    out_at = zx_at + 2 * inner
 
     @pl.when(i == 0)
     def _():
@@ -453,6 +466,9 @@
         g_next[...] = jnp.zeros_like(g_next)
         gbc_next[...] = jnp.zeros_like(gbc_next)
         product[CHUNK:, :] = jnp.zeros((8, inner), f32)
+        grads[...] = jnp.zeros_like(grads)
+        down_in[...] = jnp.zeros_like(down_in)
+        down_out[...] = jnp.zeros_like(down_out)
 
     s_pos = first + iota((CHUNK, LANES), 0)
     begin = segment_start(meta, s_pos)
@@ -472,6 +488,9 @@
     row_id = iota((LANES, CHUNK), 0)
     both = jnp.where(row_id == 0, factor, jnp.where(row_id == 1, pull, 0.0)).T
     factor_col, pull_col = column(both, 0), column(both, 1)
+    gmid_scaled = (gmid_rows[...].astype(f32) * factor_col).astype(bf16)
+    down_out[...] += mm(gmid_scaled, gained[...], TN)
+    mid_turned = mid_rows[...].astype(f32).T.astype(bf16)
 
     dt = dt_in[...]
     sig = sig_in[...]
@@ -503,7 +522,8 @@
         silu = gate * gate_sig
         ggated = weighted[:, cols] * factor_col - y * silu * pull_col
         gy_low = (ggated * silu).astype(bf16)
-        gz_out[:, cols] = (ggated * y * (gate_sig + silu * (1.0 - gate_sig))).astype(bf16)
+        ggate = (ggated * y * (gate_sig + silu * (1.0 - gate_sig))).astype(bf16)
+        gz_out[:, cols] = ggate
         gy = gy_low.astype(f32)
         gy_split = jnp.concatenate(
             [jnp.where(left, gy, 0.0).astype(bf16), jnp.where(left, 0.0, gy).astype(bf16)], axis=0
@@ -536,9 +556,9 @@
         )
         dstate[:, cols] = dstate_cols * keep_row
         gconv = gx * slope_in[:, cols].astype(f32)
-        gz_out[:, inner + pair * LANES : inner + (pair + 1) * LANES] = conv_back(
-            gconv, g_next[:, cols], taps[:, cols]
-        ).astype(bf16)
+        later = slice(inner + pair * LANES, inner + (pair + 1) * LANES)
+        gconv_in = conv_back(gconv, g_next[:, cols], taps[:, cols]).astype(bf16)
+        gz_out[:, later] = gconv_in
         g_next[:, cols] = gconv[0:8]
 
     gscores_low = gscores.astype(bf16)
@@ -559,25 +579,49 @@
     used = iota((CHUNK, LANES), 1) < heads
     grest_out[:, 2 * STATE : REST_LOCAL] = jnp.where(used, grad_pre, 0.0).astype(bf16)
 
-
-def backward_scan(meta, scan_out, gate_pre, weighted, x_act, slope, bc, dbc, dt, sig, states, stats, taps, taps_bc, decay, skip, indicator, heads, inner_all):
+    grest = grest_out[...]
+    gmid = mm(gz_out[:, 0:inner], up_gate[...], NT) + mm(gz_out[:, inner:], up_x[...], NT)
+    gmid = gmid + mm(grest, up_rest[...], NT)
+    grads[:, zx_at:out_at] += mm(mid_turned, gz_out[...])
+    gmid = (gmid * adapter_mask(meta, first, CHUNK)).astype(bf16)
+    gmid_out[...] = gmid
+    grads[:, rest_at:zx_at] += mm(mid_turned, grest)
+    down_in[...] += mm(gmid, pick_rows(meta, place, normed_mine, normed_other, scale), TN)
+
+    @pl.when(place == 0)
+    def _():
+        turn_tiles(grads, 0, down_in[...])
+        turn_tiles(grads, out_at, down_out[...])
+
+
+def backward_scan(meta, scan_out, gate_pre, weighted, x_act, slope, bc, dbc, dt, sig, states, stats, normed, mid, gained, gmid, taps, taps_bc, decay, skip, indicator, up_gate, up_x, up_rest, heads, inner_all, block):
     rows, inner = scan_out.shape
     count = rows // CHUNK
     chunk_rows = lambda width: pl.BlockSpec((CHUNK, width), lambda i, *_: (count - 1 - i, 0))
-    operands = (taps, taps_bc, decay, skip, indicator)
+    scale = block // CHUNK
+    columns = 2 * MODEL_WIDTH + REST_LOCAL + 3 * inner
+    operands = (taps, taps_bc, decay, skip, indicator, up_gate, up_x, up_rest)
     streams = (scan_out, gate_pre, weighted, x_act, slope, bc, dbc, dt, sig, states)
     outs = (
         jax.ShapeDtypeStruct((rows, 2 * inner), bf16),
         jax.ShapeDtypeStruct((rows, REST_LOCAL), bf16),
+        jax.ShapeDtypeStruct((rows, LANES), bf16),
+        jax.ShapeDtypeStruct((LANES, columns), f32),
     )
     grid = pltpu.PrefetchScalarGridSpec(
         num_scalar_prefetch=1,
         grid=(count,),
         in_specs=[chunk_rows(a.shape[1]) for a in streams]
         + [pl.BlockSpec((8, CHUNK), lambda i, *_: (0, count - 1 - i))]
+        + row_specs(CHUNK, MODEL_WIDTH, lambda i, meta: count - 1 - i, scale)
+        + [chunk_rows(LANES), chunk_rows(inner), chunk_rows(LANES)]
         + [whole(a.shape) for a in operands],
-        out_specs=[chunk_rows(2 * inner), chunk_rows(REST_LOCAL)],
+        out_specs=[
+            chunk_rows(2 * inner), chunk_rows(REST_LOCAL), chunk_rows(LANES), whole((LANES, columns))
+        ],
         scratch_shapes=[
+            pltpu.VMEM((LANES, MODEL_WIDTH), f32),
+            pltpu.VMEM((LANES, inner), f32),
             pltpu.VMEM((STATE, inner), f32),
             pltpu.VMEM((8, inner), f32),
             pltpu.VMEM((8, 2 * STATE), f32),
@@ -589,91 +633,14 @@
         ],
     )
     return pl.pallas_call(
-        partial(backward_kernel, heads=heads, inner_all=inner_all),
+        partial(backward_kernel, heads=heads, inner_all=inner_all, scale=scale),
         out_shape=outs,
         grid_spec=grid,
         compiler_params=params(),
         cost_estimate=pl.CostEstimate(
             flops=6 * rows * MODEL_WIDTH * inner, bytes_accessed=50_000_000, transcendentals=0
         ),
-    )(meta, *streams, stats, *operands)
-
-
-def turn_tiles(out, first, values):
-    for tile in range(values.shape[1] // LANES):
-        out[:, first + tile * LANES : first + (tile + 1) * LANES] = values[
-            :, tile * LANES : (tile + 1) * LANES
-        ].T
-
-
-def adapter_back_kernel(
-    meta,
-    gz, grest, normed_mine, normed_other, mid, gained, gmid_out_rows, stats, gup_out, up_gate, up_x, up_rest,
-    gmid_out, grads, down_in, down_out,
-    *, inner, inner_all,
-):
-    block = gz.shape[0]
-    place = pl.program_id(0)
-    rest_at = 2 * MODEL_WIDTH
-    zx_at = rest_at + REST_LOCAL
-    out_at = zx_at + 2 * inner
-
-    @pl.when(place == 0)
-    def _():
-        grads[...] = jnp.zeros_like(grads)
-        grads[:, MODEL_WIDTH:rest_at] = gup_out[...]
-        down_in[...] = jnp.zeros_like(down_in)
-        down_out[...] = jnp.zeros_like(down_out)
-
-    grest_rows = grest[...]
-    gmid = mm(gz[:, 0:inner], up_gate[...], NT) + mm(gz[:, inner : 2 * inner], up_x[...], NT)
-    gmid = gmid + mm(grest_rows, up_rest[...], NT)
-    gmid = (gmid * adapter_mask(meta, place * block, block)).astype(bf16)
-    gmid_out[...] = gmid
-    mid_rows = mid[...]
-    down_in[...] += mm(gmid, pick_rows(meta, place, normed_mine, normed_other), TN)
-    grads[:, zx_at:out_at] += mm(mid_rows, gz[...], TN)
-    grads[:, rest_at:zx_at] += mm(mid_rows, grest_rows, TN)
-    factor = lax.rsqrt(stats[0:1, :] * (1.0 / inner_all) + epsilon)
-    factor_col = jnp.broadcast_to(factor, (LANES, block)).T
-    scaled = (gmid_out_rows[...].astype(f32) * factor_col).astype(bf16)
-    down_out[...] += mm(scaled, gained[...], TN)
-
-    @pl.when(place == pl.num_programs(0) - 1)
-    def _():
-        turn_tiles(grads, 0, down_in[...])
-        turn_tiles(grads, out_at, down_out[...])
-
-
-def adapter_back(meta, gz, grest, normed, mid, gained, gmid, stats, gup_out, up_gate, up_x, up_rest, block, inner_all):
-    rows = gz.shape[0]
-    inner = gz.shape[1] // 2
-    block_rows = lambda width: pl.BlockSpec((block, width), lambda i, *_: (i, 0))
-    operands = (gup_out, up_gate, up_x, up_rest)
-    columns = 2 * MODEL_WIDTH + REST_LOCAL + 3 * inner
-    grid = pltpu.PrefetchScalarGridSpec(
-        num_scalar_prefetch=1,
-        grid=(rows // block,),
-        in_specs=[block_rows(2 * inner), block_rows(REST_LOCAL)]
-        + row_specs(block, MODEL_WIDTH, lambda i, meta: i)
-        + [block_rows(LANES), block_rows(inner), block_rows(LANES)]
-        + [pl.BlockSpec((8, block), lambda i, *_: (0, i))]
-        + [whole(a.shape) for a in operands],
-        out_specs=[block_rows(LANES), whole((LANES, columns))],
-        scratch_shapes=[pltpu.VMEM((LANES, MODEL_WIDTH), f32), pltpu.VMEM((LANES, inner), f32)],
-    )
-    return pl.pallas_call(
-        partial(adapter_back_kernel, inner=inner, inner_all=inner_all),
-        out_shape=(
-            jax.ShapeDtypeStruct((rows, LANES), bf16),
-            jax.ShapeDtypeStruct((LANES, columns), f32),
-        ),
-        grid_spec=grid,
-        compiler_params=params(),
-        cost_estimate=pl.CostEstimate(
-            flops=2 * rows * LANES * (5 * inner + MODEL_WIDTH), bytes_accessed=20_000_000, transcendentals=0
-        ),
-    )(meta, gz, grest, *normed, mid, gained, gmid, stats, *operands)
+    )(meta, *streams, stats, *normed, mid, gained, gmid, *operands)
 
 
 def project_back_kernel(meta, gz, grest, gmid, w_in, down_in, grad_out, *, inner):
@@ -749,7 +716,11 @@
             span = slice(tile * LANES, (tile + 1) * LANES)
             out[span, :] = total[:, first + tile * LANES : first + (tile + 1) * LANES].astype(f32)
     gup_out[...] = total[:, MODEL_WIDTH:rest_at].astype(f32)
-    gup_rest[...] = total[:, rest_at:zx_at].astype(f32)[:, 0 : gup_rest.shape[1]]
+    columns = gup_rest.shape[0]
+    for first in range(0, columns, LANES):
+        turned = total[:, rest_at + first : rest_at + first + LANES].astype(f32).T
+        count = min(LANES, columns - first)
+        gup_rest[first : first + count, :] = turned[0:count, :]
     gup[:, 0, :] = total[:, zx_at : zx_at + inner].astype(f32)
     gup[:, 1, :] = total[:, zx_at + inner : out_at].astype(f32)
 
@@ -882,9 +853,7 @@
     head_row = lambda values: jnp.pad(values, (0, LANES - heads))[None, :]
     bias_row, decay_row = head_row(step_bias), head_row(head_decay_rate)
     skip_row = jnp.repeat(skip_weight, HEADDIM)[None, :]
-    indicator = (
-        jnp.arange(inner)[:, None] // HEADDIM == jnp.arange(LANES)[None, :]
-    ).astype(bf16)
+    indicator = jnp.asarray(np.arange(inner)[:, None] // HEADDIM == np.arange(LANES)[None, :], bf16)
 
     sent_tokens, sent_cotangent = simple_call(
         pack_kernel, (token_rows, token_rows), 2 * move_flops, *keys(dealt_position), tokens, cotangent
@@ -917,9 +886,10 @@
     else:
         part_own, part_other = scatter_rows(part_sent)
 
-    gz, grest = backward_scan(
+    gz, grest, gmid_in, gradients = backward_scan(
         meta, scan_out, gate_pre, weighted, x_act, slope, bc, dbc, dt, sig, states, stats,
-        taps, taps_bc, decay_row, skip_row, indicator, heads, inner_all,
+        normed, mid_in, gained, gmid, taps, taps_bc, decay_row, skip_row, indicator,
+        up_gate, up_x, up_rest, heads, inner_all, block,
     )
     part_other, _ = lax.optimization_barrier((part_other, gz))
     sent_output, gup_out = simple_call(
@@ -929,10 +899,7 @@
         own_rows(stats, 1), grad_mine, adapter_up_out, scalars=1,
     )
     dealt_output = deal(sent_output)
-    gmid_in, gradients = adapter_back(
-        meta, gz, grest, normed, mid_in, gained, gmid, stats, gup_out, up_gate, up_x, up_rest,
-        block, inner_all,
-    )
+    gradients = lax.dynamic_update_slice(gradients, gup_out, (0, MODEL_WIDTH))
     gz, _ = lax.optimization_barrier((gz, gradients))
     back = partial(project_back, meta, gz, grest, gmid_in, w_in, adapter_down_in, half_rows)
     if pairwise:
@@ -967,13 +934,13 @@
             token_rows,
             jax.ShapeDtypeStruct((MODEL_WIDTH, LANES), f32),
             jax.ShapeDtypeStruct((LANES, 2, inner), f32),
-            jax.ShapeDtypeStruct((LANES, adapter_up_rest.shape[1]), f32),
+            jax.ShapeDtypeStruct((adapter_up_rest.shape[1], LANES), f32),
             jax.ShapeDtypeStruct((inner, LANES), f32),
             jax.ShapeDtypeStruct((LANES, MODEL_WIDTH), f32),
         ),
         move_flops, *keys(dealt_key), dealt_grad, total,
     )
-    return output, input_grad, gdown_in, gup_zx, gup_rest, gdown_out, gup_out
+    return output, input_grad, gdown_in, gup_zx, gup_rest.T, gdown_out, gup_out
 
 
 def solution(mesh):

time: 451 us -> 441 us (0.978)
  Pallas kernels: 172 us -> 167 us
  waiting for transfers between devices: 97.8 us -> 92.9 us
    ppermute x1, waiting for transfers between devices: 5.17 us -> 0.01 us  [body(): part_other = lax.ppermute(part_sent, 'tensor', swap)]
    pallas_call x2 -> x1, Pallas kernels: 45.9 us -> 40.9 us  [backward_scan(): pl.pallas_call(partial(backward_kernel, heads=heads, inner_all=inner_all,...]
  transfers between devices with their start and end apart: 15 -> 15, of which waited for: 7 -> 6; matrix products, arithmetic and copies ran while one was open for 3% -> 3% of each run, Pallas kernels for 29% -> 32%
where the time goes in v3:
time: 441 us; the launch traced here: 440 us
  Pallas kernels  167 us (38%)
  blocking collectives  117 us (27%)
  waiting for transfers between devices  92.9 us (21%)
  starting transfers between devices  22.6 us (5%)
  local copies, waits for them, and re-layouts  22.1 us (5%)
  between operations  14.1 us (3%)
    all_to_all x2, blocking collectives, deal(): return lax.all_to_all(rows, 'dp', split_axis=0, concat_axis=0, tiled=True)  117 us
    all_to_all x2, waiting for transfers between devices, deal(): return lax.all_to_all(rows, 'dp', split_axis=0, concat_axis=0, tiled=True)  41.5 us
    pallas_call x1, Pallas kernels, forward_scan(): pl.pallas_call(partial(forward_kernel, heads=heads, block=block), out_sha...  41.5 us
    pallas_call x1, Pallas kernels, backward_scan(): pl.pallas_call(partial(backward_kernel, heads=heads, inner_all=inner_all,...  40.9 us
    pallas_call x7, Pallas kernels, simple_call(): pl.pallas_call(kernel, out_shape=outs, in_specs=[scalar] * scalars + [vec...  36.6 us
    ppermute x4, waiting for transfers between devices, exchange(): return lax.ppermute(values.astype(bf16), 'dp', pairs)  26.9 us
    all_gather x2, waiting for transfers between devices, gather_weight(): lax.all_gather(jnp.concatenate(shards, axis=1), 'dp', axis=0, tiled=True)  23.7 us
    pallas_call x2, Pallas kernels, project_back(): pl.pallas_call(partial(project_back_kernel, inner=inner), out_shape=jax.S...  23.4 us
  transfers between devices with their start and end apart: 15, of which 6 were waited for; matrix products, arithmetic and copies ran while one was open for 3% of the time, Pallas kernels for 32%

profile of v3, /device:TPU:1, one launch (start us, length us, event | category | flops | bytes accessed | tf_op | source)
XLA Modules:
  0.0 440.2 jit_solution(15034818551790942025)
XLA Ops:
  8.0 2.3 fusion.18
  13.0 5.2 %shard_map.261 = (bf16[512,1536]{1,0:T(8,128)(2,1)}, bf16[512,1536]{1,0:T(8,128)(2,1)}) custom-call(s32[512,1]{1,0:T(8,128)} %copy.48.key_col, s32[1,512]{1,0:T(1,128)} %bitcast.80, bf16[512,1536]{1,0:T(8,128)(2,1)} %first.1, bf16[512,1536]{1,0:T(8,128)(2,1)} %second.1), custom_call_target="tpu_custom_call" | custom-call | flops 1610612736 | bytes 1000000 | tf_op jit(solution)/shard_map/pallas_call | solution.py:89
  18.2 61.9 %all_to_all.45 = bf16[16,32,1536]{2,1,0:T(8,128)(2,1)} all-to-all(bf16[16,32,1536]{2,1,0:T(8,128)(2,1)} %bitcast.69), channel_id=1, replica_groups=mesh['dp'=16,'tensor'=2] {'dp'}, dimensions={0} | all-to-all | bytes 3145728 | tf_op jit(solution)/shard_map/all_to_all | solution.py:763
  80.2 4.8 %all-to-all-start.1 = ((bf16[16,32,1536]{2,1,0:T(8,128)(2,1)}), bf16[16,32,1536]{2,1,0:T(8,128)(2,1)S(1)}, u32[]{:S(2)}, u32[]{:S(2)}) async-start(bf16[16,32,1536]{2,1,0:T(8,128)(2,1)} %bitcast.17), calls=%async_computation.1 | async-start | bytes 3145728 | tf_op jit(solution)/shard_map/all_to_all | solution.py:763
  89.7 4.7 %shard_map.262 = (bf16[512,1536]{1,0:T(8,128)(2,1)}, bf16[512,1536]{1,0:T(8,128)(2,1)}) custom-call(s32[512,1]{1,0:T(8,128)} %copy.49.key_col, s32[1,512]{1,0:T(1,128)} %bitcast.78, bf16[512,1536]{1,0:T(8,128)(2,1)} %bitcast.68, f32[1,1536]{1,0:T(1,128)} %broadcast_in_dim.52.gain), custom_call_target="tpu_custom_call" | custom-call | flops 805306368 | bytes 1000000 | tf_op jit(solution)/shard_map/pallas_call | solution.py:89
  94.3 1.4 collective-permute-start
  98.2 2.0 fusion.17
  100.2 41.5 %all-to-all-done.1 = bf16[16,32,1536]{2,1,0:T(8,128)(2,1)S(1)} async-done(((bf16[16,32,1536]{2,1,0:T(8,128)(2,1)}), bf16[16,32,1536]{2,1,0:T(8,128)(2,1)S(1)}, u32[]{:S(2)}, u32[]{:S(2)}) %all-to-all-start.1) | async-done | bytes 1572896 | tf_op jit(solution)/shard_map/all_to_all | solution.py:763
  142.8 4.0 shard_map.264.gd_mine.cotangent
  146.8 1.5 collective-permute-start.1
  149.3 10.6 %all-gather.4.cloned.1.call-done.w_in = bf16[1536,3456]{1,0:T(8,128)(2,1)} async-done(((bf16[96,3456]{1,0:T(8,128)(2,1)}), bf16[1536,3456]{1,0:T(8,128)(2,1)}) %all-gather.4.cloned.1.call-update) | async-done | bytes 10616848 | tf_op jit(solution)/shard_map/all_gather | solution.py:842
  159.9 41.5 %shard_map.263 = (bf16[1024,1536]{1,0:T(8,128)(2,1)}, bf16[1024,1536]{1,0:T(8,128)(2,1)}, f32[1024,1536]{1,0:T(8,128)}, f32[1024,1536]{1,0:T(8,128)}, bf16[1024,...) custom-call(s32[12]{0:T(128)} %concatenate.15.meta, ...), custom_call_target="tpu_custom_call" | custom-call | flops 12079595520 | bytes 50000000 | tf_op jit(solution)/shard_map/pallas_call | solution.py:312
  201.3 13.1 %all-gather.6.cloned.1.call-done.w_out = bf16[1536,1536]{1,0:T(8,128)(2,1)} async-done(((bf16[96,1536]{1,0:T(8,128)(2,1)}), bf16[1536,1536]{1,0:T(8,128)(2,1)}) %all-gather.6.cloned.1.call-update) | async-done | bytes 4718608 | tf_op jit(solution)/shard_map/all_gather | solution.py:842
  214.4 13.3 %shard_map.265 = (f32[1024,1536]{1,0:T(8,128)}, bf16[1024,128]{1,0:T(8,128)(2,1)}, f32[8,1024]{1,0:T(8,128)}) custom-call(s32[12]{0:T(128)} %concatenate.15.meta, bf16[512,1536]{1,0:T(8,128)(2,1)} %shard_map.264.gd_mine.cotangent, bf16[512,1536]{1,0:T(8,128)(2,1)} %copy-done.19, bf16[1024,1536]{1,0:T(8,128)(2,1)} %get-tuple-element.70.gained.theirs.own, ...), custom_call_target="tpu_custom_call" | custom-call | flops 4831838208 | bytes 20000000 | tf_op jit(solution)/shard_map/pallas_call | solution.py:379
  229.1 11.5 %shard_map.266 = (bf16[512,1664]{1,0:T(8,128)(2,1)}, bf16[512,1664]{1,0:T(8,128)(2,1)}) custom-call(s32[12]{0:T(128)} %concatenate.15.meta, bf16[1024,1536]{1,0:T(8,128)(2,1)} %get-tuple-element.70.gained.theirs.own, bf16[1024,1536]{1,0:T(8,128)(2,1)} %get-tuple-element.70.gained.theirs.own, bf16[1536,1536]{1,0:T(8,128)(2,1)} %all-gather.6.cloned.1.call-done.w_out, ...), custom_call_target="tpu_custom_call" | custom-call | flops 4831838208 | bytes 15000000 | tf_op jit(solution)/shard_map/pallas_call | solution.py:422
  242.4 40.9 %shard_map.267 = (bf16[1024,3072]{1,0:T(8,128)(2,1)}, bf16[1024,384]{1,0:T(8,128)(2,1)}, bf16[1024,128]{1,0:T(8,128)(2,1)}, f32[128,8064]{1,0:T(8,128)}) custom-call(s32[12]{0:T(128)} %concatenate.15.meta, f32[1024,1536]{1,0:T(8,128)} %get-tuple-element.56.scan_out, f32[1024,1536]{1,0:T(8,128)} %get-tuple-element.57.gate_pre, ...), custom_call_target="tpu_custom_call" | custom-call | flops 14495514624 | bytes 50000000 | tf_op jit(solution)/shard_map/pallas_call | solution.py:635
  284.5 6.4 %shard_map.268 = (bf16[512,1536]{1,0:T(8,128)(2,1)}, f32[128,1536]{1,0:T(8,128)}) custom-call(s32[12]{0:T(128)} %concatenate.15.meta, s32[512,1]{1,0:T(8,128)} %copy.57.key_col, s32[1,512]{1,0:T(1,128)} %bitcast.74, bf16[512,1536]{1,0:T(8,128)(2,1)} %get-tuple-element.77.resid, bf16[512,1664]{1,0:T(8,128)(2,1)} %get-tuple-element.78.own, ...), custom_call_target="tpu_custom_call" | custom-call | flops 1610612736 | bytes 1000000 | tf_op jit(solution)/shard_map/pallas_call | solution.py:89
  291.0 2.2 constant_dynamic-update-slice_fusion
  293.1 1.7 fusion.1
  295.7 4.3 all-to-all-start.2
  300.1 11.9 %shard_map.269 = bf16[512,1536]{1,0:T(8,128)(2,1)} custom-call(s32[12]{0:T(128)} %concatenate.15.meta, bf16[1024,3072]{1,0:T(8,128)(2,1)} %get-tuple-element.89.gz, bf16[1024,384]{1,0:T(8,128)(2,1)} %get-tuple-element.83.grest, bf16[1024,128]{1,0:T(8,128)(2,1)} %get-tuple-element.84.gmid, bf16[1536,3456]{1,0:T(8,128)(2,1)} %all-gather.4.cloned.1.call-done.w_in, ...), custom_call_target="tpu_custom_call" | custom-call | flops 4831838208 | bytes 15000000 | tf_op jit(solution)/shard_map/pallas_call | solution.py:666
  312.3 1.3 collective-permute-start.6
  314.8 18.4 %collective-permute-done.6 = bf16[32,8064]{1,0:T(8,128)(2,1)} collective-permute-done((bf16[32,8064]{1,0:T(8,128)(2,1)S(1)}, bf16[32,8064]{1,0:T(8,128)(2,1)}, u32[]{:S(2)}, u32[]{:S(2)}) %collective-permute-start.6) | collective-permute-done | bytes 516128 | tf_op jit(solution)/shard_map/ppermute | solution.py:792
  334.3 11.5 %shard_map.271.own = bf16[512,1536]{1,0:T(8,128)(2,1)} custom-call(s32[12]{0:T(128)} %concatenate.15.meta, bf16[1024,3072]{1,0:T(8,128)(2,1)} %get-tuple-element.89.gz, bf16[1024,384]{1,0:T(8,128)(2,1)} %get-tuple-element.83.grest, bf16[1024,128]{1,0:T(8,128)(2,1)} %get-tuple-element.84.gmid, bf16[1536,3456]{1,0:T(8,128)(2,1)} %all-gather.4.cloned.1.call-done.w_in, ...), custom_call_target="tpu_custom_call" | custom-call | flops 4831838208 | bytes 15000000 | tf_op jit(solution)/shard_map/pallas_call | solution.py:666
  345.9 2.6 collective-permute-start.7
  349.4 4.0 shard_map.270
  353.4 1.9 collective-permute-done.7
  355.3 1.5 collective-permute-start.8
  356.8 6.7 %collective-permute-done.8 = bf16[8,8064]{1,0:T(8,128)(2,1)S(1)} collective-permute-done((bf16[8,8064]{1,0:T(8,128)(2,1)S(1)}, bf16[8,8064]{1,0:T(8,128)(2,1)S(1)}, u32[]{:S(2)}, u32[]{:S(2)}) %collective-permute-start.8) | collective-permute-done | bytes 129056 | tf_op jit(solution)/shard_map/ppermute | solution.py:792
  365.1 6.3 %shard_map.272 = bf16[512,1536]{1,0:T(8,128)(2,1)} custom-call(s32[512,1]{1,0:T(8,128)} %copy.57.key_col, s32[1,512]{1,0:T(1,128)} %bitcast.75, bf16[512,1536]{1,0:T(8,128)(2,1)} %get-tuple-element.77.resid, bf16[512,1536]{1,0:T(8,128)(2,1)} %shard_map.271.own, bf16[512,1536]{1,0:T(8,128)(2,1)} %collective-permute-done.4.other, ...), custom_call_target="tpu_custom_call" | custom-call | flops 805306368 | bytes 1000000 | tf_op jit(solution)/shard_map/pallas_call | solution.py:89
  372.2 55.5 %all_to_all.46 = bf16[16,32,1536]{2,1,0:T(8,128)(2,1)} all-to-all(bf16[16,32,1536]{2,1,0:T(8,128)(2,1)} %bitcast.60), channel_id=1, replica_groups=mesh['dp'=16,'tensor'=2] {'dp'}, dimensions={0} | all-to-all | bytes 3145728 | tf_op jit(solution)/shard_map/all_to_all | solution.py:763
  427.7 6.0 %shard_map.273 = (bf16[512,1536]{1,0:T(8,128)(2,1)}, f32[1536,128]{1,0:T(8,128)}, f32[128,2,1536]{2,1,0:T(2,128)}, f32[304,128]{1,0:T(8,128)}, f32[1536,128]{1,0:T(8,128)}, /*index=5*/f32[128,1536]{1,0:T(8,128)}) custom-call(s32[512,1]{1,0:T(8,128)} %copy.58.key_col, s32[1,512]{1,0:T(1,128)} %bitcast.73, bf16[512,1536]{1,0:T(8,128)(2,1)} %bitcast.61, ...), custom_call_target="tpu_custom_call" | custom-call | flops 805306368 | bytes 1000000 | tf_op jit(solution)/shard_map/pallas_call | solution.py:89
  (114 shorter events, 23.8 us)
Async XLA Ops:
  7.2 152.7 %all-gather.4.cloned.1.call-start = ((), (), s32[]{:S(2)}) async-start(), calls=%async_computation.4 | async-start | bytes 11280384 | tf_op jit(solution)/shard_map/all_gather | solution.py:842
  11.4 203.1 %all-gather.6.cloned.1.call-start = ((), (), s32[]{:S(2)}) async-start(), calls=%async_computation.5 | async-start | bytes 5013504 | tf_op jit(solution)/shard_map/all_gather | solution.py:842
  80.1 5.2 %copy-start.20 = (s32[64]{0:T(128)S(1)}, s32[64]{0:T(128)}, u32[]{:S(2)}) copy-start(s32[64]{0:T(128)} %param.25) | copy-start | bytes 772
  80.1 5.3 %copy-start.5 = (bf16[128,304]{0,1:T(8,128)(2,1)S(1)}, bf16[128,304]{0,1:T(8,128)(2,1)}, u32[]{:S(2)}) copy-start(bf16[128,304]{0,1:T(8,128)(2,1)} %param.40) | copy-start | bytes 233476
  80.1 5.4 %slice-start = ((bf16[128,304]{0,1:T(8,128)(2,1)}), bf16[128,256]{0,1:T(8,128)(2,1)S(1)}, s32[]{:S(2)}) async-start(bf16[128,304]{0,1:T(8,128)(2,1)} %param.40), calls=%async_computation.7 | async-start | bytes 131072 | tf_op jit(solution)/shard_map/slice | solution.py:838
  80.1 5.5 %copy-start.10 = (s32[512]{0:T(512)S(1)}, s32[512]{0:T(512)}, u32[]{:S(2)}) copy-start(s32[512]{0:T(512)} %param.26) | copy-start | bytes 6148
  80.1 6.4 %copy-start.14 = (f32[1536]{0:T(1024)S(1)}, f32[1536]{0:T(1024)}, u32[]{:S(2)}) copy-start(f32[1536]{0:T(1024)} %param.28) | copy-start | bytes 18436
  80.1 7.0 %copy-start.17 = (f32[24]{0:T(128)S(1)}, f32[24]{0:T(128)}, u32[]{:S(2)}) copy-start(f32[24]{0:T(128)} %param.35) | copy-start | bytes 292
  80.1 7.7 %copy-start.7 = (f32[5,1536]{1,0:T(8,128)S(1)}, f32[5,1536]{1,0:T(8,128)}, u32[]{:S(2)}) copy-start(f32[5,1536]{1,0:T(8,128)} %param.31) | copy-start | bytes 92164
  80.1 8.3 %copy-start.16 = (f32[5,256]{1,0:T(8,128)S(1)}, f32[5,256]{1,0:T(8,128)}, u32[]{:S(2)}) copy-start(f32[5,256]{1,0:T(8,128)} %param.32) | copy-start | bytes 15364
  80.2 8.9 %copy-start.15 = (f32[1536]{0:T(1024)S(1)}, f32[1536]{0:T(1024)}, u32[]{:S(2)}) copy-start(f32[1536]{0:T(1024)} %param.36) | copy-start | bytes 18436
  80.2 61.5 %all-to-all-start.1 = ((bf16[16,32,1536]{2,1,0:T(8,128)(2,1)}), bf16[16,32,1536]{2,1,0:T(8,128)(2,1)S(1)}, u32[]{:S(2)}, u32[]{:S(2)}) async-start(bf16[16,32,1536]{2,1,0:T(8,128)(2,1)} %bitcast.17), calls=%async_computation.1 | async-start | bytes 3145728 | tf_op jit(solution)/shard_map/all_to_all | solution.py:763
  87.2 9.3 %copy-start.21 = (f32[24]{0:T(128)S(1)}, f32[24]{0:T(128)}, u32[]{:S(2)}) copy-start(f32[24]{0:T(128)} %param.34) | copy-start | bytes 292
  87.2 9.8 %copy-start.22 = (f32[24]{0:T(128)S(1)}, f32[24]{0:T(128)}, u32[]{:S(2)}) copy-start(f32[24]{0:T(128)} %param.33) | copy-start | bytes 292
  89.7 8.5 %copy-start.1 = (bf16[128,2,1536]{2,1,0:T(2,128)(2,1)S(1)}, bf16[128,2,1536]{2,1,0:T(2,128)(2,1)}, u32[]{:S(2)}) copy-start(bf16[128,2,1536]{2,1,0:T(2,128)(2,1)} %param.39) | copy-start | bytes 2359300
  94.3 54.9 %collective-permute-start = (bf16[512,1536]{1,0:T(8,128)(2,1)}, bf16[512,1536]{1,0:T(8,128)(2,1)}, u32[]{:S(2)}, u32[]{:S(2)}) collective-permute-start(bf16[512,1536]{1,0:T(8,128)(2,1)} %get-tuple-element.55.mine.normed_mine), channel_id=1, source_target_pairs={{0,1},{1,0},{2,3},{3,2},{4,5},{5,4},{6,7},{7,6},{8,9},{9,8},{10,11... | collective-permute-start | bytes 4718600 | tf_op jit(solution)/shard_map/ppermute | solution.py:772
  142.8 5.5 %copy-start.2 = (bf16[128,1,1536]{2,1,0:T(2,128)(2,1)S(1)}, bf16[128,1,1536]{2,1,0:T(2,128)(2,1)}, u32[]{:S(2)}) copy-start(bf16[128,1,1536]{2,1,0:T(2,128)(2,1)} %get-tuple-element.102) | copy-start | bytes 1179652
  146.8 54.5 %collective-permute-start.1 = (bf16[512,1536]{1,0:T(8,128)(2,1)}, bf16[512,1536]{1,0:T(8,128)(2,1)S(1)}, u32[]{:S(2)}, u32[]{:S(2)}) collective-permute-start(bf16[512,1536]{1,0:T(8,128)(2,1)} %shard_map.264.gd_mine.cotangent), channel_id=1, source_target_pairs={{0,1},{1,0},{2,3},{3,2},{4,5},{5,4},{6,7},{7,6},{8,9},{9,8},{10,11... | collective-permute-start | bytes 4718600 | tf_op jit(solution)/shard_map/ppermute | solution.py:772
  201.3 13.1 %copy-start.19 = (bf16[512,1536]{1,0:T(8,128)(2,1)}, bf16[512,1536]{1,0:T(8,128)(2,1)S(1)}, u32[]{:S(2)}) copy-start(bf16[512,1536]{1,0:T(8,128)(2,1)S(1)} %collective-permute-done.1.gd_other) | copy-start | bytes 4718596
  227.8 12.8 %copy-start.9 = (f32[8,1024]{1,0:T(8,128)S(1)}, f32[8,1024]{1,0:T(8,128)}, u32[]{:S(2)}) copy-start(f32[8,1024]{1,0:T(8,128)} %get-tuple-element.69) | copy-start | bytes 98308
  227.8 12.8 %collective-permute-start.2 = (f32[8,1024]{1,0:T(8,128)}, f32[8,1024]{1,0:T(8,128)S(1)}, u32[]{:S(2)}, u32[]{:S(2)}) collective-permute-start(f32[8,1024]{1,0:T(8,128)} %get-tuple-element.69), channel_id=1, source_target_pairs={{0,1},{1,0},{2,3},{3,2},{4,5},{5,4},{6,7},{7,6},{8,9},{9,8},{10,11... | collective-permute-start | bytes 98312 | tf_op jit(solution)/shard_map/ppermute | solution.py:781
  240.6 42.7 %collective-permute-start.3 = (bf16[512,1664]{1,0:T(8,128)(2,1)}, bf16[512,1664]{1,0:T(8,128)(2,1)S(1)}, u32[]{:S(2)}, u32[]{:S(2)}) collective-permute-start(bf16[512,1664]{1,0:T(8,128)(2,1)} %get-tuple-element.79), channel_id=1, source_target_pairs={{0,1},{1,0},{2,3},{3,2},{4,5},{5,4},{6,7},{7,6},{8,9},{9,8},{10,11... | collective-permute-start | bytes 5111816 | tf_op jit(solution)/shard_map/ppermute | solution.py:885
  294.8 17.2 %collective-permute-start.5 = (bf16[64,8064]{1,0:T(8,128)(2,1)S(1)}, bf16[64,8064]{1,0:T(8,128)(2,1)S(1)}, u32[]{:S(2)}, u32[]{:S(2)}) collective-permute-start(bf16[64,8064]{1,0:T(8,128)(2,1)S(1)} %fusion.1), channel_id=1, source_target_pairs={{0,2},{2,0},{4,6},{6,4},{8,10},{10,8},{12,14},{14,12},{16,18},{18,... | collective-permute-start | bytes 3096584 | tf_op jit(solution)/shard_map/ppermute | solution.py:792
  295.7 38.6 %all-to-all-start.2 = ((bf16[16,32,1536]{2,1,0:T(8,128)(2,1)}), bf16[16,32,1536]{2,1,0:T(8,128)(2,1)}, u32[]{:S(2)}, u32[]{:S(2)}) async-start(bf16[16,32,1536]{2,1,0:T(8,128)(2,1)} %bitcast.24), calls=%async_computation.2 | async-start | bytes 3145728 | tf_op jit(solution)/shard_map/all_to_all | solution.py:763
  300.0 127.7 %all-gather.8.cloned.1.call-start = ((), (), s32[]{:S(2)}) async-start(), calls=%async_computation.6 | async-start | bytes 2193408 | tf_op jit(solution)/shard_map/all_gather | solution.py:808
  300.1 11.9 %copy-start.3 = (f32[128,8064]{1,0:T(8,128)S(1)}, f32[128,8064]{1,0:T(8,128)}, u32[]{:S(2)}) copy-start(f32[128,8064]{1,0:T(8,128)} %constant_dynamic-update-slice_fusion) | copy-start | bytes 12386308
  312.3 20.9 %collective-permute-start.6 = (bf16[32,8064]{1,0:T(8,128)(2,1)S(1)}, bf16[32,8064]{1,0:T(8,128)(2,1)}, u32[]{:S(2)}, u32[]{:S(2)}) collective-permute-start(bf16[32,8064]{1,0:T(8,128)(2,1)S(1)} %fusion.3), channel_id=1, source_target_pairs={{0,4},{2,6},{4,0},{6,2},{8,12},{10,14},{12,8},{14,10},{16,20},{18,... | collective-permute-start | bytes 1548296 | tf_op jit(solution)/shard_map/ppermute | solution.py:792
  313.6 39.7 %collective-permute-start.4 = (bf16[512,1536]{1,0:T(8,128)(2,1)}, bf16[512,1536]{1,0:T(8,128)(2,1)}, u32[]{:S(2)}, u32[]{:S(2)}) collective-permute-start(bf16[512,1536]{1,0:T(8,128)(2,1)} %shard_map.269), channel_id=1, source_target_pairs={{0,1},{1,0},{2,3},{3,2},{4,5},{5,4},{6,7},{7,6},{8,9},{9,8},{10,11... | collective-permute-start | bytes 4718600 | tf_op jit(solution)/shard_map/ppermute | solution.py:907
  334.3 14.2 %copy-start.13 = (s32[512]{0:T(512)S(1)}, s32[512]{0:T(512)}, u32[]{:S(2)}) copy-start(s32[512]{0:T(512)} %param.27) | copy-start | bytes 6148
  345.9 9.4 %collective-permute-start.7 = (bf16[16,8064]{1,0:T(8,128)(2,1)S(1)}, bf16[16,8064]{1,0:T(8,128)(2,1)S(1)}, u32[]{:S(2)}, u32[]{:S(2)}) collective-permute-start(bf16[16,8064]{1,0:T(8,128)(2,1)S(1)} %fusion.4), channel_id=1, source_target_pairs={{0,8},{2,10},{4,12},{6,14},{8,0},{10,2},{12,4},{14,6},{16,24},{18,... | collective-permute-start | bytes 774152 | tf_op jit(solution)/shard_map/ppermute | solution.py:792
  355.3 8.2 %collective-permute-start.8 = (bf16[8,8064]{1,0:T(8,128)(2,1)S(1)}, bf16[8,8064]{1,0:T(8,128)(2,1)S(1)}, u32[]{:S(2)}, u32[]{:S(2)}) collective-permute-start(bf16[8,8064]{1,0:T(8,128)(2,1)S(1)} %fusion.6), channel_id=1, source_target_pairs={{0,16},{2,18},{4,20},{6,22},{8,24},{10,26},{12,28},{14,30},{16,0},... | collective-permute-start | bytes 387080 | tf_op jit(solution)/shard_map/ppermute | solution.py:792
  363.8 7.7 %collective-permute-start.9 = (f32[8,3456]{1,0:T(8,128)S(1)}, f32[8,3456]{1,0:T(8,128)S(1)}, u32[]{:S(2)}, u32[]{:S(2)}) collective-permute-start(f32[8,3456]{1,0:T(8,128)S(1)} %pad_maximum_fusion.1), channel_id=1, source_target_pairs={{0,1},{1,0},{2,3},{3,2},{4,5},{5,4},{6,7},{7,6},{8,9},{9,8},{10,11... | collective-permute-start | bytes 331784 | tf_op jit(solution)/shard_map/ppermute | solution.py:781
  (8 other events, 18.2 us)
Sparse Core Ops, SparseCore 0:
  11.5 148.3 all-gather.3
  162.1 52.2 all-gather.5
  372.3 52.1 all-gather.7

commit v4 on v3

--- a/solution.py
+++ b/solution.py
@@ -905,7 +905,7 @@
     if pairwise:
         sent_back = back(0)
         grad_other = lax.ppermute(sent_back, "tensor", swap)
-        gz, _, dealt_output = lax.optimization_barrier((gz, sent_back, dealt_output))
+        gz, _ = lax.optimization_barrier((gz, sent_back))
         grad_own = project_back(meta, gz, grest, gmid_in, w_in, adapter_down_in, half_rows, 1)
     else:
         grad_own, grad_other = scatter_rows(back(0))
@@ -919,7 +919,7 @@
     rest_at = 2 * MODEL_WIDTH
     zx_at = rest_at + REST_LOCAL
     out_at = zx_at + 2 * inner
-    total = sum_dp(gradients, (sent_back, grad_own, grad_other) if pairwise else ())
+    total = sum_dp(gradients, (sent_back, (grad_own, dealt_output), grad_other) if pairwise else ())
     steps = total[:, rest_at + 2 * STATE : rest_at + 2 * STATE + heads]
     wide = jnp.zeros((total.shape[0], LANES), f32)
     wide = lax.dynamic_update_slice(wide, steps, (0, tensor_rank * heads))

time: 441 us -> 435 us (0.986)
  waiting for transfers between devices: 92.9 us -> 86.2 us
    ppermute x4, waiting for transfers between devices: 26.9 us -> 12.9 us  [exchange(): return lax.ppermute(values.astype(bf16), 'dp', pairs)]
    ppermute x1, waiting for transfers between devices: 0.01 us -> 7.43 us  [body(): grad_other = lax.ppermute(sent_back, 'tensor', swap)]
  transfers between devices with their start and end apart: 15 -> 15, of which waited for: 6 -> 6; matrix products, arithmetic and copies ran while one was open for 3% -> 3% of each run, Pallas kernels for 32% -> 33%
where the time goes in v4:
time: 435 us; the launch traced here: 434 us
  Pallas kernels  167 us (38%)
  blocking collectives  117 us (27%)
  waiting for transfers between devices  86.2 us (20%)
  starting transfers between devices  23.3 us (5%)
  local copies, waits for them, and re-layouts  22.2 us (5%)
  between operations  14.1 us (3%)
    all_to_all x2, blocking collectives, deal(): return lax.all_to_all(rows, 'dp', split_axis=0, concat_axis=0, tiled=True)  117 us
    all_to_all x2, waiting for transfers between devices, deal(): return lax.all_to_all(rows, 'dp', split_axis=0, concat_axis=0, tiled=True)  41.5 us
    pallas_call x1, Pallas kernels, forward_scan(): pl.pallas_call(partial(forward_kernel, heads=heads, block=block), out_sha...  41.5 us
    pallas_call x1, Pallas kernels, backward_scan(): pl.pallas_call(partial(backward_kernel, heads=heads, inner_all=inner_all,...  40.9 us
    pallas_call x7, Pallas kernels, simple_call(): pl.pallas_call(kernel, out_shape=outs, in_specs=[scalar] * scalars + [vec...  36.5 us
    all_gather x2, waiting for transfers between devices, gather_weight(): lax.all_gather(jnp.concatenate(shards, axis=1), 'dp', axis=0, tiled=True)  23.7 us
    pallas_call x2, Pallas kernels, project_back(): pl.pallas_call(partial(project_back_kernel, inner=inner), out_shape=jax.S...  23.3 us
    pallas_call x1, Pallas kernels, out_grad(): pl.pallas_call(partial(out_grad_kernel, pairwise=pairwise), out_shape=out...  13.3 us
  transfers between devices with their start and end apart: 15, of which 6 were waited for; matrix products, arithmetic and copies ran while one was open for 3% of the time, Pallas kernels for 33%

profile of v4, /device:TPU:1, one launch (start us, length us, event | category | flops | bytes accessed | tf_op | source)
XLA Modules:
  0.0 434.0 jit_solution(10230610327915575191)
XLA Ops:
  8.0 2.3 fusion.18
  13.0 5.2 %shard_map.261 = (bf16[512,1536]{1,0:T(8,128)(2,1)}, bf16[512,1536]{1,0:T(8,128)(2,1)}) custom-call(s32[512,1]{1,0:T(8,128)} %copy.48.key_col, s32[1,512]{1,0:T(1,128)} %bitcast.80, bf16[512,1536]{1,0:T(8,128)(2,1)} %first.1, bf16[512,1536]{1,0:T(8,128)(2,1)} %second.1), custom_call_target="tpu_custom_call" | custom-call | flops 1610612736 | bytes 1000000 | tf_op jit(solution)/shard_map/pallas_call | solution.py:89
  18.2 61.9 %all_to_all.44 = bf16[16,32,1536]{2,1,0:T(8,128)(2,1)} all-to-all(bf16[16,32,1536]{2,1,0:T(8,128)(2,1)} %bitcast.69), channel_id=1, replica_groups=mesh['dp'=16,'tensor'=2] {'dp'}, dimensions={0} | all-to-all | bytes 3145728 | tf_op jit(solution)/shard_map/all_to_all | solution.py:763
  80.2 4.8 %all-to-all-start.1 = ((bf16[16,32,1536]{2,1,0:T(8,128)(2,1)}), bf16[16,32,1536]{2,1,0:T(8,128)(2,1)S(1)}, u32[]{:S(2)}, u32[]{:S(2)}) async-start(bf16[16,32,1536]{2,1,0:T(8,128)(2,1)} %bitcast.17), calls=%async_computation.1 | async-start | bytes 3145728 | tf_op jit(solution)/shard_map/all_to_all | solution.py:763
  89.7 4.7 %shard_map.262 = (bf16[512,1536]{1,0:T(8,128)(2,1)}, bf16[512,1536]{1,0:T(8,128)(2,1)}) custom-call(s32[512,1]{1,0:T(8,128)} %copy.49.key_col, s32[1,512]{1,0:T(1,128)} %bitcast.78, bf16[512,1536]{1,0:T(8,128)(2,1)} %bitcast.68, f32[1,1536]{1,0:T(1,128)} %broadcast_in_dim.52.gain), custom_call_target="tpu_custom_call" | custom-call | flops 805306368 | bytes 1000000 | tf_op jit(solution)/shard_map/pallas_call | solution.py:89
  94.3 1.4 collective-permute-start
  98.2 2.0 fusion.17
  100.2 41.5 %all-to-all-done.1 = bf16[16,32,1536]{2,1,0:T(8,128)(2,1)S(1)} async-done(((bf16[16,32,1536]{2,1,0:T(8,128)(2,1)}), bf16[16,32,1536]{2,1,0:T(8,128)(2,1)S(1)}, u32[]{:S(2)}, u32[]{:S(2)}) %all-to-all-start.1) | async-done | bytes 1572896 | tf_op jit(solution)/shard_map/all_to_all | solution.py:763
  142.8 4.0 shard_map.264.gd_mine.cotangent
  146.8 1.5 collective-permute-start.1
  149.3 10.6 %all-gather.4.cloned.1.call-done.w_in = bf16[1536,3456]{1,0:T(8,128)(2,1)} async-done(((bf16[96,3456]{1,0:T(8,128)(2,1)}), bf16[1536,3456]{1,0:T(8,128)(2,1)}) %all-gather.4.cloned.1.call-update) | async-done | bytes 10616848 | tf_op jit(solution)/shard_map/all_gather | solution.py:842
  159.9 41.5 %shard_map.263 = (bf16[1024,1536]{1,0:T(8,128)(2,1)}, bf16[1024,1536]{1,0:T(8,128)(2,1)}, f32[1024,1536]{1,0:T(8,128)}, f32[1024,1536]{1,0:T(8,128)}, bf16[1024,...) custom-call(s32[12]{0:T(128)} %concatenate.15.meta, ...), custom_call_target="tpu_custom_call" | custom-call | flops 12079595520 | bytes 50000000 | tf_op jit(solution)/shard_map/pallas_call | solution.py:312
  201.3 13.1 %all-gather.6.cloned.1.call-done.w_out = bf16[1536,1536]{1,0:T(8,128)(2,1)} async-done(((bf16[96,1536]{1,0:T(8,128)(2,1)}), bf16[1536,1536]{1,0:T(8,128)(2,1)}) %all-gather.6.cloned.1.call-update) | async-done | bytes 4718608 | tf_op jit(solution)/shard_map/all_gather | solution.py:842
  214.4 13.3 %shard_map.265 = (f32[1024,1536]{1,0:T(8,128)}, bf16[1024,128]{1,0:T(8,128)(2,1)}, f32[8,1024]{1,0:T(8,128)}) custom-call(s32[12]{0:T(128)} %concatenate.15.meta, bf16[512,1536]{1,0:T(8,128)(2,1)} %shard_map.264.gd_mine.cotangent, bf16[512,1536]{1,0:T(8,128)(2,1)} %copy-done.19, bf16[1024,1536]{1,0:T(8,128)(2,1)} %get-tuple-element.69.gained.theirs.own, ...), custom_call_target="tpu_custom_call" | custom-call | flops 4831838208 | bytes 20000000 | tf_op jit(solution)/shard_map/pallas_call | solution.py:379
  229.1 11.5 %shard_map.266 = (bf16[512,1664]{1,0:T(8,128)(2,1)}, bf16[512,1664]{1,0:T(8,128)(2,1)}) custom-call(s32[12]{0:T(128)} %concatenate.15.meta, bf16[1024,1536]{1,0:T(8,128)(2,1)} %get-tuple-element.69.gained.theirs.own, bf16[1024,1536]{1,0:T(8,128)(2,1)} %get-tuple-element.69.gained.theirs.own, bf16[1536,1536]{1,0:T(8,128)(2,1)} %all-gather.6.cloned.1.call-done.w_out, ...), custom_call_target="tpu_custom_call" | custom-call | flops 4831838208 | bytes 15000000 | tf_op jit(solution)/shard_map/pallas_call | solution.py:422
  242.4 40.9 %shard_map.267 = (bf16[1024,3072]{1,0:T(8,128)(2,1)}, bf16[1024,384]{1,0:T(8,128)(2,1)}, bf16[1024,128]{1,0:T(8,128)(2,1)}, f32[128,8064]{1,0:T(8,128)}) custom-call(s32[12]{0:T(128)} %concatenate.15.meta, f32[1024,1536]{1,0:T(8,128)} %get-tuple-element.55.scan_out, f32[1024,1536]{1,0:T(8,128)} %get-tuple-element.56.gate_pre, ...), custom_call_target="tpu_custom_call" | custom-call | flops 14495514624 | bytes 50000000 | tf_op jit(solution)/shard_map/pallas_call | solution.py:635
  284.5 6.4 %shard_map.268 = (bf16[512,1536]{1,0:T(8,128)(2,1)}, f32[128,1536]{1,0:T(8,128)}) custom-call(s32[12]{0:T(128)} %concatenate.15.meta, s32[512,1]{1,0:T(8,128)} %copy.57.key_col, s32[1,512]{1,0:T(1,128)} %bitcast.74, bf16[512,1536]{1,0:T(8,128)(2,1)} %get-tuple-element.76.resid, bf16[512,1664]{1,0:T(8,128)(2,1)} %get-tuple-element.77.own, ...), custom_call_target="tpu_custom_call" | custom-call | flops 1610612736 | bytes 1000000 | tf_op jit(solution)/shard_map/pallas_call | solution.py:89
  291.0 2.2 constant_dynamic-update-slice_fusion
  293.1 1.7 fusion.1
  295.7 4.3 all-to-all-start.2
  300.1 11.9 %shard_map.269 = bf16[512,1536]{1,0:T(8,128)(2,1)} custom-call(s32[12]{0:T(128)} %concatenate.15.meta, bf16[1024,3072]{1,0:T(8,128)(2,1)} %get-tuple-element.87.gz, bf16[1024,384]{1,0:T(8,128)(2,1)} %get-tuple-element.82.grest, bf16[1024,128]{1,0:T(8,128)(2,1)} %get-tuple-element.83.gmid, bf16[1536,3456]{1,0:T(8,128)(2,1)} %all-gather.4.cloned.1.call-done.w_in, ...), custom_call_target="tpu_custom_call" | custom-call | flops 4831838208 | bytes 15000000 | tf_op jit(solution)/shard_map/pallas_call | solution.py:666
  312.3 1.3 collective-permute-start.6
  314.8 11.4 %shard_map.271.own = bf16[512,1536]{1,0:T(8,128)(2,1)} custom-call(s32[12]{0:T(128)} %concatenate.15.meta, bf16[1024,3072]{1,0:T(8,128)(2,1)} %get-tuple-element.87.gz, bf16[1024,384]{1,0:T(8,128)(2,1)} %get-tuple-element.82.grest, bf16[1024,128]{1,0:T(8,128)(2,1)} %get-tuple-element.83.gmid, bf16[1536,3456]{1,0:T(8,128)(2,1)} %all-gather.4.cloned.1.call-done.w_in, ...), custom_call_target="tpu_custom_call" | custom-call | flops 4831838208 | bytes 15000000 | tf_op jit(solution)/shard_map/pallas_call | solution.py:666
  326.2 7.0 %collective-permute-done.6 = bf16[32,8064]{1,0:T(8,128)(2,1)} collective-permute-done((bf16[32,8064]{1,0:T(8,128)(2,1)S(1)}, bf16[32,8064]{1,0:T(8,128)(2,1)}, u32[]{:S(2)}, u32[]{:S(2)}) %collective-permute-start.6) | collective-permute-done | bytes 516128 | tf_op jit(solution)/shard_map/ppermute | solution.py:792
  334.4 2.7 collective-permute-start.7
  337.9 4.0 shard_map.270
  341.9 7.4 %collective-permute-done.4.other = bf16[512,1536]{1,0:T(8,128)(2,1)} collective-permute-done((bf16[512,1536]{1,0:T(8,128)(2,1)}, bf16[512,1536]{1,0:T(8,128)(2,1)}, u32[]{:S(2)}, u32[]{:S(2)}) %collective-permute-start.4) | collective-permute-done | bytes 1572896 | tf_op jit(solution)/shard_map/ppermute | solution.py:907
  349.4 2.2 collective-permute-start.8
  351.6 5.9 %collective-permute-done.8 = bf16[8,8064]{1,0:T(8,128)(2,1)S(1)} collective-permute-done((bf16[8,8064]{1,0:T(8,128)(2,1)S(1)}, bf16[8,8064]{1,0:T(8,128)(2,1)S(1)}, u32[]{:S(2)}, u32[]{:S(2)}) %collective-permute-start.8) | collective-permute-done | bytes 129056 | tf_op jit(solution)/shard_map/ppermute | solution.py:792
  359.1 6.3 %shard_map.272 = bf16[512,1536]{1,0:T(8,128)(2,1)} custom-call(s32[512,1]{1,0:T(8,128)} %copy.57.key_col, s32[1,512]{1,0:T(1,128)} %bitcast.75, bf16[512,1536]{1,0:T(8,128)(2,1)} %get-tuple-element.76.resid, bf16[512,1536]{1,0:T(8,128)(2,1)} %shard_map.271.own, bf16[512,1536]{1,0:T(8,128)(2,1)} %collective-permute-done.4.other, ...), custom_call_target="tpu_custom_call" | custom-call | flops 805306368 | bytes 1000000 | tf_op jit(solution)/shard_map/pallas_call | solution.py:89
  366.2 55.4 %all_to_all.45 = bf16[16,32,1536]{2,1,0:T(8,128)(2,1)} all-to-all(bf16[16,32,1536]{2,1,0:T(8,128)(2,1)} %bitcast.60), channel_id=1, replica_groups=mesh['dp'=16,'tensor'=2] {'dp'}, dimensions={0} | all-to-all | bytes 3145728 | tf_op jit(solution)/shard_map/all_to_all | solution.py:763
  421.5 6.0 %shard_map.273 = (bf16[512,1536]{1,0:T(8,128)(2,1)}, f32[1536,128]{1,0:T(8,128)}, f32[128,2,1536]{2,1,0:T(2,128)}, f32[304,128]{1,0:T(8,128)}, f32[1536,128]{1,0:T(8,128)}, /*index=5*/f32[128,1536]{1,0:T(8,128)}) custom-call(s32[512,1]{1,0:T(8,128)} %copy.58.key_col, s32[1,512]{1,0:T(1,128)} %bitcast.73, bf16[512,1536]{1,0:T(8,128)(2,1)} %bitcast.61, ...), custom_call_target="tpu_custom_call" | custom-call | flops 805306368 | bytes 1000000 | tf_op jit(solution)/shard_map/pallas_call | solution.py:89
  (114 shorter events, 23.8 us)
Async XLA Ops:
  7.2 152.7 %all-gather.4.cloned.1.call-start = ((), (), s32[]{:S(2)}) async-start(), calls=%async_computation.4 | async-start | bytes 11280384 | tf_op jit(solution)/shard_map/all_gather | solution.py:842
  11.4 203.1 %all-gather.6.cloned.1.call-start = ((), (), s32[]{:S(2)}) async-start(), calls=%async_computation.5 | async-start | bytes 5013504 | tf_op jit(solution)/shard_map/all_gather | solution.py:842
  80.1 5.2 %copy-start.20 = (s32[64]{0:T(128)S(1)}, s32[64]{0:T(128)}, u32[]{:S(2)}) copy-start(s32[64]{0:T(128)} %param.25) | copy-start | bytes 772
  80.1 5.3 %copy-start.5 = (bf16[128,304]{0,1:T(8,128)(2,1)S(1)}, bf16[128,304]{0,1:T(8,128)(2,1)}, u32[]{:S(2)}) copy-start(bf16[128,304]{0,1:T(8,128)(2,1)} %param.40) | copy-start | bytes 233476
  80.1 5.4 %slice-start = ((bf16[128,304]{0,1:T(8,128)(2,1)}), bf16[128,256]{0,1:T(8,128)(2,1)S(1)}, s32[]{:S(2)}) async-start(bf16[128,304]{0,1:T(8,128)(2,1)} %param.40), calls=%async_computation.7 | async-start | bytes 131072 | tf_op jit(solution)/shard_map/slice | solution.py:838
  80.1 5.5 %copy-start.10 = (s32[512]{0:T(512)S(1)}, s32[512]{0:T(512)}, u32[]{:S(2)}) copy-start(s32[512]{0:T(512)} %param.26) | copy-start | bytes 6148
  80.1 6.4 %copy-start.14 = (f32[1536]{0:T(1024)S(1)}, f32[1536]{0:T(1024)}, u32[]{:S(2)}) copy-start(f32[1536]{0:T(1024)} %param.28) | copy-start | bytes 18436
  80.1 7.0 %copy-start.17 = (f32[24]{0:T(128)S(1)}, f32[24]{0:T(128)}, u32[]{:S(2)}) copy-start(f32[24]{0:T(128)} %param.35) | copy-start | bytes 292
  80.1 7.7 %copy-start.7 = (f32[5,1536]{1,0:T(8,128)S(1)}, f32[5,1536]{1,0:T(8,128)}, u32[]{:S(2)}) copy-start(f32[5,1536]{1,0:T(8,128)} %param.31) | copy-start | bytes 92164
  80.1 8.3 %copy-start.16 = (f32[5,256]{1,0:T(8,128)S(1)}, f32[5,256]{1,0:T(8,128)}, u32[]{:S(2)}) copy-start(f32[5,256]{1,0:T(8,128)} %param.32) | copy-start | bytes 15364
  80.2 8.9 %copy-start.15 = (f32[1536]{0:T(1024)S(1)}, f32[1536]{0:T(1024)}, u32[]{:S(2)}) copy-start(f32[1536]{0:T(1024)} %param.36) | copy-start | bytes 18436
  80.2 61.5 %all-to-all-start.1 = ((bf16[16,32,1536]{2,1,0:T(8,128)(2,1)}), bf16[16,32,1536]{2,1,0:T(8,128)(2,1)S(1)}, u32[]{:S(2)}, u32[]{:S(2)}) async-start(bf16[16,32,1536]{2,1,0:T(8,128)(2,1)} %bitcast.17), calls=%async_computation.1 | async-start | bytes 3145728 | tf_op jit(solution)/shard_map/all_to_all | solution.py:763
  87.2 9.3 %copy-start.21 = (f32[24]{0:T(128)S(1)}, f32[24]{0:T(128)}, u32[]{:S(2)}) copy-start(f32[24]{0:T(128)} %param.34) | copy-start | bytes 292
  87.2 9.8 %copy-start.22 = (f32[24]{0:T(128)S(1)}, f32[24]{0:T(128)}, u32[]{:S(2)}) copy-start(f32[24]{0:T(128)} %param.33) | copy-start | bytes 292
  89.7 8.5 %copy-start.1 = (bf16[128,2,1536]{2,1,0:T(2,128)(2,1)S(1)}, bf16[128,2,1536]{2,1,0:T(2,128)(2,1)}, u32[]{:S(2)}) copy-start(bf16[128,2,1536]{2,1,0:T(2,128)(2,1)} %param.39) | copy-start | bytes 2359300
  94.3 54.9 %collective-permute-start = (bf16[512,1536]{1,0:T(8,128)(2,1)}, bf16[512,1536]{1,0:T(8,128)(2,1)}, u32[]{:S(2)}, u32[]{:S(2)}) collective-permute-start(bf16[512,1536]{1,0:T(8,128)(2,1)} %get-tuple-element.54.mine.normed_mine), channel_id=1, source_target_pairs={{0,1},{1,0},{2,3},{3,2},{4,5},{5,4},{6,7},{7,6},{8,9},{9,8},{10,11... | collective-permute-start | bytes 4718600 | tf_op jit(solution)/shard_map/ppermute | solution.py:772
  142.8 5.5 %copy-start.2 = (bf16[128,1,1536]{2,1,0:T(2,128)(2,1)S(1)}, bf16[128,1,1536]{2,1,0:T(2,128)(2,1)}, u32[]{:S(2)}) copy-start(bf16[128,1,1536]{2,1,0:T(2,128)(2,1)} %get-tuple-element.100) | copy-start | bytes 1179652
  146.8 54.5 %collective-permute-start.1 = (bf16[512,1536]{1,0:T(8,128)(2,1)}, bf16[512,1536]{1,0:T(8,128)(2,1)S(1)}, u32[]{:S(2)}, u32[]{:S(2)}) collective-permute-start(bf16[512,1536]{1,0:T(8,128)(2,1)} %shard_map.264.gd_mine.cotangent), channel_id=1, source_target_pairs={{0,1},{1,0},{2,3},{3,2},{4,5},{5,4},{6,7},{7,6},{8,9},{9,8},{10,11... | collective-permute-start | bytes 4718600 | tf_op jit(solution)/shard_map/ppermute | solution.py:772
  201.3 13.1 %copy-start.19 = (bf16[512,1536]{1,0:T(8,128)(2,1)}, bf16[512,1536]{1,0:T(8,128)(2,1)S(1)}, u32[]{:S(2)}) copy-start(bf16[512,1536]{1,0:T(8,128)(2,1)S(1)} %collective-permute-done.1.gd_other) | copy-start | bytes 4718596
  227.8 12.8 %copy-start.9 = (f32[8,1024]{1,0:T(8,128)S(1)}, f32[8,1024]{1,0:T(8,128)}, u32[]{:S(2)}) copy-start(f32[8,1024]{1,0:T(8,128)} %get-tuple-element.68) | copy-start | bytes 98308
  227.8 12.8 %collective-permute-start.2 = (f32[8,1024]{1,0:T(8,128)}, f32[8,1024]{1,0:T(8,128)S(1)}, u32[]{:S(2)}, u32[]{:S(2)}) collective-permute-start(f32[8,1024]{1,0:T(8,128)} %get-tuple-element.68), channel_id=1, source_target_pairs={{0,1},{1,0},{2,3},{3,2},{4,5},{5,4},{6,7},{7,6},{8,9},{9,8},{10,11... | collective-permute-start | bytes 98312 | tf_op jit(solution)/shard_map/ppermute | solution.py:781
  240.6 42.7 %collective-permute-start.3 = (bf16[512,1664]{1,0:T(8,128)(2,1)}, bf16[512,1664]{1,0:T(8,128)(2,1)S(1)}, u32[]{:S(2)}, u32[]{:S(2)}) collective-permute-start(bf16[512,1664]{1,0:T(8,128)(2,1)} %get-tuple-element.78), channel_id=1, source_target_pairs={{0,1},{1,0},{2,3},{3,2},{4,5},{5,4},{6,7},{7,6},{8,9},{9,8},{10,11... | collective-permute-start | bytes 5111816 | tf_op jit(solution)/shard_map/ppermute | solution.py:885
  294.8 17.2 %collective-permute-start.5 = (bf16[64,8064]{1,0:T(8,128)(2,1)S(1)}, bf16[64,8064]{1,0:T(8,128)(2,1)S(1)}, u32[]{:S(2)}, u32[]{:S(2)}) collective-permute-start(bf16[64,8064]{1,0:T(8,128)(2,1)S(1)} %fusion.1), channel_id=1, source_target_pairs={{0,2},{2,0},{4,6},{6,4},{8,10},{10,8},{12,14},{14,12},{16,18},{18,... | collective-permute-start | bytes 3096584 | tf_op jit(solution)/shard_map/ppermute | solution.py:792
  295.7 38.6 %all-to-all-start.2 = ((bf16[16,32,1536]{2,1,0:T(8,128)(2,1)}), bf16[16,32,1536]{2,1,0:T(8,128)(2,1)}, u32[]{:S(2)}, u32[]{:S(2)}) async-start(bf16[16,32,1536]{2,1,0:T(8,128)(2,1)} %bitcast.24), calls=%async_computation.2 | async-start | bytes 3145728 | tf_op jit(solution)/shard_map/all_to_all | solution.py:763
  300.0 121.5 %all-gather.8.cloned.1.call-start = ((), (), s32[]{:S(2)}) async-start(), calls=%async_computation.6 | async-start | bytes 2193408 | tf_op jit(solution)/shard_map/all_gather | solution.py:808
  300.0 11.9 %copy-start.3 = (f32[128,8064]{1,0:T(8,128)S(1)}, f32[128,8064]{1,0:T(8,128)}, u32[]{:S(2)}) copy-start(f32[128,8064]{1,0:T(8,128)} %constant_dynamic-update-slice_fusion) | copy-start | bytes 12386308
  312.3 20.9 %collective-permute-start.6 = (bf16[32,8064]{1,0:T(8,128)(2,1)S(1)}, bf16[32,8064]{1,0:T(8,128)(2,1)}, u32[]{:S(2)}, u32[]{:S(2)}) collective-permute-start(bf16[32,8064]{1,0:T(8,128)(2,1)S(1)} %fusion.3), channel_id=1, source_target_pairs={{0,4},{2,6},{4,0},{6,2},{8,12},{10,14},{12,8},{14,10},{16,20},{18,... | collective-permute-start | bytes 1548296 | tf_op jit(solution)/shard_map/ppermute | solution.py:792
  313.6 35.7 %collective-permute-start.4 = (bf16[512,1536]{1,0:T(8,128)(2,1)}, bf16[512,1536]{1,0:T(8,128)(2,1)}, u32[]{:S(2)}, u32[]{:S(2)}) collective-permute-start(bf16[512,1536]{1,0:T(8,128)(2,1)} %shard_map.269), channel_id=1, source_target_pairs={{0,1},{1,0},{2,3},{3,2},{4,5},{5,4},{6,7},{7,6},{8,9},{9,8},{10,11... | collective-permute-start | bytes 4718600 | tf_op jit(solution)/shard_map/ppermute | solution.py:907
  326.2 10.8 %copy-start.13 = (s32[512]{0:T(512)S(1)}, s32[512]{0:T(512)}, u32[]{:S(2)}) copy-start(s32[512]{0:T(512)} %param.27) | copy-start | bytes 6148
  334.4 14.9 %collective-permute-start.7 = (bf16[16,8064]{1,0:T(8,128)(2,1)S(1)}, bf16[16,8064]{1,0:T(8,128)(2,1)S(1)}, u32[]{:S(2)}, u32[]{:S(2)}) collective-permute-start(bf16[16,8064]{1,0:T(8,128)(2,1)S(1)} %fusion.4), channel_id=1, source_target_pairs={{0,8},{2,10},{4,12},{6,14},{8,0},{10,2},{12,4},{14,6},{16,24},{18,... | collective-permute-start | bytes 774152 | tf_op jit(solution)/shard_map/ppermute | solution.py:792
  349.4 8.1 %collective-permute-start.8 = (bf16[8,8064]{1,0:T(8,128)(2,1)S(1)}, bf16[8,8064]{1,0:T(8,128)(2,1)S(1)}, u32[]{:S(2)}, u32[]{:S(2)}) collective-permute-start(bf16[8,8064]{1,0:T(8,128)(2,1)S(1)} %fusion.6), channel_id=1, source_target_pairs={{0,16},{2,18},{4,20},{6,22},{8,24},{10,26},{12,28},{14,30},{16,0},... | collective-permute-start | bytes 387080 | tf_op jit(solution)/shard_map/ppermute | solution.py:792
  357.8 7.7 %collective-permute-start.9 = (f32[8,3456]{1,0:T(8,128)S(1)}, f32[8,3456]{1,0:T(8,128)S(1)}, u32[]{:S(2)}, u32[]{:S(2)}) collective-permute-start(f32[8,3456]{1,0:T(8,128)S(1)} %pad_maximum_fusion.1), channel_id=1, source_target_pairs={{0,1},{1,0},{2,3},{3,2},{4,5},{5,4},{6,7},{7,6},{8,9},{9,8},{10,11... | collective-permute-start | bytes 331784 | tf_op jit(solution)/shard_map/ppermute | solution.py:781
  (8 other events, 18.2 us)
Sparse Core Ops, SparseCore 0:
  11.5 148.3 all-gather.3
  162.1 52.2 all-gather.5
  366.3 52.0 all-gather.7
